TPU v7x, 32 devices: a whole 2x2x4 slice. The times are simulated.
32 devices in a mesh: dp: 4 (over z), row: 4 (over y, core), col: 2 (over x).
Axes of the slice: x: 2, y: 2, z: 4, core: 2. Of those that a mesh axis runs over, the one named last changes fastest.
Arguments:
- hidden_in: bfloat16 [1536, 16384], P('col', ('dp', 'row')), may hold values from -6 to 6
- grad_out: bfloat16 [1536, 16384], P('col', ('dp', 'row')), may hold values from -6 to 6
- lengths: int32 [4, 3], P('dp'), may hold values from 512 to 2048, as said below
- norm_gain: bfloat16 [1536], replicated, may hold values from 0.5 to 1.5
- inner_proj: bfloat16 [3072, 2, 1536], P('col', None, 'row'), may hold values from -0.15625 to 0.15625
- state_proj: bfloat16 [1536, 256], P('row'), may hold values from -0.15625 to 0.15625
- step_proj: bfloat16 [48, 1536], P('col', 'row'), may hold values from -0.15625 to 0.15625
- conv_inner: bfloat16 [4, 3072], P(None, 'col'), may hold values from -3 to 3
- conv_inner_bias: bfloat16 [3072], P('col'), may hold values from -3 to 3
- conv_state: bfloat16 [4, 256], replicated, may hold values from -3 to 3
- conv_state_bias: bfloat16 [256], replicated, may hold values from -3 to 3
- step_bias: float32 [48], P('col'), may hold values from -5 to -1
- decay_log: float32 [48], P('col'), may hold values from -5 to 2.5
- skip_gain: float32 [48], P('col'), may hold values from 0.5 to 1.5
- gate_gain: bfloat16 [3072], P('col'), may hold values from 0.5 to 1.5
- out_proj: bfloat16 [3072, 1536], P('col', 'row'), may hold values from -0.109375 to 0.109375
Outputs:
- block_out: bfloat16 [1536, 16384], P('col', ('dp', 'row'))
- grad_in: bfloat16 [1536, 16384], P('col', ('dp', 'row'))
- grad_norm_gain: float32 [1536], replicated
- grad_inner_proj: float32 [3072, 2, 1536], P('col', None, ('dp', 'row'))
- grad_state_proj: float32 [1536, 256], replicated
- grad_step_proj: float32 [48, 1536], P('col', ('dp', 'row'))
- grad_conv_inner: float32 [4, 3072], replicated
- grad_inner_bias: float32 [3072], replicated
- grad_conv_state: float32 [4, 256], replicated
- grad_state_bias: float32 [256], replicated
- grad_step_bias: float32 [48], replicated
- grad_decay_log: float32 [48], replicated
- grad_skip_gain: float32 [48], replicated
- grad_gate_gain: float32 [3072], replicated
- grad_out_proj: float32 [3072, 1536], P('col', ('dp', 'row'))
Inputs may be any that keep to these rules, and one draw needn't show every extreme that they name: In every group one length, at a place drawn from the seed, is exactly 2048; the other lengths lie between 512 and 1024, so a group's lengths sum to at most 4096.
All inputs are finite; a program needn't handle non-finite values.
Results may differ from a plain program's by a relative error of at most 0.012.
The roundings to bfloat16 on the way count: a program that leaves them out, or rounds other values in their place, can miss the bound.
Values may be sent and summed in bfloat16 or wider, within the bound.
A program may use at most 320 MiB of HBM per device.

v0:
```python
import jax
import jax.numpy as jnp
from jax import lax
from jax.sharding import PartitionSpec as P

HEADDIM = 64
STATE = 128
CONV = 4
SPAN = 256


EPS = 1e-05
PRECISE = lax.Precision.HIGHEST


def passed_along(value, axis, steps):
    count = lax.axis_size(axis)
    leading, last = (max(0, -steps), min(count, count - steps))
    return lax.ppermute(value, axis, [(source, source + steps) for source in range(leading, last)])


def carried_in(shard, axis, combine, identity, reverse):
    devices, mine = (lax.axis_size(axis), lax.axis_index(axis))
    everything = jax.tree.map(lambda part: lax.all_gather(part, axis), shard)
    start = jax.tree.map(
        lambda part, zero: jnp.broadcast_to(jnp.asarray(zero, part.dtype), part.shape),
        shard,
        identity,
    )

    def lap(k, before):
        at = devices - 1 - k if reverse else k
        reached = at > mine if reverse else at < mine
        new = combine(before, jax.tree.map(lambda part: part[at], everything))
        return jax.tree.map(lambda a, b: jnp.where(reached, a, b), new, before)

    return lax.fori_loop(0, devices, lap, start)


def causal_conv(padded, taps, bias, padded_segment, segment):
    count = segment.shape[0]
    total = bias
    for index in range(taps.shape[0]):
        same = (padded_segment[index : index + count] == segment).astype(jnp.float32)
        total = total + taps[index] * padded[index : index + count] * same[:, None]
    return total


def span_step(state, pieces, rate, skip):
    values, keys_b, keys_c, steps, segment, before = pieces
    size = segment.shape[0]
    logs = steps * rate
    cums = jnp.cumsum(logs, axis=0)
    order = jnp.arange(size)
    same = ((segment[:, None] == segment[None, :]) & (order[:, None] >= order[None, :])).astype(
        jnp.float32
    )
    mask = same[:, :, None, None]
    diffs = cums[:, None] - cums[None, :]
    decay = jnp.exp(jnp.where(mask > 0, diffs, 0.0)) * mask
    scores = jnp.einsum("ign,jgn->ijg", keys_c, keys_b, precision=PRECISE)
    mixing = scores[:, :, :, None] * decay * steps[None]
    inner = jnp.einsum("ijgk,jgkp->igkp", mixing, values, precision=PRECISE)
    carry = (segment == before).astype(jnp.float32)
    entry = jnp.exp(cums) * carry[:, None, None]
    outer = jnp.einsum("ign,gkpn->igkp", keys_c, state, precision=PRECISE) * entry[..., None]
    result = inner + outer + skip[None, :, :, None] * values
    last_same = (segment == segment[size - 1]).astype(jnp.float32)
    tail = jnp.exp(cums[size - 1][None] - cums) * last_same[:, None, None] * steps
    weighted = values * tail[..., None]
    fresh = jnp.einsum("jgkp,jgn->gkpn", weighted, keys_b, precision=PRECISE)
    kept = state * (jnp.exp(cums[size - 1]) * carry[size - 1])[:, :, None, None]
    return (fresh + kept, result)


def scan_spans(state, values, keys_b, keys_c, steps, segment, before, rate, skip, size):
    count = values.shape[0] // size
    ends = segment.reshape(count, size)[:, size - 1]
    befores = jnp.concatenate([jnp.reshape(before, (1,)), ends[: count - 1]])

    def step(carry_state, pieces):
        return span_step(carry_state, pieces, rate, skip)

    pieces = (
        values.reshape((count, size) + values.shape[1:]),
        keys_b.reshape((count, size) + keys_b.shape[1:]),
        keys_c.reshape((count, size) + keys_c.shape[1:]),
        steps.reshape((count, size) + steps.shape[1:]),
        segment.reshape(count, size),
        befores,
    )
    final, outputs = lax.scan(jax.checkpoint(step), state, pieces)
    return (final, outputs.reshape((count * size,) + outputs.shape[2:]))


def mixer_local(
    ext_inner,
    ext_state,
    c_inner,
    c_inner_b,
    c_state,
    c_state_b,
    dt_in,
    s_bias,
    d_log,
    s_gain,
    padded_segment,
    segment,
    before,
):
    x_conv = jax.nn.silu(causal_conv(ext_inner, c_inner, c_inner_b, padded_segment, segment))
    bc_conv = jax.nn.silu(causal_conv(ext_state, c_state, c_state_b, padded_segment, segment))
    steps = jax.nn.softplus(dt_in + s_bias)
    rate = -jnp.exp(d_log)
    rows, heads = steps.shape
    values = x_conv.reshape(rows, 1, heads, HEADDIM)
    keys_b = bc_conv[:, None, :STATE]
    keys_c = bc_conv[:, None, STATE:]
    start = jnp.zeros((1, heads, HEADDIM, STATE), jnp.float32)
    final, outputs = scan_spans(
        start,
        values,
        keys_b,
        keys_c,
        steps[:, None],
        segment,
        before,
        rate[None],
        s_gain[None],
        SPAN,
    )
    cums = jnp.cumsum(steps * rate, axis=0)
    carry = (segment == before).astype(jnp.float32)
    passing = jnp.exp(cums[rows - 1]) * carry[rows - 1]
    return (outputs, final, passing, keys_c, cums)


def carried(state_in, keys_c, cums, carry):
    lifted = jnp.einsum("ign,gkpn->igkp", keys_c, state_in, precision=PRECISE)
    return lifted * (jnp.exp(cums) * carry[:, None])[:, None, :, None]


def chain(earlier, later):
    return (earlier[0] * later[0], earlier[1] * later[0][None, :, None, None] + later[1])


def place_block(piece, count, index, axis):
    shape_all = list(piece.shape)
    shape_all[axis] = shape_all[axis] * count
    return lax.dynamic_update_slice_in_dim(
        jnp.zeros(tuple(shape_all), piece.dtype), piece, index * piece.shape[axis], axis
    )


def per_device(
    hidden_in,
    grad_out,
    lengths,
    norm_gain,
    inner_proj,
    state_proj,
    step_proj,
    conv_inner,
    conv_inner_bias,
    conv_state,
    conv_state_bias,
    step_bias,
    decay_log,
    skip_gain,
    gate_gain,
    out_proj,
):
    cols_here, rows = hidden_in.shape
    ncols = lax.axis_size("col")
    width = cols_here * ncols
    inner_here = inner_proj.shape[0]
    heads_here = step_proj.shape[0]
    col_index = lax.axis_index("col")
    ends = jnp.cumsum(lengths[0])
    places = lax.axis_index("row") * rows + jnp.arange(-(CONV - 1), rows, dtype=jnp.int32)
    counted = jnp.sum((places[:, None] >= ends[None, :]).astype(jnp.int32), axis=1)
    padded_segment = jnp.where(places < 0, -1, counted)
    segment = padded_segment[CONV - 1 :]
    before = padded_segment[CONV - 2]
    live = (places[CONV - 1 :] < ends[ends.shape[0] - 1]).astype(jnp.float32)[None, :]
    gain_full = norm_gain.astype(jnp.float32)
    whole_x = lax.all_gather(hidden_in, "col", axis=0, tiled=True)
    whole_f = whole_x.astype(jnp.float32)
    rstd_in = lax.rsqrt(jnp.mean(whole_f * whole_f, axis=0, keepdims=True) + EPS)
    normed = (whole_f * rstd_in * gain_full[:, None]).astype(jnp.bfloat16)
    inner_all, state_all, step_all, out_all = (
        lax.all_gather(inner_proj, "row", axis=2, tiled=True),
        lax.all_gather(state_proj, "row", axis=0, tiled=True),
        lax.all_gather(step_proj, "row", axis=1, tiled=True),
        lax.all_gather(out_proj, "row", axis=1, tiled=True),
    )
    inner_cols = jnp.transpose(inner_all, (2, 1, 0)).reshape(width, 2 * inner_here)
    proj_weight = jnp.concatenate([inner_cols, state_all, step_all.T], axis=1)
    projected = lax.dot_general(
        normed, proj_weight, (((0,), (0,)), ((), ())), preferred_element_type=jnp.float32
    )
    gate_z = projected[:, :inner_here]
    x_part = projected[:, inner_here : 2 * inner_here]
    bc_part = projected[:, 2 * inner_here : 2 * inner_here + 2 * STATE]
    dt_part = projected[:, 2 * inner_here + 2 * STATE :]
    rim_inner, rim_state = passed_along(
        (x_part[rows - (CONV - 1) :], bc_part[rows - (CONV - 1) :]), "row", 1
    )
    ext_inner = jnp.concatenate([rim_inner, x_part], axis=0)
    ext_state = jnp.concatenate([rim_state, bc_part], axis=0)

    def local_fn(
        e_inner, e_state, c_inner, c_inner_b, c_state, c_state_b, dt_in, s_bias, d_log, s_gain
    ):
        return mixer_local(
            e_inner,
            e_state,
            c_inner,
            c_inner_b,
            c_state,
            c_state_b,
            dt_in,
            s_bias,
            d_log,
            s_gain,
            padded_segment,
            segment,
            before,
        )

    local_args = (
        ext_inner,
        ext_state,
        conv_inner.astype(jnp.float32),
        conv_inner_bias.astype(jnp.float32),
        conv_state.astype(jnp.float32),
        conv_state_bias.astype(jnp.float32),
        dt_part,
        step_bias,
        decay_log,
        skip_gain,
    )
    outputs, final, passing, keys_c, cums = local_fn(*local_args)
    unit = (jnp.ones_like(passing), jnp.zeros_like(final))
    _, state_in = carried_in((passing, final), "row", chain, unit, False)
    carry = (segment == before).astype(jnp.float32)
    y_all = (outputs + carried(state_in, keys_c, cums, carry)).reshape(rows, inner_here)
    silu_z = jax.nn.silu(gate_z)
    gz = y_all * silu_z
    inner_width = inner_here * ncols
    gate_full = gate_gain.astype(jnp.float32)
    total_sq = lax.psum(jnp.sum(gz * gz, axis=1), "col")
    rstd_gate = lax.rsqrt(total_sq / inner_width + EPS)[:, None]
    gated = (gz * rstd_gate * gate_full).astype(jnp.bfloat16)
    mixed_part = lax.dot_general(
        out_all, gated, (((0,), (1,)), ((), ())), preferred_element_type=jnp.float32
    )
    mixed = lax.psum_scatter(mixed_part, "col", scatter_dimension=0, tiled=True)
    hidden_f = hidden_in.astype(jnp.float32)
    block_out = (hidden_f + live * mixed).astype(jnp.bfloat16)
    grad_f = grad_out.astype(jnp.float32)
    grad_mixed = (live * grad_f).astype(jnp.bfloat16)
    grad_whole = lax.all_gather(grad_mixed, "col", axis=0, tiled=True)
    grad_gated = lax.dot_general(
        grad_whole, out_all, (((0,), (1,)), ((), ())), preferred_element_type=jnp.float32
    )
    grad_out_w = lax.dot_general(
        gated, grad_whole, (((0,), (1,)), ((), ())), preferred_element_type=jnp.float32
    )
    partial_stat = jnp.sum(gz * gate_full * grad_gated, axis=1)
    total_stat = lax.psum(partial_stat, "col")
    cube_gate = rstd_gate * rstd_gate * rstd_gate
    grad_gz = (
        rstd_gate * gate_full * grad_gated - gz * cube_gate * (total_stat / inner_width)[:, None]
    )
    grad_gate_here = jnp.sum(gz * rstd_gate * grad_gated, axis=0)
    grad_y = (grad_gz * silu_z).reshape(rows, 1, heads_here, HEADDIM)
    sigma = jax.nn.sigmoid(gate_z)
    grad_z = grad_gz * y_all * sigma * (1.0 + gate_z * (1.0 - sigma))
    _, pull_carried = jax.vjp(lambda s, c, u: carried(s, c, u, carry), state_in, keys_c, cums)
    state_direct, grad_keys_c, grad_cums = pull_carried(grad_y)
    _, grad_final = carried_in((passing, state_direct), "row", chain, unit, True)
    grad_passing = jnp.sum(grad_final * state_in, axis=(0, 2, 3))
    _, pull_local = jax.vjp(local_fn, *local_args)
    (
        grad_ext_inner,
        grad_ext_state,
        grad_c_inner,
        grad_c_inner_b,
        grad_c_state,
        grad_c_state_b,
        grad_dt,
        grad_s_bias,
        grad_d_log,
        grad_s_gain,
    ) = pull_local((grad_y, grad_final, grad_passing, grad_keys_c, grad_cums))
    back_inner, back_state = passed_along(
        (grad_ext_inner[: CONV - 1], grad_ext_state[: CONV - 1]), "row", -1
    )
    grad_x_part = grad_ext_inner[CONV - 1 :] + jnp.concatenate(
        [jnp.zeros((rows - (CONV - 1), inner_here), jnp.float32), back_inner], axis=0
    )
    grad_bc_part = grad_ext_state[CONV - 1 :] + jnp.concatenate(
        [jnp.zeros((rows - (CONV - 1), 2 * STATE), jnp.float32), back_state], axis=0
    )
    grad_proj = jnp.concatenate(
        [
            grad_z.astype(jnp.bfloat16),
            grad_x_part.astype(jnp.bfloat16),
            grad_bc_part.astype(jnp.bfloat16),
            grad_dt.astype(jnp.bfloat16),
        ],
        axis=1,
    )
    grad_normed = lax.dot_general(
        proj_weight, grad_proj, (((1,), (1,)), ((), ())), preferred_element_type=jnp.float32
    )
    norm_stat = jnp.sum(whole_f * gain_full[:, None] * grad_normed, axis=0)
    grad_normed_here, stat_total = (
        lax.psum_scatter(grad_normed, "col", scatter_dimension=0, tiled=True),
        lax.psum_scatter(
            jnp.broadcast_to(norm_stat[None, :], (ncols, rows)),
            "col",
            scatter_dimension=0,
            tiled=True,
        ),
    )
    gain_here = lax.dynamic_slice_in_dim(gain_full, col_index * cols_here, cols_here)[:, None]
    cube_in = rstd_in * rstd_in * rstd_in
    grad_in = (
        grad_f + rstd_in * gain_here * grad_normed_here - hidden_f * cube_in * stat_total / width
    )
    grad_gain_here = jnp.sum(hidden_f * rstd_in * grad_normed_here, axis=1)
    grad_weight = lax.dot_general(
        grad_proj, normed, (((0,), (1,)), ((), ())), preferred_element_type=jnp.float32
    )
    grad_inner_w = jnp.transpose(
        grad_weight[: 2 * inner_here].reshape(2, inner_here, width), (1, 0, 2)
    )
    grad_state_w = grad_weight[2 * inner_here : 2 * inner_here + 2 * STATE].T
    grad_step_w = grad_weight[2 * inner_here + 2 * STATE :]
    summed_inner, summed_step, summed_out = (
        lax.psum_scatter(grad_inner_w, ("dp", "row"), scatter_dimension=2, tiled=True),
        lax.psum_scatter(grad_step_w, ("dp", "row"), scatter_dimension=1, tiled=True),
        lax.psum_scatter(grad_out_w, ("dp", "row"), scatter_dimension=1, tiled=True),
    )
    small = lax.psum(
        (
            grad_state_w,
            place_block(grad_gain_here, ncols, col_index, 0),
            place_block(grad_c_inner, ncols, col_index, 1),
            place_block(grad_c_inner_b, ncols, col_index, 0),
            grad_c_state,
            grad_c_state_b,
            place_block(grad_s_bias, ncols, col_index, 0),
            place_block(grad_d_log, ncols, col_index, 0),
            place_block(grad_s_gain, ncols, col_index, 0),
            place_block(grad_gate_here, ncols, col_index, 0),
        ),
        ("dp", "row", "col"),
    )
    return (
        block_out,
        grad_in.astype(jnp.bfloat16),
        small[1],
        summed_inner,
        small[0],
        summed_step,
        small[2],
        small[3],
        small[4],
        small[5],
        small[6],
        small[7],
        small[8],
        small[9],
        summed_out,
    )


def solution(mesh):
    return jax.shard_map(
        per_device,
        mesh=mesh,
        in_specs=(
            P("col", ("dp", "row")),
            P("col", ("dp", "row")),
            P("dp", None),
            P(),
            P("col", None, "row"),
            P("row", None),
            P("col", "row"),
            P(None, "col"),
            P("col"),
            P(),
            P(),
            P("col"),
            P("col"),
            P("col"),
            P("col"),
            P("col", "row"),
        ),
        out_specs=(
            P("col", ("dp", "row")),
            P("col", ("dp", "row")),
            P(),
            P("col", None, ("dp", "row")),
            P(),
            P("col", ("dp", "row")),
            P(),
            P(),
            P(),
            P(),
            P(),
            P(),
            P(),
            P(),
            P("col", ("dp", "row")),
        ),
        check_vma=False,
    )
```

profile of v0, /device:TPU:0, one launch (start us, length us, event | category | flops | bytes accessed | tf_op | source)
XLA Modules:
  0.0 2002.7 jit_solution(1369950110044074408)
XLA Ops:
  13.8 6.3 all_gather.39
  23.7 9.1 all_gather.38
  32.8 24.5 %all-gather.10.cloned.1.call-done = bf16[1536,1024]{1,0:T(8,128)(2,1)} async-done(((bf16[768,1024]{1,0:T(8,128)(2,1)}), bf16[1536,1024]{1,0:T(8,128)(2,1)}) %all-gather.10.cloned.1.call-update) | async-done | bytes 3145744 | tf_op jit(solution)/shard_map/all_gather | solution.py:187
  60.5 62.5 %all-gather.12.cloned.1.call-done = bf16[1536,2,1536]{2,0,1:T(8,128)(2,1)} async-done(((bf16[1536,2,384]{2,0,1:T(8,128)(2,1)}), bf16[1536,2,1536]{2,0,1:T(8,128)(2,1)}) %all-gather.12.cloned.1.call-update) | async-done | bytes 9437200 | tf_op jit(solution)/shard_map/all_gather | solution.py:192
  123.0 21.9 %fusion.187 = f32[1024,3352]{0,1:T(8,128)} fusion(bf16[1536,24]{0,1:T(8,128)(2,1)S(1)} %bitcast.860, bf16[1536,256]{0,1:T(8,128)(2,1)S(1)} %all_gather.38, bf16[1536,3072]{0,1:T(8,128)(2,1)} %bitcast.883, bf16[1536,1024]{1,0:T(8,128)(2,1)} %all-gather.10.cloned.1.call-done, f32[1536]{0:T(1024)S(1)} %convert_element_type.167, f32[1024]{0:T(1024)S(1)} %get-tuple-element.1441), kind=kOutput, calls=%fused_computation.282 | convolution fusion | flops 10581663744 | bytes 27183104 | tf_op jit(solution)/shard_map/dot_general | solution.py:199
  152.6 6.9 slice.341
  167.4 19.6 fusion.183
  187.0 8.1 reshape_reshape.6
  195.1 6.6 copy.371
  205.8 246.4 %while.83 = (s32[]{:T(128)}, f32[1,24,64,128]{3,2,1,0:T(8,128)S(1)}, f32[4,256,1,24,64]{1,0,4,3,2:T(4,128)}, f32[4,256,1,24,64]{1,4,3,2,0:T(8,128)}, f32[4,256,1...) while((s32[]{:T(128)}, ...), condition=%wide.region_6.7_spmd.clone, body=%wide.region_3.6_spmd.clone.sunk | while | flops 2528345088 | bytes 21093044 | solution.py:92
  218.9 9.4 fusion.311
  233.0 34.5 %dynamic_update_slice.91 = f32[4,256,1,24,64]{1,0,4,3,2:T(4,128)} dynamic-update-slice(f32[4,256,1,24,64]{1,0,4,3,2:T(4,128)} %get-tuple-element.1853, f32[1,256,1,24,64]{1,0,4,3,2:T(1,128)S(1)} %copy.552, s32[]{:T(128)S(6)} %copy.581, s32[]{:T(128)} %constant.234.clone.1..sunk, s32[]{:T(128)} %constant.234.clone.1..sunk, s32[]{:T(128)} %constant.234.clone.1..sunk, s32[]{:T(128)} %constant.234.clone.1..sunk) | dynamic-update-slice | bytes 3145732 | tf_op jit(solution)/shard_map/while/body/jit(dynamic_update_index_in_dim)/dynamic_update_slice | solution.py:92
  280.4 9.5 fusion.311
  294.7 34.5 %dynamic_update_slice.91 = f32[4,256,1,24,64]{1,0,4,3,2:T(4,128)} dynamic-update-slice(f32[4,256,1,24,64]{1,0,4,3,2:T(4,128)} %get-tuple-element.1853, f32[1,256,1,24,64]{1,0,4,3,2:T(1,128)S(1)} %copy.552, s32[]{:T(128)S(6)} %copy.581, s32[]{:T(128)} %constant.234.clone.1..sunk, s32[]{:T(128)} %constant.234.clone.1..sunk, s32[]{:T(128)} %constant.234.clone.1..sunk, s32[]{:T(128)} %constant.234.clone.1..sunk) | dynamic-update-slice | bytes 3145732 | tf_op jit(solution)/shard_map/while/body/jit(dynamic_update_index_in_dim)/dynamic_update_slice | solution.py:92
  342.0 9.3 fusion.311
  356.1 34.5 %dynamic_update_slice.91 = f32[4,256,1,24,64]{1,0,4,3,2:T(4,128)} dynamic-update-slice(f32[4,256,1,24,64]{1,0,4,3,2:T(4,128)} %get-tuple-element.1853, f32[1,256,1,24,64]{1,0,4,3,2:T(1,128)S(1)} %copy.552, s32[]{:T(128)S(6)} %copy.581, s32[]{:T(128)} %constant.234.clone.1..sunk, s32[]{:T(128)} %constant.234.clone.1..sunk, s32[]{:T(128)} %constant.234.clone.1..sunk, s32[]{:T(128)} %constant.234.clone.1..sunk) | dynamic-update-slice | bytes 3145732 | tf_op jit(solution)/shard_map/while/body/jit(dynamic_update_index_in_dim)/dynamic_update_slice | solution.py:92
  403.5 9.4 fusion.311
  417.7 34.5 %dynamic_update_slice.91 = f32[4,256,1,24,64]{1,0,4,3,2:T(4,128)} dynamic-update-slice(f32[4,256,1,24,64]{1,0,4,3,2:T(4,128)} %get-tuple-element.1853, f32[1,256,1,24,64]{1,0,4,3,2:T(1,128)S(1)} %copy.552, s32[]{:T(128)S(6)} %copy.581, s32[]{:T(128)} %constant.234.clone.1..sunk, s32[]{:T(128)} %constant.234.clone.1..sunk, s32[]{:T(128)} %constant.234.clone.1..sunk, s32[]{:T(128)} %constant.234.clone.1..sunk) | dynamic-update-slice | bytes 3145732 | tf_op jit(solution)/shard_map/while/body/jit(dynamic_update_index_in_dim)/dynamic_update_slice | solution.py:92
  461.4 13.3 reduce-window.90
  485.1 8.6 reshape.1247
  493.7 5.5 while.84
  499.2 9.6 fusion.173
  508.7 7.9 multiply_reduce_fusion.9
  521.7 7.4 all-gather.16.cloned.1.call-done
  529.1 38.8 %all-gather.14.cloned.1.call-done = bf16[1536,1536]{1,0:T(8,128)(2,1)} async-done(((bf16[1536,384]{1,0:T(8,128)(2,1)}), bf16[1536,1536]{1,0:T(8,128)(2,1)}) %all-gather.14.cloned.1.call-update) | async-done | bytes 4718608 | tf_op jit(solution)/shard_map/all_gather | solution.py:195
  567.9 12.3 multiply_reduce_fusion.3
  585.2 12.5 fusion.181
  600.4 6.0 fusion.177
  606.5 43.2 %while.86 = (s32[]{:T(128)}, f32[1,24,64,128]{3,2,1,0:T(8,128)S(1)}, f32[4,1,24,64,128]{4,3,2,1,0:T(8,128)}, f32[4,256,1,24,64]{1,4,3,2,0:T(8,128)}, f32[4,256,1...) while((s32[]{:T(128)}, ...), condition=%wide.region_21.22_spmd.clone, body=%wide.region_18.21_spmd.clone.sunk | while | flops 605971072 | bytes 5299361 | solution.py:92
  649.7 8.1 reshape_reshape.7
  657.8 7.1 fusion.174
  664.9 10.5 convolution_bitcast_fusion.3
  675.5 5.4 while.85
  688.3 433.7 %while.87 = (s32[]{:T(128)}, f32[1,24]{1,0:T(1,128)}, f32[1,24]{1,0:T(1,128)}, f32[1,24,64,128]{3,2,1,0:T(8,128)}, f32[4,256,1,24,64]{1,0,4,3,2:T(4,128)}, /*ind...) while((s32[]{:T(128)}, f32[1,24]{1,0:T(1,128)}, ...), condition=%wide.region_37.38_spmd.clone, body=%wide.region_22.37_spmd.clone.sunk | while | flops 5777224704 | bytes 64163144 | solution.py:92
  719.2 12.1 fusion.335
  737.2 6.4 fusion.341
  759.6 34.5 %dynamic_update_slice.94 = f32[4,256,1,24,64]{1,0,4,3,2:T(4,128)} dynamic-update-slice(f32[4,256,1,24,64]{1,0,4,3,2:T(4,128)} %get-tuple-element.1994, f32[1,256,1,24,64]{1,0,4,3,2:T(1,128)S(1)} %copy.569, s32[]{:T(128)S(6)} %sub.338, s32[]{:T(128)} %constant.234.clone.1..sunk.4, s32[]{:T(128)} %constant.234.clone.1..sunk.4, s32[]{:T(128)} %constant.234.clone.1..sunk.4, s32[]{:T(128)} %constant.234.clone.1..sunk.4) | dynamic-update-slice | bytes 3145732 | tf_op jit(solution)/shard_map/transpose(jvp())/while/body/jit(dynamic_update_index_in_dim)/dynamic_update_slice | solution.py:92
  824.5 12.1 fusion.335
  843.1 6.4 fusion.341
  866.2 34.5 %dynamic_update_slice.94 = f32[4,256,1,24,64]{1,0,4,3,2:T(4,128)} dynamic-update-slice(f32[4,256,1,24,64]{1,0,4,3,2:T(4,128)} %get-tuple-element.1994, f32[1,256,1,24,64]{1,0,4,3,2:T(1,128)S(1)} %copy.569, s32[]{:T(128)S(6)} %sub.338, s32[]{:T(128)} %constant.234.clone.1..sunk.4, s32[]{:T(128)} %constant.234.clone.1..sunk.4, s32[]{:T(128)} %constant.234.clone.1..sunk.4, s32[]{:T(128)} %constant.234.clone.1..sunk.4) | dynamic-update-slice | bytes 3145732 | tf_op jit(solution)/shard_map/transpose(jvp())/while/body/jit(dynamic_update_index_in_dim)/dynamic_update_slice | solution.py:92
  931.1 12.1 fusion.335
  949.7 6.4 fusion.341
  972.7 34.5 %dynamic_update_slice.94 = f32[4,256,1,24,64]{1,0,4,3,2:T(4,128)} dynamic-update-slice(f32[4,256,1,24,64]{1,0,4,3,2:T(4,128)} %get-tuple-element.1994, f32[1,256,1,24,64]{1,0,4,3,2:T(1,128)S(1)} %copy.569, s32[]{:T(128)S(6)} %sub.338, s32[]{:T(128)} %constant.234.clone.1..sunk.4, s32[]{:T(128)} %constant.234.clone.1..sunk.4, s32[]{:T(128)} %constant.234.clone.1..sunk.4, s32[]{:T(128)} %constant.234.clone.1..sunk.4) | dynamic-update-slice | bytes 3145732 | tf_op jit(solution)/shard_map/transpose(jvp())/while/body/jit(dynamic_update_index_in_dim)/dynamic_update_slice | solution.py:92
  1037.6 12.1 fusion.335
  1056.2 6.4 fusion.341
  1079.3 34.5 %dynamic_update_slice.94 = f32[4,256,1,24,64]{1,0,4,3,2:T(4,128)} dynamic-update-slice(f32[4,256,1,24,64]{1,0,4,3,2:T(4,128)} %get-tuple-element.1994, f32[1,256,1,24,64]{1,0,4,3,2:T(1,128)S(1)} %copy.569, s32[]{:T(128)S(6)} %sub.338, s32[]{:T(128)} %constant.234.clone.1..sunk.4, s32[]{:T(128)} %constant.234.clone.1..sunk.4, s32[]{:T(128)} %constant.234.clone.1..sunk.4, s32[]{:T(128)} %constant.234.clone.1..sunk.4) | dynamic-update-slice | bytes 3145732 | tf_op jit(solution)/shard_map/transpose(jvp())/while/body/jit(dynamic_update_index_in_dim)/dynamic_update_slice | solution.py:92
  1126.5 29.7 %reduce-window.92 = f32[24,8,128]{2,1,0:T(8,128)S(1)} reduce-window(f32[24,8,128]{2,1,0:T(8,128)S(1)} %bitcast.852, f32[]{:T(128)} %constant.235.clone.1), window={size=1x1x128 pad=0_0x0_0x0_127}, to_apply=%region_40.41 | reduce-window | flops 3121152 | bytes 196612 | tf_op jit(solution)/shard_map/reduce-window.11
  1159.9 6.7 fusion.202
  1175.2 11.7 multiply_reduce_fusion.6
  1186.9 7.5 broadcast_multiply_fusion
  1208.9 13.3 pad_add_fusion
  1232.7 19.5 fusion.169
  1252.2 6.6 copy.404
  1259.5 22.6 %fusion.205 = f32[3352,1536]{1,0:T(8,128)} fusion(bf16[1024,24]{0,1:T(8,128)(2,1)S(1)} %get-tuple-element.1388, bf16[1024,256]{0,1:T(8,128)(2,1)} %fusion.210, bf16[1024,1536]{0,1:T(8,128)(2,1)} %copy-done.25, bf16[1024,1536]{0,1:T(8,128)(2,1)S(1)} %copy-done.23, bf16[1536,1024]{1,0:T(8,128)(2,1)} %all-gather.10.cloned.1.call-done, ...), kind=kOutput, calls=%fused_computation.306 | convolution fusion | flops 10578231296 | bytes 30615552 | tf_op jit(solution)/shard_map/dot_general | solution.py:334
  1287.0 11.5 fusion.241
  1304.7 5.2 all-reduce.23
  1310.6 27.5 %reduce-scatter.10.cloned.1.call-done = f32[768,1024]{0,1:T(8,128)} async-done(((f32[1536,1024]{0,1:T(8,128)}), f32[768,1024]{0,1:T(8,128)}) %reduce-scatter.10.cloned.1.call-update) | async-done | bytes 3145744 | tf_op jit(solution)/shard_map/reduce_scatter | solution.py:320
  1344.2 14.8 slice.376
  1359.0 18.7 copy.405
  1377.7 20.5 %reduce-scatter.16.cloned.1.call-done = f32[96,24]{1,0:T(8,128)} async-done(((f32[1536,24]{1,0:T(8,128)}), f32[96,24]{1,0:T(8,128)}) %reduce-scatter.16.cloned.1.call-update) | async-done | bytes 9232
  1399.6 136.2 %all-reduce.28.cloned.1.call-done = f32[1536,256]{0,1:T(8,128)} async-done(((f32[1536,256]{0,1:T(8,128)}), f32[1536,256]{0,1:T(8,128)}) %all-reduce.28.cloned.1.call-update) | async-done | bytes 1572880 | tf_op jit(solution)/shard_map/psum | solution.py:347
  1542.1 109.2 %reduce-scatter.14.cloned.1.call-done = f32[1536,96]{0,1:T(8,128)} async-done(((f32[1536,1536]{0,1:T(8,128)}), f32[1536,96]{0,1:T(8,128)}) %reduce-scatter.14.cloned.1.call-update) | async-done | bytes 589840 | tf_op jit(solution)/shard_map/reduce_scatter | solution.py:345
  1651.3 132.2 %all-reduce.30.cloned.1.call-done = (f32[1536]{0:T(1024)}, f32[4,3072]{1,0:T(4,128)}, f32[3072]{0:T(1024)}, f32[4,256]{1,0:T(4,128)}, f32[256]{0:T(256)}, /*inde...) async-done(((f32[1536]{0:T(1024)}, f32[4,3072]{1,0:T(4,128)}, f32[3072]{0:T(1024)}, f32[4,256]{1,0:T(4,128)}, f32[256]{0:T(256)}, /*index=5*/f32[48]{0:T(128)}, ...) | async-done | bytes 85584 | tf_op jit(solution)/shard_map/psum | solution.py:347
  1783.5 201.2 %reduce-scatter.12.cloned.1.call-done = f32[1536,2,96]{0,2,1:T(8,128)} async-done(((f32[1536,2,1536]{0,2,1:T(8,128)}), f32[1536,2,96]{0,2,1:T(8,128)}) %reduce-scatter.12.cloned.1.call-update) | async-done | bytes 1179664 | tf_op jit(solution)/shard_map/reduce_scatter | solution.py:343
  (934 shorter events, 480.7 us)
Async XLA Ops:
  7.3 15.1 copy-start.105
  7.3 15.6 copy-start.97
  7.3 50.0 %all-gather.10.cloned.1.call-start = ((), (), s32[]{:S(2)}) async-start(), calls=%async_computation.5 | async-start | bytes 4718592 | tf_op jit(solution)/shard_map/all_gather | solution.py:187
  8.0 115.0 %all-gather.12.cloned.1.call-start = ((), (), s32[]{:S(2)}) async-start(), calls=%async_computation.6 | async-start | bytes 11796480 | tf_op jit(solution)/shard_map/all_gather | solution.py:192
  11.5 482.2 %all-gather.18.cloned.1.call-start = ((), (), s32[]{:S(2)}) async-start(), calls=%async_computation.14 | async-start | bytes 3932160 | tf_op jit(solution)/shard_map/all_gather | solution.py:24
  13.0 131.9 %copy-start.94 = (f32[1536]{0:T(1024)}, f32[1536]{0:T(1024)S(1)}, u32[]{:S(2)}) copy-start(f32[1536]{0:T(1024)S(1)} %convert_element_type.167) | copy-start | bytes 18436
  20.1 124.8 %copy-start.52 = (bf16[24,1536]{1,0:T(8,128)(2,1)}, bf16[24,1536]{1,0:T(8,128)(2,1)S(1)}, u32[]{:S(2)}) copy-start(bf16[24,1536]{1,0:T(8,128)(2,1)S(1)} %all_gather.39) | copy-start | bytes 221188
  22.3 145.0 %copy-start.54 = (f32[1536]{0:T(1024)}, f32[1536]{0:T(1024)S(1)}, u32[]{:S(2)}) copy-start(f32[1536]{0:T(1024)S(1)} %get-tuple-element.1274) | copy-start | bytes 18436
  22.3 145.0 %copy-start.56 = (f32[1536]{0:T(1024)}, f32[1536]{0:T(1024)S(1)}, u32[]{:S(2)}) copy-start(f32[1536]{0:T(1024)S(1)} %get-tuple-element.1275) | copy-start | bytes 18436
  22.4 145.0 %copy-start.58 = (f32[1536]{0:T(1024)}, f32[1536]{0:T(1024)S(1)}, u32[]{:S(2)}) copy-start(f32[1536]{0:T(1024)S(1)} %get-tuple-element.1276) | copy-start | bytes 18436
  22.4 145.0 %copy-start.60 = (f32[1536]{0:T(1024)}, f32[1536]{0:T(1024)S(1)}, u32[]{:S(2)}) copy-start(f32[1536]{0:T(1024)S(1)} %get-tuple-element.1277) | copy-start | bytes 18436
  22.9 139.8 %copy-start.86 = (f32[1,256]{1,0:T(1,128)}, f32[1,256]{1,0:T(1,128)S(1)}, u32[]{:S(2)}) copy-start(f32[1,256]{1,0:T(1,128)S(1)} %get-tuple-element.1444) | copy-start | bytes 3076
  22.9 139.8 %copy-start.88 = (f32[1,256]{1,0:T(1,128)}, f32[1,256]{1,0:T(1,128)S(1)}, u32[]{:S(2)}) copy-start(f32[1,256]{1,0:T(1,128)S(1)} %get-tuple-element.1445) | copy-start | bytes 3076
  22.9 139.8 %copy-start.90 = (f32[1,256]{1,0:T(1,128)}, f32[1,256]{1,0:T(1,128)S(1)}, u32[]{:S(2)}) copy-start(f32[1,256]{1,0:T(1,128)S(1)} %get-tuple-element.1446) | copy-start | bytes 3076
  22.9 139.8 %copy-start.92 = (f32[1,256]{1,0:T(1,128)}, f32[1,256]{1,0:T(1,128)S(1)}, u32[]{:S(2)}) copy-start(f32[1,256]{1,0:T(1,128)S(1)} %get-tuple-element.1447) | copy-start | bytes 3076
  23.7 143.7 %copy-start.43 = (f32[1024]{0:T(1024)}, f32[1024]{0:T(1024)S(1)}, u32[]{:S(2)}) copy-start(f32[1024]{0:T(1024)S(1)} %get-tuple-element.1437) | copy-start | bytes 12292
  23.7 143.7 %copy-start.45 = (f32[1024]{0:T(1024)}, f32[1024]{0:T(1024)S(1)}, u32[]{:S(2)}) copy-start(f32[1024]{0:T(1024)S(1)} %get-tuple-element.1438) | copy-start | bytes 12292
  23.7 143.7 %copy-start.47 = (f32[1024]{0:T(1024)}, f32[1024]{0:T(1024)S(1)}, u32[]{:S(2)}) copy-start(f32[1024]{0:T(1024)S(1)} %get-tuple-element.1439) | copy-start | bytes 12292
  23.7 460.7 %copy-start.66 = (f32[1024]{0:T(1024)}, f32[1024]{0:T(1024)S(1)}, u32[]{:S(2)}) copy-start(f32[1024]{0:T(1024)S(1)} %get-tuple-element.1436) | copy-start | bytes 12292
  32.8 112.1 %copy-start.30 = (bf16[1536,256]{0,1:T(8,128)(2,1)}, bf16[1536,256]{0,1:T(8,128)(2,1)S(1)}, u32[]{:S(2)}) copy-start(bf16[1536,256]{0,1:T(8,128)(2,1)S(1)} %all_gather.38) | copy-start | bytes 2359300
  60.5 84.4 %copy-start.78 = (f32[1024]{0:T(1024)}, f32[1024]{0:T(1024)S(1)}, u32[]{:S(2)}) copy-start(f32[1024]{0:T(1024)S(1)} %get-tuple-element.1441) | copy-start | bytes 12292
  123.0 25.1 %copy-start.103 = (f32[24]{0:T(128)S(1)}, f32[24]{0:T(128)}, u32[]{:S(2)}) copy-start(f32[24]{0:T(128)} %param.37) | copy-start | bytes 292
  145.9 16.7 collective-permute-start.1
  160.4 6.6 collective-permute-start
  162.7 24.3 %copy-start.34 = (f32[3,256]{0,1:T(8,128)}, f32[3,256]{0,1:T(8,128)S(1)}, u32[]{:S(2)}) copy-start(f32[3,256]{0,1:T(8,128)S(1)} %collective-permute-done.1) | copy-start | bytes 9220
  167.3 19.7 copy-start.18
  452.2 41.4 %copy-start.67 = (f32[24]{0:T(128)}, f32[24]{0:T(128)S(1)}, u32[]{:S(2)}) copy-start(f32[24]{0:T(128)S(1)} %get-tuple-element.2121) | copy-start | bytes 292
  453.1 76.0 %all-gather.16.cloned.1.call-start = ((), (), s32[]{:S(2)}) async-start(), calls=%async_computation.9 | async-start | bytes 4718592 | tf_op jit(solution)/shard_map/all_gather | solution.py:263
  456.9 20.5 %copy-start.64 = (f32[1024]{0:T(1024)}, f32[1024]{0:T(1024)S(1)}, u32[]{:S(2)}) copy-start(f32[1024]{0:T(1024)S(1)} %fusion.227) | copy-start | bytes 12292
  458.4 109.5 %all-gather.14.cloned.1.call-start = ((), (), s32[]{:S(2)}) async-start(), calls=%async_computation.7 | async-start | bytes 5898240 | tf_op jit(solution)/shard_map/all_gather | solution.py:195
  459.0 216.5 %all-gather.20.cloned.1.call-start = ((), (), s32[]{:S(2)}) async-start(), calls=%async_computation.15 | async-start | bytes 3932160 | tf_op jit(solution)/shard_map/all_gather | solution.py:24
  459.1 205.8 %copy-start.73 = (f32[1536]{0:T(1024)}, f32[1536]{0:T(1024)S(1)}, u32[]{:S(2)}) copy-start(f32[1536]{0:T(1024)S(1)} %convert_element_type.176) | copy-start | bytes 18436
  521.7 143.3 %copy-start.80 = (f32[1024]{0:T(1024)}, f32[1024]{0:T(1024)S(1)}, u32[]{:S(2)}) copy-start(f32[1024]{0:T(1024)S(1)} %get-tuple-element.1443) | copy-start | bytes 12292
  585.2 15.3 copy-start.26
  606.5 704.1 %reduce-scatter.8.cloned.1.call-start = ((), (), s32[]{:S(2)}) async-start(), calls=%async_computation.8 | async-start | bytes 9437184 | tf_op jit(solution)/shard_map/reduce_scatter | solution.py:258
  649.7 15.2 slice-start.6
  675.4 662.7 %reduce-scatter.10.cloned.1.call-start = ((), (), s32[]{:S(2)}) async-start(), calls=%async_computation.10 | async-start | bytes 9437184 | tf_op jit(solution)/shard_map/reduce_scatter | solution.py:320
  719.2 13.6 copy-start.1
  931.0 13.6 copy-start.1
  1037.6 13.6 copy-start.1
  1122.1 44.5 %copy-start.16 = (f32[1024,256]{0,1:T(8,128)S(1)}, f32[1024,256]{0,1:T(8,128)}, u32[]{:S(2)}) copy-start(f32[1024,256]{0,1:T(8,128)} %copy-done.15) | copy-start | bytes 3145732
  1122.1 44.5 %copy-start.22 = (f32[1024,256]{0,1:T(8,128)S(1)}, f32[1024,256]{0,1:T(8,128)}, u32[]{:S(2)}) copy-start(f32[1024,256]{0,1:T(8,128)} %get-tuple-element.1396) | copy-start | bytes 3145732
  1122.1 44.5 %copy-start.35 = (f32[3,256]{0,1:T(8,128)S(1)}, f32[3,256]{0,1:T(8,128)}, u32[]{:S(2)}) copy-start(f32[3,256]{0,1:T(8,128)} %copy-done.34) | copy-start | bytes 9220
  1122.1 44.5 %copy-start.44 = (f32[1024]{0:T(1024)S(1)}, f32[1024]{0:T(1024)}, u32[]{:S(2)}) copy-start(f32[1024]{0:T(1024)} %copy-done.43) | copy-start | bytes 12292
  1122.1 44.5 %copy-start.46 = (f32[1024]{0:T(1024)S(1)}, f32[1024]{0:T(1024)}, u32[]{:S(2)}) copy-start(f32[1024]{0:T(1024)} %copy-done.45) | copy-start | bytes 12292
  1122.1 44.5 %copy-start.48 = (f32[1024]{0:T(1024)S(1)}, f32[1024]{0:T(1024)}, u32[]{:S(2)}) copy-start(f32[1024]{0:T(1024)} %copy-done.47) | copy-start | bytes 12292
  1170.6 53.3 %collective-permute-start.3 = (f32[3,256]{0,1:T(8,128)S(1)}, f32[3,256]{0,1:T(8,128)}, u32[]{:S(2)}, u32[]{:S(2)}) collective-permute-start(f32[3,256]{0,1:T(8,128)S(1)} %pad_add_fusion.3), channel_id=1, source_target_pairs={{2,0},{4,2},{6,4},{3,1},{5,3},{7,5},{10,8},{12,10},{14,12},{11,9},... | collective-permute-start | bytes 9224 | tf_op jit(solution)/shard_map/ppermute | solution.py:19
  1205.3 20.7 %collective-permute-start.2 = (f32[3,1536]{1,0:T(4,128)}, f32[3,1536]{1,0:T(4,128)}, u32[]{:S(2)}, u32[]{:S(2)}) collective-permute-start(f32[3,1536]{1,0:T(4,128)} %copy.395), channel_id=1, source_target_pairs={{2,0},{4,2},{6,4},{3,1},{5,3},{7,5},{10,8},{12,10},{14,12},{11,9},... | collective-permute-start | bytes 55304 | tf_op jit(solution)/shard_map/ppermute | solution.py:19
  1232.6 19.6 copy-start.25
  1258.8 139.3 %reduce-scatter.16.cloned.1.call-start = ((), (), s32[]{:S(2)}) async-start(), calls=%async_computation.16 | async-start | bytes 835584
  1284.2 251.6 %all-reduce.28.cloned.1.call-start = ((), (), s32[]{:S(2)}) async-start(), calls=%async_computation.12 | async-start | bytes 3145728 | tf_op jit(solution)/shard_map/psum | solution.py:347
  1287.0 364.3 %reduce-scatter.14.cloned.1.call-start = ((), (), s32[]{:S(2)}) async-start(), calls=%async_computation.13 | async-start | bytes 10027008 | tf_op jit(solution)/shard_map/reduce_scatter | solution.py:345
  1298.7 39.4 %copy-start.13 = (bf16[768,1024]{0,1:T(8,128)(2,1)S(1)}, bf16[768,1024]{0,1:T(8,128)(2,1)}, u32[]{:S(2)}) copy-start(bf16[768,1024]{0,1:T(8,128)(2,1)} %copy-done.12) | copy-start | bytes 4718596
  1298.7 39.4 %copy-start.65 = (f32[1024]{0:T(1024)S(1)}, f32[1024]{0:T(1024)}, u32[]{:S(2)}) copy-start(f32[1024]{0:T(1024)} %copy-done.64) | copy-start | bytes 12292
  1298.7 39.4 %copy-start.77 = (f32[1024]{0:T(1024)S(1)}, f32[1024]{0:T(1024)}, u32[]{:S(2)}) copy-start(f32[1024]{0:T(1024)} %get-tuple-element.1440) | copy-start | bytes 12292
  1298.8 484.8 %all-reduce.30.cloned.1.call-start = ((), (), s32[]{:S(2)}) async-start(), calls=%async_computation.17 | async-start | bytes 177152 | tf_op jit(solution)/shard_map/psum | solution.py:347
  1302.5 40.7 %copy-start.62 = (f32[3072]{0:T(1024)}, f32[3072]{0:T(1024)S(1)}, u32[]{:S(2)}) copy-start(f32[3072]{0:T(1024)S(1)} %dynamic_update_slice.73) | copy-start | bytes 36868
  1302.9 40.3 %copy-start.63 = (f32[3072]{0:T(1024)}, f32[3072]{0:T(1024)S(1)}, u32[]{:S(2)}) copy-start(f32[3072]{0:T(1024)S(1)} %dynamic_update_slice.69) | copy-start | bytes 36868
  1303.1 40.0 %copy-start.109 = (f32[48]{0:T(128)}, f32[48]{0:T(128)S(1)}, u32[]{:S(2)}) copy-start(f32[48]{0:T(128)S(1)} %dynamic_update_slice.70) | copy-start | bytes 580
  1304.5 38.7 %copy-start.110 = (f32[48]{0:T(128)}, f32[48]{0:T(128)S(1)}, u32[]{:S(2)}) copy-start(f32[48]{0:T(128)S(1)} %bitcast_dynamic-update-slice_fusion.1) | copy-start | bytes 580
  1304.6 38.6 %copy-start.108 = (f32[48]{0:T(128)}, f32[48]{0:T(128)S(1)}, u32[]{:S(2)}) copy-start(f32[48]{0:T(128)S(1)} %fusion.233) | copy-start | bytes 580
  1304.6 38.6 %copy-start.50 = (f32[4,3072]{1,0:T(4,128)}, f32[4,3072]{1,0:T(4,128)S(1)}, u32[]{:S(2)}) copy-start(f32[4,3072]{1,0:T(4,128)S(1)} %add_dynamic-update-slice_fusion) | copy-start | bytes 147460
  1344.1 640.6 %reduce-scatter.12.cloned.1.call-start = ((), (), s32[]{:S(2)}) async-start(), calls=%async_computation.11 | async-start | bytes 20054016 | tf_op jit(solution)/shard_map/reduce_scatter | solution.py:343
  1377.7 161.2 %copy-start.21 = (bf16[768,1024]{0,1:T(8,128)(2,1)S(1)}, bf16[768,1024]{0,1:T(8,128)(2,1)}, u32[]{:S(2)}) copy-start(bf16[768,1024]{0,1:T(8,128)(2,1)} %get-tuple-element.1427) | copy-start | bytes 4718596
  (121 other events, 780.6 us)
Sparse Core Ops, SparseCore 0:
  9.7 47.6 all-gather.9
  58.9 64.1 all-gather.11
  453.3 28.7 all-gather.17
  484.0 45.0 all-gather.15
  530.5 37.3 all-gather.13
  606.6 28.5 all-gather.19
  675.5 76.8 reduce-scatter.7
  1259.0 79.1 reduce-scatter.9
  1341.7 56.4 reduce-scatter.15
  1404.7 131.0 all-reduce.27
  1541.0 110.2 reduce-scatter.13
  1658.7 124.7 all-reduce.29
  1788.8 195.9 reduce-scatter.11
where the time goes:
time: 2030 us; the launch traced here: 2000 us
  waiting for transfers between devices  762 us (38%)
  local copies, waits for them, and re-layouts  582 us (29%)
  matrix products  330 us (16%)
  other arithmetic  255 us (13%)
  blocking collectives  35.5 us (2%)
    dynamic_update_slice x32, local copies, waits for them, and re-layouts, scan_spans(): final, outputs = lax.scan(jax.checkpoint(step), state, pieces)  312 us
    psum x2, waiting for transfers between devices, per_device(): lax.psum((grad_state_w, place_block(grad_gain_here, ncols, col_index, 0),...  268 us
    reduce_scatter x1, waiting for transfers between devices, per_device(): lax.psum_scatter(grad_inner_w, ('dp', 'row'), scatter_dimension=2, tiled=...  201 us
    dot_general x12, matrix products, span_step(): inner = jnp.einsum('ijgk,jgkp->igkp', mixing, values, precision=PRECISE)  112 us
    reduce_scatter x1, waiting for transfers between devices, per_device(): lax.psum_scatter(grad_out_w, ('dp', 'row'), scatter_dimension=1, tiled=True)  109 us
    another operation x51, other arithmetic  68.4 us
    all_gather x1, waiting for transfers between devices, per_device(): lax.all_gather(inner_proj, 'row', axis=2, tiled=True)  62.5 us
    unnamed x247, local copies, waits for them, and re-layouts  58.2 us
  transfers between devices with their start and end apart: 17, of which 10 were waited for; matrix products, arithmetic and copies ran while one was open for 40% of the time, Pallas kernels for 0%

commit v1 on v0

v1 whole, which is shorter than its diff:
```python
import functools

import jax
import jax.numpy as jnp
from jax import lax
from jax.experimental import pallas as pl
from jax.experimental.pallas import tpu as pltpu
from jax.sharding import PartitionSpec as P

HEADDIM = 64
STATE = 128
CONV = 4
Q = 128
EPS = 1e-05
LOG2E = 1.4426950408889634
F32 = jnp.float32
BF16 = jnp.bfloat16
HIGHEST = lax.Precision.HIGHEST
MESH = pl.DeviceIdType.MESH
VMEM_LIMIT = 56 * 1024 * 1024
CUM, STEP, ENTRY, TAIL, DEC, SIG = range(6)


def nn(a, b, precision=None):
    return lax.dot_general(a, b, (((1,), (0,)), ((), ())), precision=precision, preferred_element_type=F32)


def nt(a, b, precision=None):
    return lax.dot_general(a, b, (((1,), (1,)), ((), ())), precision=precision, preferred_element_type=F32)


def tn(a, b, precision=None):
    return lax.dot_general(a, b, (((0,), (0,)), ((), ())), precision=precision, preferred_element_type=F32)


def halves(v):
    high = v.astype(BF16)
    return high, (v - high.astype(F32)).astype(BF16)


def nn3(a, b):
    (ah, al), (bh, bl) = halves(a), halves(b)
    return nn(jnp.concatenate([ah, ah, al], 1), jnp.concatenate([bh, bl, bh], 0))


def nt3(a, b):
    (ah, al), (bh, bl) = halves(a), halves(b)
    return nt(jnp.concatenate([ah, ah, al], 1), jnp.concatenate([bh, bl, bh], 1))


def sigm(v):
    return 0.5 + 0.5 * jnp.tanh(0.5 * v)


def iota(shape, dim):
    return lax.broadcasted_iota(jnp.int32, shape, dim)


def segment_of(place, ends):
    total = (place >= ends[0]).astype(jnp.int32)
    for end in ends[1:]:
        total = total + (place >= end).astype(jnp.int32)
    return jnp.where(place < 0, -1, total)


def chunk_of(c):
    return pl.ds(pl.multiple_of(c * Q, Q), Q)


def shift_masks(place, ends):
    segment = segment_of(place, ends)
    return [(segment_of(place - d, ends) == segment).astype(F32) for d in range(1, CONV)]


def shifted_right(now, earlier, d, lane):
    return pltpu.roll(jnp.where(lane >= Q - d, earlier, now), d, 1)


def shifted_left(now, later, d, lane):
    return pltpu.roll(jnp.where(lane < d, later, now), Q - d, 1)


def conv_tile(now, earlier, taps, masks, lane):
    total = taps(CONV) + taps(CONV - 1) * now
    for d in range(1, CONV):
        total = total + taps(CONV - 1 - d) * (shifted_right(now, earlier, d, lane) * masks[d - 1])
    return total


def spread(rows_ref, out):
    cols = jnp.transpose(rows_ref[...])
    for k in range(out.shape[0]):
        out[k] = jnp.broadcast_to(cols[:, k : k + 1], out.shape[1:])


def thirds(v):
    high, rest = v.astype(BF16), v
    rest = rest - high.astype(F32)
    middle = rest.astype(BF16)
    return jnp.concatenate([high, middle, (rest - middle.astype(F32)).astype(BF16)], -1)


def times_flags(v, flags):
    return nn(thirds(v), jnp.concatenate([flags.astype(BF16)] * 3, 0))


def stacked(v, count):
    return jnp.concatenate([v[:, c * Q : (c + 1) * Q] for c in range(count)], 0)


def scalars(lengths_ref, rows):
    ends = [lengths_ref[0, 0]]
    for k in range(1, lengths_ref.shape[1]):
        ends.append(ends[-1] + lengths_ref[0, k])
    return lax.axis_index("row") * rows, ends


def enter_kernel(nc, hb, place_ref, xin_ref, bcin_ref, dt_ref, heads_ref, taps8_ref, bctaps8_ref, wait_ref,
                 u_ref, ubc_ref, bc_ref, rows_ref, scores_ref, y_ref, fresh_ref, final_ref, pass_ref, hpar_ref, state, taps_ref, bctaps_ref):
    base, ends = scalars(place_ref, nc * Q)
    wide = iota((HEADDIM, Q), 1)
    block = pl.program_id(0)
    spread(taps8_ref, taps_ref)

    @pl.when(block == 0)
    def _():
        spread(bctaps8_ref, bctaps_ref)
        lane = iota((1, Q), 1)
        row, col = iota((Q, Q), 0), iota((Q, Q), 1)

        def body(c, _):
            masks = shift_masks(base + c * Q + lane, ends)
            for part in range(2 * STATE // HEADDIM):
                at = slice(part * HEADDIM, (part + 1) * HEADDIM)
                u = conv_tile(bcin_ref[at, chunk_of(c + 1)], bcin_ref[at, chunk_of(c)], lambda k: bctaps_ref[k, at, :], masks, wide)
                ubc_ref[at, chunk_of(c)] = u
                bc_ref[at, chunk_of(c)] = u * sigm(u)
            start = base + c * Q
            same = (segment_of(start + row, ends) == segment_of(start + col, ends)) & (row >= col)
            score = nn3(jnp.transpose(bc_ref[STATE:, chunk_of(c)]), bc_ref[:STATE, chunk_of(c)])
            scores_ref[c] = jnp.where(same, score, 0.0)
            return 0

        lax.fori_loop(0, nc, body, 0, unroll=2)

        nb = dt_ref.shape[0]
        by_head = jnp.transpose(heads_ref[...])[:, :8]
        for n in range(nb):
            own = by_head[n * hb : (n + 1) * hb]
            hpar_ref[n] = own if hb == 8 else jnp.concatenate([own, jnp.zeros((8 - hb, 8), F32)], 0)
        raw = jnp.concatenate([dt_ref[n] + hpar_ref[n, :, 0:1] for n in range(nb)], 0)
        rate = jnp.concatenate([-jnp.exp(hpar_ref[n, :, 1:2]) for n in range(nb)], 0)
        small = jnp.exp(-jnp.abs(raw))
        steps = jnp.maximum(raw, 0.0) + jnp.log1p(small)
        sig = jnp.where(raw >= 0, 1.0, small) / (1.0 + small)
        each = nb * 8
        cums = times_flags(stacked(steps * rate * LOG2E, nc), row <= col)
        whole_sum = jnp.zeros((each, 1), F32)
        for c in range(nc):
            at = slice(c * Q, (c + 1) * Q)
            start = base + c * Q
            segment = segment_of(start + lane, ends)
            before = segment_of(start - 1, ends)
            after = segment_of(start + Q - 1, ends)
            cum = cums[c * each : (c + 1) * each]
            last = cum[:, Q - 1 : Q]
            entry = jnp.exp2(cum) * (segment == before).astype(F32)
            tail = jnp.exp2(last - cum) * (segment == after).astype(F32)
            decay = jnp.broadcast_to(jnp.exp2(last), (each, Q)) * (before == after).astype(F32)
            for n in range(nb):
                part = slice(n * 8, (n + 1) * 8)
                rows_ref[n, CUM, :, at] = cum[part]
                rows_ref[n, STEP, :, at] = steps[part, at]
                rows_ref[n, ENTRY, :, at] = entry[part]
                rows_ref[n, TAIL, :, at] = tail[part]
                rows_ref[n, DEC, :, at] = decay[part]
                rows_ref[n, SIG, :, at] = sig[part, at]
            whole_sum = whole_sum + last
        end = segment_of(base + nc * Q - 1, ends)
        keep = jnp.broadcast_to(jnp.exp2(whole_sum), (each, Q)) * (segment_of(base - 1, ends) == end).astype(F32)
        for n in range(nb):
            pass_ref[n] = keep[n * 8 : (n + 1) * 8]

    state[...] = jnp.zeros_like(state)

    def chunk(c, _):
        now = chunk_of(c)
        masks = shift_masks(base + c * Q + iota((1, Q), 1), ends)
        cum8 = rows_ref[block, CUM, :, now]
        cols = jnp.transpose(cum8)
        weighted = []
        for h in range(hb):
            at = slice(h * HEADDIM, (h + 1) * HEADDIM)
            hr = slice(h, h + 1)
            u = conv_tile(xin_ref[at, chunk_of(c + 1)], xin_ref[at, now], lambda k: taps_ref[k, at, :], masks, wide)
            u_ref[at, now] = u
            x = u * sigm(u)
            moved = x * rows_ref[block, STEP, hr, now]
            decay = jnp.exp2(jnp.minimum(cols[:, hr] - cum8[hr, :], 0.0))
            mixing = (decay * scores_ref[c]).astype(BF16)
            y_ref[at, now] = nt(moved.astype(BF16), mixing) + hpar_ref[block, hr, 2:3] * x
            weighted.append((moved * rows_ref[block, TAIL, hr, now]).astype(BF16))
        fresh = nt(jnp.concatenate(weighted, 0), bc_ref[:STATE, now].astype(BF16))
        fresh_ref[c] = fresh
        for h in range(hb):
            at = slice(h * HEADDIM, (h + 1) * HEADDIM)
            state[at, :] = state[at, :] * rows_ref[block, DEC, h : h + 1, now] + fresh[at, :]
        return 0

    lax.fori_loop(0, nc, chunk, 0, unroll=2)
    final_ref[...] = state[...].astype(BF16)


def across_kernel(nc, hb, y_ref, fresh_ref, start_ref, bc_ref, rows_ref, z_ref, gg_ref, gate8_ref,
                  y_out, states_ref, stat_ref, state, gate_ref):
    first = pl.program_id(0) == 0

    @pl.when(first)
    def _():
        stat_ref[...] = jnp.zeros_like(stat_ref)

    state[...] = start_ref[...]
    spread(gate8_ref, gate_ref)

    def chunk(c, _):
        states_ref[c] = state[...]
        outer = nn3(state[...], bc_ref[STATE:, chunk_of(c)])
        square = jnp.zeros((8, Q), F32)
        cross = jnp.zeros((8, Q), F32)
        for h in range(hb):
            at = slice(h * HEADDIM, (h + 1) * HEADDIM)
            y = y_ref[at, chunk_of(c)] + outer[at, :] * rows_ref[0, ENTRY, h : h + 1, chunk_of(c)]
            y_out[at, chunk_of(c)] = y
            z = z_ref[at, chunk_of(c)]
            gz = y * (z * sigm(z))
            other = gz * gate_ref[0, at, :] * gg_ref[at, chunk_of(c)]
            squared = gz * gz
            for k in range(HEADDIM // 8):
                square = square + squared[k * 8 : (k + 1) * 8]
                cross = cross + other[k * 8 : (k + 1) * 8]
            state[at, :] = state[at, :] * rows_ref[0, DEC, h : h + 1, chunk_of(c)] + fresh_ref[c, at, :]
        stat_ref[0, :, chunk_of(c)] += square
        stat_ref[1, :, chunk_of(c)] += cross
        return 0

    lax.fori_loop(0, nc, chunk, 0, unroll=2)


def lane_sums(v):
    return nt(jnp.ones((8, 2 * Q), BF16), jnp.concatenate(halves(v), 1))


def gate_kernel(nc, hb, y_ref, z_ref, gg_ref, tok_ref, gate8_ref, bc_ref, rows_ref,
                gated_ref, gz_ref, gy_ref, adj_ref, first_ref, ggate_ref, adjoint, gsum, gate_ref):
    spread(gate8_ref, gate_ref)
    adjoint[...] = jnp.zeros_like(adjoint)
    gsum[...] = jnp.zeros_like(gsum)

    def chunk(k, _):
        c = nc - 1 - k
        rstd = tok_ref[0:1, chunk_of(c)]
        pull = tok_ref[1:2, chunk_of(c)]
        lifted = []
        for h in range(hb):
            at = slice(h * HEADDIM, (h + 1) * HEADDIM)
            y, z, gg = y_ref[at, chunk_of(c)], z_ref[at, chunk_of(c)], gg_ref[at, chunk_of(c)]
            s = sigm(z)
            silu = z * s
            gz = y * silu
            gate = gate_ref[0, at, :]
            gzr = gz * rstd
            gated_ref[at, chunk_of(c)] = (gzr * gate).astype(BF16)
            gsum[at, :] += gzr * gg
            ggz = rstd * (gate * gg) - gz * pull
            gy = ggz * silu
            gz_ref[at, chunk_of(c)] = (ggz * y * (s * (1.0 + z * (1.0 - s)))).astype(BF16)
            gy_ref[at, chunk_of(c)] = gy
            lifted.append(gy * rows_ref[0, ENTRY, h : h + 1, chunk_of(c)])
        adj = nt3(jnp.concatenate(lifted, 0), bc_ref[STATE:, chunk_of(c)])
        adj_ref[c] = adj
        for h in range(hb):
            at = slice(h * HEADDIM, (h + 1) * HEADDIM)
            adjoint[at, :] = adjoint[at, :] * rows_ref[0, DEC, h : h + 1, chunk_of(c)] + adj[at, :]
        return 0

    lax.fori_loop(0, nc, chunk, 0, unroll=2)
    first_ref[...] = adjoint[...].astype(BF16)
    ggate_ref[...] = lane_sums(gsum[...])


def conv_back(gu, later, taps, masks, lane):
    moved = [gu]
    total = taps(CONV - 1) * gu
    for d in range(1, CONV):
        part = shifted_left(gu * masks[d - 1], later * masks[CONV - 1 + d - 1], d, lane)
        moved.append(part)
        total = total + taps(CONV - 1 - d) * part
    return total, moved


def conv_rim(gu, taps, masks, lane, rim_in):
    total = jnp.zeros_like(gu)
    sums = []
    for d in range(1, CONV):
        part = pltpu.roll(jnp.where(lane < d, gu * masks[d - 1], 0.0), Q - d, 1)
        total = total + taps(CONV - 1 - d) * part
        sums.append(rim_in * part)
    return total, sums


def back_masks(base, c, ends):
    lane = iota((1, Q), 1)
    return shift_masks(base + c * Q + lane, ends) + shift_masks(base + (c + 1) * Q + lane, ends)


def total_rows(v):
    return jnp.sum(v, 0, keepdims=True)


def early_sums(early, n_dp, grads, outs, come1, come2, come3, sems):
    half = grads[0].shape[0] // 2
    views = []
    for k, (a, at, width) in enumerate(early["pieces"]):
        columns = pl.ds(at, width)
        views.append((grads[a].at[pl.ds(0, half), columns], grads[a].at[pl.ds(half, half), columns], come1.at[k], come2.at[k], come3.at[k],
                      outs[a].at[:, columns]))
    return RowSums(n_dp, views, sems)


def sent_sums(early, n_dp, grads, outs, *refs):
    sums = early_sums(early, n_dp, grads, outs, *refs)
    groups = early["groups"]
    for t in range(early["steps"]):
        @pl.when(pl.program_id(0) == t)
        def _():
            if t == 0:
                meet(sums.partners())
            for stage, lag in ((sums.along, 2), (sums.across, 1), (sums.pair, 0), (sums.finish, 3)):
                if 0 <= t - lag < len(groups):
                    for p in groups[t - lag]:
                        stage(p)


def end_sums(early, n_dp, grads, outs, *refs):
    sums = early_sums(early, n_dp, grads, outs, *refs)
    groups, steps = early["groups"], early["steps"]

    @pl.when(pl.program_id(0) == steps - 1)
    def _():
        for t in range(steps, len(groups) + 3):
            for stage, lag in ((sums.along, 2), (sums.across, 1), (sums.finish, 3)):
                if 0 <= t - lag < len(groups):
                    for p in groups[t - lag]:
                        stage(p)
        for p in range(len(early["pieces"])):
            sums.first(p).wait_send()
            sums.sent(p)


def back_kernel(nc, hb, heads, early, n_dp, place_ref, u_ref, xin_ref, gy_ref, y_ref, states_ref, adj_ref, start_ref, bc_ref, scores_ref,
                rows_ref, hpar_ref, taps8_ref, *refs):
    refs = list(refs)
    take = lambda count: [refs.pop(0) for _ in range(count)]
    arrays = 2 if early else 0
    grads = take(arrays)
    gx_ref, gxlast_ref, rim_ref, gtaps_ref, gdt_ref, gscores, gbct, hsum_ref = take(8)
    sums_out = take(arrays)
    adjoint, gnext, tapsum, hrow, taps_ref, ends_at = take(6)
    if early:
        sent_sums(early, n_dp, grads, sums_out, *refs)
    spread(taps8_ref, taps_ref)
    base, ends = scalars(place_ref, nc * Q)
    wide = iota((HEADDIM, Q), 1)
    block = pl.program_id(0)

    @pl.when(block == 0)
    def _():
        hsum_ref[...] = jnp.zeros_like(hsum_ref)
        gscores[...] = jnp.zeros_like(gscores)
        gbct[...] = jnp.zeros_like(gbct)
        hrow[...] = jnp.zeros_like(hrow)

    adjoint[...] = start_ref[...]
    gnext[...] = jnp.zeros_like(gnext)
    tapsum[...] = jnp.zeros_like(tapsum)

    def chunk(k, _):
        c = nc - 1 - k
        now = chunk_of(c)
        masks = back_masks(base, c, ends)
        from_later = nn(adjoint[...].astype(BF16), bc_ref[:STATE, now].astype(BF16))
        cum8 = rows_ref[0, CUM, :, now]
        cols = jnp.transpose(cum8)
        lifted, weighted = [], []
        for h in range(hb):
            at = slice(h * HEADDIM, (h + 1) * HEADDIM)
            hr = slice(h, h + 1)
            u = u_ref[at, now]
            gy = gy_ref[at, now]
            s = sigm(u)
            x = u * s
            step = rows_ref[0, STEP, hr, now]
            tail = rows_ref[0, TAIL, hr, now]
            moved = x * step
            moved_low = moved.astype(BF16)
            gy_low = gy.astype(BF16)
            decay = jnp.exp2(jnp.minimum(cols[:, hr] - cum8[hr, :], 0.0))
            gmix = tn(gy_low, moved_low)
            gscores[c] += gmix * decay
            gmoved = nn(gy_low, (decay * scores_ref[c]).astype(BF16))
            later = from_later[at, :] * tail
            lifted.append((gy * rows_ref[0, ENTRY, hr, now]).astype(BF16))
            weighted.append((moved * tail).astype(BF16))
            skip = hpar_ref[0, hr, 2:3]
            taken = gy_low.astype(F32) * (y_ref[at, now] - skip * x) - moved_low.astype(F32) * gmoved
            hrow[0, block, hr, now] = total_rows(taken)
            hrow[1, block, hr, now] = total_rows(moved * later)
            hrow[2, block, hr, now] = total_rows(adjoint[at, :] * states_ref[c, at, :]) * rows_ref[0, DEC, hr, now]
            gmoved = gmoved + later
            hrow[3, block, hr, now] = total_rows(x * gmoved)
            hrow[4, block, hr, now] = total_rows(x * gy)
            gx = gmoved * step + skip * gy
            gu = gx * (s * (1.0 + u * (1.0 - s)))
            gin, shifts = conv_back(gu, gnext[at, :], lambda k: taps_ref[k, at, :], masks, wide)
            gnext[at, :] = gu
            gx_ref[at, now] = gin.astype(BF16)

            ends_at[jnp.minimum(k, 1), at, :] = gin
            xin = xin_ref[at, chunk_of(c + 1)]
            for d in range(CONV):
                tapsum[d, at, :] += xin * shifts[d]
            tapsum[CONV, at, :] += gu
        gbct[STATE:, now] += tn(states_ref[c].astype(BF16), jnp.concatenate(lifted, 0))
        gbct[:STATE, now] += tn(adjoint[...].astype(BF16), jnp.concatenate(weighted, 0))
        for h in range(hb):
            at = slice(h * HEADDIM, (h + 1) * HEADDIM)
            adjoint[at, :] = adjoint[at, :] * rows_ref[0, DEC, h : h + 1, now] + adj_ref[c, at, :]
        return 0

    lax.fori_loop(0, nc, chunk, 0, unroll=2)

    gxlast_ref[...] = ends_at[0]
    masks = back_masks(base, 0, ends)
    for h in range(hb):
        at = slice(h * HEADDIM, (h + 1) * HEADDIM)
        rim, sums = conv_rim(gnext[at, :], lambda k: taps_ref[k, at, :], masks, wide, xin_ref[at, :Q])
        rim_ref[at, :] = rim.astype(BF16)
        for d in range(1, CONV):
            tapsum[d, at, :] += sums[d - 1]
    gtaps_ref[...] = jnp.concatenate([lane_sums(tapsum[d])[0:1] for d in range(CONV + 1)] + [jnp.zeros((7 - CONV, hb * HEADDIM), F32)], 0)

    row, col = iota((Q, Q), 0), iota((Q, Q), 1)
    glogs = (times_flags(stacked(hrow[0, block], nc), row >= col) + times_flags(stacked(hrow[1, block], nc), row < col)
             + times_flags(stacked(hrow[2, block], nc), row >= 0))
    rate = -jnp.exp(hpar_ref[0, :, 1:2])
    total = [jnp.zeros((8, Q), F32) for _ in range(3)]
    for c in range(nc):
        at = slice(c * Q, (c + 1) * Q)
        glog = glogs[c * 8 : (c + 1) * 8] * rate
        gdt = (hrow[3, block, :, at] + glog) * rows_ref[0, SIG, :, at]
        gdt_ref[0, :, at] = gdt
        total[0] = total[0] + gdt
        total[1] = total[1] + glog * rows_ref[0, STEP, :, at]
        total[2] = total[2] + hrow[4, block, :, at]
    sums = times_flags(jnp.concatenate(total, 0), row >= 0)
    first = lax.axis_index("col") * heads + block * hb
    lane = iota((1, Q), 1)
    for k in range(3):
        for h in range(hb):
            hsum_ref[k : k + 1, :] += jnp.where(lane == first + h, sums[k * 8 + h : k * 8 + h + 1, :], 0.0)

    if early:
        end_sums(early, n_dp, grads, sums_out, *refs)


def state_kernel(nc, place_ref, bc_ref, ubc_ref, bcin_ref, bctaps8_ref, gscores_in, gbct_in,
                 gbc_ref, gbclast_ref, bcrim_ref, gbctaps_ref, gnext, tapsum, bctaps_ref, ends_at):
    spread(bctaps8_ref, bctaps_ref)
    base, ends = scalars(place_ref, nc * Q)
    row, col = iota((Q, Q), 0), iota((Q, Q), 1)
    wide = iota((HEADDIM, Q), 1)
    gnext[...] = jnp.zeros_like(gnext)
    tapsum[...] = jnp.zeros_like(tapsum)
    tiles = [slice(k * HEADDIM, (k + 1) * HEADDIM) for k in range(2 * STATE // HEADDIM)]

    def body(k, _):
        c = nc - 1 - k
        now = chunk_of(c)
        start = base + c * Q
        same = (segment_of(start + row, ends) == segment_of(start + col, ends)) & (row >= col)
        gscore = jnp.where(same, gscores_in[c], 0.0)
        masks = back_masks(base, c, ends)
        inter = gbct_in[:, now]
        g_c = inter[STATE:] + nt3(bc_ref[:STATE, now], gscore)
        g_b = inter[:STATE] + nn3(bc_ref[STATE:, now], gscore)
        g_bc = jnp.concatenate([g_b, g_c], 0)
        for at in tiles:
            u = ubc_ref[at, now]
            s = sigm(u)
            gu = g_bc[at] * (s * (1.0 + u * (1.0 - s)))
            gin, shifts = conv_back(gu, gnext[at, :], lambda k: bctaps_ref[k, at, :], masks, wide)
            gnext[at, :] = gu
            gbc_ref[at, now] = gin.astype(BF16)

            ends_at[jnp.minimum(k, 1), at, :] = gin
            xin = bcin_ref[at, chunk_of(c + 1)]
            for d in range(CONV):
                tapsum[d, at, :] += xin * shifts[d]
            tapsum[CONV, at, :] += gu
        return 0

    lax.fori_loop(0, nc, body, 0)
    gbclast_ref[...] = ends_at[0]
    masks = back_masks(base, 0, ends)
    for at in tiles:
        rim, more = conv_rim(gnext[at, :], lambda k: bctaps_ref[k, at, :], masks, wide, bcin_ref[at, :Q])
        bcrim_ref[at, :] = rim.astype(BF16)
        for d in range(1, CONV):
            tapsum[d, at, :] += more[d - 1]
    for d in range(CONV + 1):
        gbctaps_ref[:, d * 2 * STATE : (d + 1) * 2 * STATE] = lane_sums(tapsum[d])


def whole(*shape):
    return pl.BlockSpec(shape, lambda n: (0,) * len(shape))


def params():
    return pltpu.CompilerParams(vmem_limit_bytes=VMEM_LIMIT)


SMEM = pl.BlockSpec(memory_space=pltpu.SMEM)


def shape(dtype, *dims):
    return jax.ShapeDtypeStruct(dims, dtype)


def after(value, *others):
    return lax.optimization_barrier((value,) + others)[0]


def moved(value, axis, steps):
    n = lax.axis_size(axis)
    return lax.ppermute(value, axis, [(k, (k + steps) % n) for k in range(n)])


def swapped(value, axis, bit):
    n = lax.axis_size(axis)
    return lax.ppermute(value, axis, [(k, k ^ bit) for k in range(n)])


def col_sum(value):
    if lax.axis_size("col") == 2:
        return value + swapped(value, "col", 1)
    return lax.psum(value, "col")


def from_before(value, steps):
    n = lax.axis_size("row")
    pairs = [(k, k + steps) for k in range(max(0, -steps), min(n, n - steps))]
    return lax.ppermute(value, "row", pairs)


def chained(state, keep, hb, direction):
    nb, inner = keep.shape[0], state.shape[0]
    flat = keep.reshape(nb * 8, Q)
    high, low = halves(flat)
    packed = jnp.concatenate([state, high, low], axis=0)
    total, decay = None, None
    for k in range(1, lax.axis_size("row")):
        part = from_before(packed, direction * k)
        passing = part[inner : inner + nb * 8].astype(F32) + part[inner + nb * 8 :].astype(F32)
        passing = jnp.repeat(passing.reshape(nb, 8, Q)[:, :hb].reshape(nb * hb, Q), HEADDIM, axis=0)
        part = part[:inner].astype(F32)
        total = part if total is None else total + decay * part
        decay = passing if decay is None else decay * passing
    return total


def sum_stages(n_row):
    order, bits = [0], []
    bit = n_row // 2
    while bit:
        order = [k + bit for k in order] + order
        bits.insert(0, bit)
        bit //= 2
    return order, bits


def far(source, target, sems, k, axis, place):
    return pltpu.make_async_remote_copy(
        src_ref=source, dst_ref=target, send_sem=sems.at[0, k], recv_sem=sems.at[1, k],
        device_id={axis: place}, device_id_type=MESH)


def meet(partners):
    barrier = pltpu.get_barrier_semaphore()
    for axis, place in partners:
        pl.semaphore_signal(barrier, inc=1, device_id={axis: place}, device_id_type=MESH)
    pl.semaphore_wait(barrier, len(partners))


class RowSums:
    def __init__(self, n_dp, pieces, sems):
        self.row, dp = lax.axis_index("row"), lax.axis_index("dp")
        self.n_dp, self.pieces, self.sems = n_dp, pieces, sems
        self.dps = [lax.rem(dp + k, n_dp) for k in range(n_dp)]
        self.quarter = pieces[0][3].shape[0]
        self.block = self.quarter // n_dp
        self.per = n_dp + 1

    def partners(self):
        return [("row", self.row ^ 1), ("row", self.row ^ 2)] + [("dp", d) for d in self.dps[1:]]

    def first(self, p):
        send, _, come1, _, _, _ = self.pieces[p]
        return far(send, come1, self.sems, p * self.per, "row", self.row ^ 1)

    def second(self, p):
        _, _, come1, come2, _, _ = self.pieces[p]
        return far(come1.at[pl.ds(0, self.quarter)], come2, self.sems, p * self.per + 1, "row", self.row ^ 2)

    def third(self, p):
        _, _, _, come2, come3, _ = self.pieces[p]
        block = self.block
        return [far(come2.at[pl.ds(k * block, block)], come3.at[pl.ds((k - 1) * block, block)], self.sems, p * self.per + 1 + k, "dp", self.dps[k])
                for k in range(self.n_dp - 1, 0, -1)]

    def pair(self, p):
        self.first(p).start()

    def across(self, p):
        _, kept, come1, _, _, _ = self.pieces[p]
        self.first(p).wait_recv()
        add_rows(come1, 0, kept, 0, self.quarter)
        self.second(p).start()
        add_rows(come1, self.quarter, kept, self.quarter, self.quarter)

    def along(self, p):
        _, _, come1, come2, _, _ = self.pieces[p]
        self.second(p).wait_recv()
        add_rows(come2, 0, come1, self.quarter, self.quarter)
        for copy in self.third(p):
            copy.start()

    def finish(self, p):
        _, _, _, come2, come3, out = self.pieces[p]
        for copy in self.third(p):
            copy.wait_recv()

        def body(i, _):
            at = i * 32
            total = come2[pl.ds(at, 32), :].astype(F32)
            for k in range(1, self.n_dp):
                total = total + come3[pl.ds((k - 1) * self.block + at, 32), :].astype(F32)
            out[pl.ds(at, 32), :] = total
            return 0

        lax.fori_loop(0, self.block // 32, body, 0, unroll=True)

    def sent(self, p):
        self.second(p).wait_send()
        for copy in self.third(p):
            copy.wait_send()


def add_rows(out, out_at, other, other_at, count):
    def body(i, _):
        at = i * 32
        out[pl.ds(out_at + at, 32), :] = (
            out[pl.ds(out_at + at, 32), :].astype(F32) + other[pl.ds(other_at + at, 32), :].astype(F32)).astype(out.dtype)
        return 0

    lax.fori_loop(0, count // 32, body, 0, unroll=4)


def close_kernel(n_row, n_dp, n_col, sources, pieces, has_gn, fused, *refs):
    refs = list(refs)
    take = lambda count: [refs.pop(0) for _ in range(count)]
    lefts = take(1 + max(left for left, _, _ in sources))
    if fused:
        nc, hb, n_late = fused
        lengths_ref, = take(1)
        rows_given = take(3)
    else:
        gbd, = take(1)
        rows_given = take(4)
    if has_gn:
        gain8, rstd8 = take(2)
    else:
        stat, gain_row = take(2)
    later_given = take(n_late if fused else 2 + len(sources) - 3 + (5 if has_gn else 0))
    outs = take(len(sources))
    state_out, small_out, stat_out = take(3)
    if has_gn:
        grad_in, = take(1)
    come1, come2, come3 = take(len(sources)), take(len(sources)), take(len(sources))
    grad_slots, = take(1)
    later_held = take(len(later_given))
    small_a, small_b, small_c, state_a, state_b = take(5)
    sems_grad, sems_small, sems_state, sems_other, sems_local, small = take(6)
    if has_gn:
        gn_sum, gn, gn_come, gain, gsum, stat = take(6)
    if fused:
        gbd, gbctaps, gbclast, rim_bc, rims, gnext, tapsum, bctaps, ends_at, sems_rim = take(10)
        rows_given = rows_given[:2] + [gbctaps] + rows_given[2:]

    loads = [pltpu.make_async_copy(source, held, sems_local.at[k]) for k, (source, held) in enumerate(zip(later_given, later_held))]
    for load in loads:
        load.start()
    loaded = set()

    def held(k):
        if k not in loaded:
            loads[k].wait()
            loaded.add(k)
        return later_held[k]

    row, dp, col = lax.axis_index("row"), lax.axis_index("dp"), lax.axis_index("col")
    dps = [lax.rem(dp + k, n_dp) for k in range(n_dp)]
    cols = [lax.rem(col + k, n_col) for k in range(n_col)]
    rows = lefts[0].shape[0]
    half, quarter = rows // 2, rows // 4
    block = quarter // n_dp
    count = len(pieces)
    slots = grad_slots.shape[0]
    views = []
    for p, (a, at, width) in enumerate(pieces):
        columns, mine = pl.ds(at, width), grad_slots.at[p % slots, :, pl.ds(0, width)]
        views.append((mine.at[pl.ds(0, half)], mine.at[pl.ds(half, half)], come1[a].at[:, columns], come2[a].at[:, columns],
                      come3[a].at[:, columns], outs[a].at[:, columns]))
    sums = RowSums(n_dp, views, sems_grad)
    ahead, behind = lax.rem(row + 1, n_row), lax.rem(row + n_row - 1, n_row)
    meet(sums.partners() + [("col", c) for c in cols[1:]] + ([("row", ahead), ("row", behind)] if fused else []))
    started = []

    def start(copy):
        copy.start()
        started.append(copy)
        return copy

    def make(p):
        a, at, width = pieces[p]
        left, first_row, right = sources[a]
        if p >= slots:
            sums.first(p - slots).wait_send()
        right = gbd if right is None else held(right)
        value = right[first_row + at : min(first_row + at + width, right.shape[0]), :]
        if value.shape[0] < width:
            value = jnp.concatenate([value, jnp.zeros((width - value.shape[0], value.shape[1]), BF16)], 0)
        for part in range(2):
            rows_here = slice(part * half, (part + 1) * half)
            grad_slots[p % slots, rows_here, :width] = nt(lefts[left][rows_here, :], value).astype(BF16)
            if part == 0:
                sums.pair(p)

    group = lambda r: pl.ds(pl.multiple_of(r * (n_dp * block), 16), n_dp * block)
    here = pl.ds(pl.multiple_of((row * n_dp + dp) * block, 16), block)
    n0 = n_col - 1
    n1 = n0 + n_dp - 1
    later = {"others": []}

    def send_rim():
        later["rim"] = start(far(held(7), rims.at[pl.ds(0, held(7).shape[0])], sems_rim, 0, "row", behind))

    def add_rim(target, last, at, count):
        tokens = target.shape[1]
        come = jnp.where(row < n_row - 1, rims[at : at + count, :].astype(F32), 0.0)
        target[:count, tokens - Q :] = (last[...] + come).astype(BF16)

    def take_rim():
        later["rim"].wait_recv()
        add_rim(held(0), held(8), 0, held(8).shape[0])

    def state_back():
        bc, ubc, bcin, bctaps8, gscores, gbct, gdt = (held(k) for k in range(9, 16))
        state_kernel(nc, lengths_ref, bc, ubc, bcin, bctaps8, gscores, gbct, gbd, gbclast, rim_bc, gbctaps, gnext, tapsum, bctaps, ends_at)
        channels = held(8).shape[0]
        later["rim_bc"] = start(far(rim_bc, rims.at[pl.ds(channels, 2 * STATE)], sems_rim, 1, "row", behind))
        steps = [gdt[n, :hb, :] for n in range(gdt.shape[0])]
        rest = gbd.shape[0] - 2 * STATE - hb * gdt.shape[0]
        gbd[2 * STATE :, :] = jnp.concatenate(steps + [jnp.zeros((rest, gdt.shape[2]), F32)], 0).astype(BF16)

    def take_rim_bc():
        later["rim_bc"].wait_recv()
        add_rim(gbd, gbclast, held(8).shape[0], 2 * STATE)

    def product(place, unit):
        gx, gz, x4, z4, bd4 = (held(k) for k in range(5))
        each = x4.shape[2]
        index = place * (n_row // 2) + unit
        gn_sum[unit * each : (unit + 1) * each, :] = tn(x4[index], gx[...]) + tn(z4[index], gz[...]) + tn(bd4[index], gbd[: bd4.shape[1], :])

    def prepare(k, place):
        hx = held(5)
        width = gn_sum.shape[0]
        rstd = rstd8[0:1, :]

        def body(i, total):
            at = pl.ds(i * 16, 16)
            there = pl.ds(pl.multiple_of(place * width + i * 16, 16), 16)
            pushed = gn_sum[at, :]
            if k == 0:
                gn[at, :] = pushed.astype(BF16)
            product = hx[there, Q:].astype(F32) * pushed
            scaled = product * rstd
            summed = scaled[:, :128]
            for tile in range(1, scaled.shape[1] // 128):
                summed = summed + scaled[:, tile * 128 : (tile + 1) * 128]
            gsum[at, :] = summed
            product = product * gain[0, there, 0:1]
            return total + product[:8] + product[8:]

        total = lax.fori_loop(0, width // 16, body, jnp.zeros((8, rstd.shape[1]), F32), unroll=2)
        total = rstd * total_rows(total)
        stat[...] = total if k == 0 else stat[...] + total
        small[6:7, pl.ds(pl.multiple_of(place * width, 128), width)] = lane_sums(gsum[...])[0:1]

    def begin_rows():
        channels = rows_given[0].shape[1]
        small[0 : CONV + 1, :channels] = rows_given[0][0 : CONV + 1, :]
        small[CONV + 1 : CONV + 2, :channels] = rows_given[1][0:1, :]
        small[7:8, : rows_given[2].shape[1]] = rows_given[2][0:1, :]
        for k in range(3):
            small[8:9, k * 128 : (k + 1) * 128] = rows_given[3][k : k + 1, :]

    def begin():
        small[...] = jnp.zeros_like(small)
        if has_gn:
            spread(gain8, gain)
        else:
            small[6:7, : gain_row.shape[1]] = gain_row[...]
        if not fused:
            begin_rows()

    def send_norm():
        if fused:
            begin()
        prepare(0, 1 - col)
        later["others"].append(start(far(gn, gn_come, sems_other, 0, "col", cols[1])))

    def send_small():
        if fused:
            begin_rows()
        if has_gn:
            prepare(1, col)
        later["small1"] = start(far(small, small_a.at[0], sems_small, 0, "row", row ^ 1))
        later["others"] += [start(far(stat, stat_out.at[col], sems_other, k, "col", cols[k])) for k in range(1, n_col)]
        stat_out[col] = stat[...]

    def small_pair():
        later["small1"].wait_recv()
        small_a[1] = small[...] + small_a[0]
        later["small2"] = start(far(small_a.at[1], small_b.at[0], sems_small, 1, "row", row ^ 2))

    def small_dp():
        later["small2"].wait_recv()
        small_b[1] = small_a[1] + small_b[0]
        later["small3"] = [start(far(small_b.at[1], small_c.at[k], sems_small, 1 + k, "dp", dps[k])) for k in range(1, n_dp)]

    def small_col():
        for copy in later["small3"]:
            copy.wait_recv()
        total = small_b[1]
        for k in range(1, n_dp):
            total = total + small_c[k]
        small_out[col] = total
        later["small4"] = [start(far(small_out.at[col], small_out.at[col], sems_small, n_dp + k, "col", cols[k])) for k in range(1, n_col)]

    def state_col():
        state_a[0] = outs[0][:, : state_a.shape[2]]
        later["state1"] = [start(far(state_a.at[0], state_a.at[k], sems_state, k - 1, "col", cols[k])) for k in range(1, n_col)]

    def state_dp():
        for copy in later["state1"]:
            copy.wait_recv()
        total = state_a[0]
        for k in range(1, n_col):
            total = total + state_a[k]
        state_b[...] = total.astype(state_b.dtype)
        state_out[here, :] = state_b[...]
        later["state2"] = [start(far(state_b, state_out.at[here], sems_state, n0 + k - 1, "dp", dps[k])) for k in range(1, n_dp)]

    def state_row():
        for copy in later["state2"]:
            copy.wait_recv()
        later["state3"] = start(far(state_out.at[group(row)], state_out.at[group(row)], sems_state, n1, "row", row ^ 2))

    def state_pair():
        later["state3"].wait_recv()
        later["state4"] = [start(far(state_out.at[group(r)], state_out.at[group(r)], sems_state, n1 + 1 + k, "row", row ^ 1))
                           for k, r in enumerate((row, row ^ 2))]

    def norm_back():
        for copy in later["others"]:
            copy.wait_recv()
        if not has_gn:
            return
        hx, grad_out = held(5), held(6)
        rstd = rstd8[0:1, :]
        total = stat_out[0]
        for k in range(1, n_col):
            total = total + stat_out[k]
        own = gn_sum.shape[0]
        width = n_col * own
        pull = (rstd * rstd) * (total / width)

        def body(i, _):
            at = pl.ds(i * 16, 16)
            there = pl.ds(pl.multiple_of(col * own + i * 16, 16), 16)
            pushed = gn_sum[at, :] + gn_come[at, :].astype(F32)
            grad_in[at, :] = (grad_out[at, :].astype(F32) + (rstd * gain[0, there, 0:1]) * pushed
                              - hx[there, Q:].astype(F32) * pull).astype(BF16)
            return 0

        lax.fori_loop(0, own // 16, body, 0, unroll=2)

    ahead_of = {}
    if fused:
        ahead_of = {4: [take_rim_bc], 6: [take_rim]}
        extra = {0: [send_rim], 1: [state_back], 7: [lambda: product(1 - col, 0)], 8: [lambda: product(1 - col, 1), send_norm],
                 9: [lambda: product(col, 0), state_col], 10: [lambda: product(col, 1), send_small], 11: [state_dp, small_pair],
                 12: [state_row, small_dp], 13: [state_pair, small_col], 15: [norm_back]}
    elif has_gn:
        extra = {1: [lambda: product(1 - col, 0)], 2: [lambda: product(1 - col, 1), send_norm], 4: [lambda: product(col, 0)],
                 6: [lambda: product(col, 1), send_small], 7: [state_col], 8: [small_pair], 9: [state_dp], 10: [small_dp], 11: [state_row],
                 12: [small_col], 13: [state_pair, norm_back]}
    else:
        extra = {1: [send_small], 3: [small_pair], 4: [small_dp], 5: [small_col], 7: [state_col], 8: [state_dp], 9: [state_row],
                 10: [state_pair], 11: [norm_back]}
    for step in extra.get(0, ()):
        step()
    make(0)
    if not fused:
        begin()
    for t in range(1, max(count + 6, 16)):
        if 0 <= t - 1 < count:
            sums.across(t - 1)
        for step in ahead_of.get(t, ()):
            step()
        if t < count:
            make(t)
        if 0 <= t - 3 < count:
            sums.along(t - 3)
        if 0 <= t - 5 < count:
            sums.finish(t - 5)
        for step in extra.get(t, ()):
            step()
    for copy in later["small4"] + later["state4"]:
        copy.wait_recv()
    for k in range(len(loads)):
        held(k)
    for copy in started:
        copy.wait_send()
    for p in range(count):
        if p + slots >= count:
            sums.first(p).wait_send()
        sums.sent(p)


def close(sources, pieces, lefts, gbd, given, gn, plain, later, fused=()):
    n_row, n_dp, n_col = (lax.axis_size(axis) for axis in ("row", "dp", "col"))
    assert n_row == 4
    rows, tokens = lefts[0].shape
    widths = [max(at + width for a, at, width in pieces if a == k) for k in range(len(sources))]
    half, quarter, block = rows // 2, rows // 4, rows // 4 // n_dp
    vmem, anywhere = pl.BlockSpec(memory_space=pltpu.VMEM), pl.BlockSpec(memory_space=pl.ANY)
    has_gn = gn is not None
    here = rows // n_col
    given = list(given)
    small = (16, max(rows, given[1 if fused else 0].shape[1]))
    channels = given[1].shape[1]
    extra = list(gn) if has_gn else list(plain)
    out = pl.pallas_call(
        functools.partial(close_kernel, n_row, n_dp, n_col, sources, pieces, has_gn, fused),
        in_specs=[vmem] * len(lefts) + ([SMEM] + [vmem] * 3 if fused else [vmem] * 5) + [vmem] * len(extra) + [anywhere] * len(later),
        out_specs=[vmem] * (len(sources) + 3 + has_gn),
        out_shape=[shape(F32, block, width) for width in widths]
        + [shape(BF16, rows, 2 * STATE), shape(F32, n_col, *small), shape(F32, n_col, 1, tokens)] + [shape(BF16, here, tokens)] * has_gn,
        scratch_shapes=[pltpu.VMEM((half, width), BF16) for width in widths] + [pltpu.VMEM((quarter, width), BF16) for width in widths]
        + [pltpu.VMEM(((n_dp - 1) * block, width), BF16) for width in widths]
        + [pltpu.VMEM((min(3 if fused else 4, len(pieces)), rows, max(width for _, _, width in pieces)), BF16)]
        + [pltpu.VMEM(value.shape, value.dtype) for value in later]
        + [pltpu.VMEM((2,) + small, F32), pltpu.VMEM((2,) + small, F32), pltpu.VMEM((n_dp,) + small, F32),
           pltpu.VMEM((n_col, block, 2 * STATE), F32), pltpu.VMEM((block, 2 * STATE), BF16),
           pltpu.SemaphoreType.DMA((2, len(pieces) * (n_dp + 1))), pltpu.SemaphoreType.DMA((2, n_dp + n_col)),
           pltpu.SemaphoreType.DMA((2, n_col + n_dp + 2)), pltpu.SemaphoreType.DMA((2, n_col)),
           pltpu.SemaphoreType.DMA((len(later),)), pltpu.VMEM(small, F32)]
        + ([pltpu.VMEM((here, tokens), F32), pltpu.VMEM((here, tokens), BF16), pltpu.VMEM((here, tokens), BF16), pltpu.VMEM((1, rows, 128), F32),
            pltpu.VMEM((here, 128), F32), pltpu.VMEM((1, tokens), F32)] if has_gn else [])
        + ([pltpu.VMEM((widths[0], tokens), BF16), pltpu.VMEM((8, (CONV + 1) * 2 * STATE), F32), pltpu.VMEM((2 * STATE, Q), F32),
            pltpu.VMEM((2 * STATE, Q), BF16), pltpu.VMEM((channels + 2 * STATE, Q), BF16), pltpu.VMEM((2 * STATE, Q), F32),
            pltpu.VMEM((CONV + 1, 2 * STATE, Q), F32), pltpu.VMEM((CONV + 1, 2 * STATE, Q), F32), pltpu.VMEM((2, 2 * STATE, Q), F32),
            pltpu.SemaphoreType.DMA((2, 2))] if fused else []),
        compiler_params=pltpu.CompilerParams(vmem_limit_bytes=60 * 1024 * 1024, collective_id=1, has_side_effects=True),
        cost_estimate=pl.CostEstimate(flops=10**6, bytes_accessed=10**8, transcendentals=0),
        name="close",
    )(*lefts, *([] if fused else [gbd]), *given, *extra, *later)
    count = len(sources)
    return out[:count], out[count], out[count + 1], out[count + 2], out[count + 3] if has_gn else None


def last_kernel(n_row, n_dp, n_col, heads, n_z, bd, x, state, small, *refs):
    refs = list(refs)
    take = lambda count: [refs.pop(0) for _ in range(count)]
    z_parts = take(n_z)
    norm_gain, inner, state_out, step, taps, bias, bc_taps, bc_bias, step_bias, decay, skip, gate = refs
    block = x.shape[0]
    at, channels = 0, inner.shape[2]
    for part in z_parts:
        count = min(part.shape[1], channels - at)
        inner[0, :, at : at + count] = part[:, :count]
        at += count
    inner[1] = x[:, :channels]
    for r in range(n_row):
        for d in range(n_dp):
            state_out[(d * n_row + r) * block : (d * n_row + r + 1) * block, :] = state[
                (r * n_dp + d) * block : (r * n_dp + d + 1) * block, :].astype(F32)
    step[...] = jnp.transpose(bd[:, 2 * STATE :])[:heads]
    by_col = lambda k: jnp.concatenate([small[c, k : k + 1, :channels] for c in range(n_col)], 1)
    for k in range(CONV):
        taps[k : k + 1, :] = by_col(CONV - 1 - k)
    bias[...] = by_col(CONV)
    gate[...] = by_col(CONV + 1)
    over = lambda k, at, count: sum(small[c, k : k + 1, at : at + count] for c in range(n_col))
    norm_gain[...] = over(6, 0, norm_gain.shape[1])
    for k in range(CONV):
        bc_taps[k : k + 1, :] = over(7, (CONV - 1 - k) * 2 * STATE, 2 * STATE)
    bc_bias[...] = over(7, CONV * 2 * STATE, 2 * STATE)
    for k, target in enumerate((step_bias, decay, skip)):
        target[...] = over(8, k * 128, 128)[:, : target.shape[1]]


def last(bd, x, state, small, z_parts, heads, channels):
    n_row, n_dp, n_col = (lax.axis_size(axis) for axis in ("row", "dp", "col"))
    block = x.shape[0]
    width = state.shape[0]
    row = lambda count: shape(F32, 1, count)
    return pl.pallas_call(
        functools.partial(last_kernel, n_row, n_dp, n_col, heads, len(z_parts)),
        out_shape=[row(width), shape(F32, 2, block, channels), shape(F32, width, 2 * STATE), shape(F32, heads, block),
                   shape(F32, CONV, n_col * channels), row(n_col * channels), shape(F32, CONV, 2 * STATE), row(2 * STATE),
                   row(n_col * heads), row(n_col * heads), row(n_col * heads), row(n_col * channels)],
        compiler_params=params(),
        cost_estimate=pl.CostEstimate(flops=10**6, bytes_accessed=10**7, transcendentals=0),
        name="last",
    )(bd, x, state, small, *z_parts)


def open_kernel(n_row, n_col, parts, hidden, inner, state_w, step_w, hx, x4, z_w, bd4, sems):
    row, col = lax.axis_index("row"), lax.axis_index("col")
    cols = [lax.rem(col + k, n_col) for k in range(n_col)]
    ahead, behind = lax.rem(row + 1, n_row), lax.rem(row + n_row - 1, n_row)
    partners = [("row", row ^ 1), ("row", row ^ 2), ("row", ahead), ("row", behind)] + [("col", c) for c in cols[1:]]
    meet(partners)
    width, tokens = hidden.shape
    each = inner.shape[0] // parts
    heads = step_w.shape[0]
    mine = pl.ds(pl.multiple_of(col * width, 16), width)
    counter = [0]
    started = []

    def start(source, target, axis, place):
        copy = far(source, target, sems, counter[0], axis, place)
        counter[0] += 1
        copy.start()
        started.append(copy)
        return copy

    rim = start(hidden.at[:, pl.ds(tokens - Q, Q)], hx.at[mine, pl.ds(0, Q)], "row", ahead)
    wide = [start(hidden, hx.at[mine, pl.ds(Q, tokens)], "col", cols[k]) for k in range(1, n_col)]
    part = lambda p: pl.ds(p * each, each)
    send = lambda p: start(x4.at[row, part(p)], x4.at[row, part(p)], "row", row ^ 2)

    def split(p):
        def body(i, _):
            at = pl.ds(p * each + i * 16, 16)
            x4[row, at, :] = inner[at, 1, :]
            z_w[at, :] = inner[at, 0, :]
            return 0

        lax.fori_loop(0, each // 16, body, 0, unroll=2)

    split(0)
    over = [send(0)]
    bd4[row, : 2 * STATE, :] = jnp.transpose(state_w[...].astype(F32)).astype(BF16)
    rest = bd4.shape[1] - 2 * STATE - heads
    bd4[row, 2 * STATE :, :] = jnp.concatenate([step_w[...], jnp.zeros((rest, step_w.shape[1]), BF16)], 0)
    bd_over = start(bd4.at[row], bd4.at[row], "row", row ^ 2)
    near = [start(bd4.at[row], bd4.at[row], "row", row ^ 1)]
    for p in range(1, parts):
        split(p)
        if p == 1:
            over.append(send(1))
    near.append(start(x4.at[row], x4.at[row], "row", row ^ 1))

    def keep_hidden(i, _):
        hx[pl.ds(pl.multiple_of(col * width + i * 16, 16), 16), pl.ds(Q, tokens)] = hidden[pl.ds(i * 16, 16), :]
        return 0

    lax.fori_loop(0, width // 16, keep_hidden, 0)
    rim.wait_recv()
    wide += [start(hx.at[mine, pl.ds(0, Q)], hx.at[mine, pl.ds(0, Q)], "col", cols[k]) for k in range(1, n_col)]
    bd_over.wait_recv()
    near.append(start(bd4.at[row ^ 2], bd4.at[row ^ 2], "row", row ^ 1))
    waited = []
    for p in range(parts):
        over[p].wait_recv()
        near.append(start(x4.at[row ^ 2, part(p)], x4.at[row ^ 2, part(p)], "row", row ^ 1))
        if p + 2 < parts:
            over[p].wait_send()
            waited.append(id(over[p]))
            over.append(send(p + 2))
    for copy in wide + near:
        copy.wait_recv()
    for copy in started:
        if id(copy) not in waited:
            copy.wait_send()


def open_up(hidden, inner, state_w, step_w):
    n_row, n_col = lax.axis_size("row"), lax.axis_size("col")
    assert n_row == 4
    channels, _, block = inner.shape
    heads = step_w.shape[0]
    parts = 4 if channels % 64 == 0 else 1
    vmem = pl.BlockSpec(memory_space=pltpu.VMEM)
    return pl.pallas_call(
        functools.partial(open_kernel, n_row, n_col, parts),
        in_specs=[vmem] * 4,
        out_specs=[vmem] * 4,
        out_shape=[shape(BF16, hidden.shape[0] * n_col, Q + hidden.shape[1]), shape(BF16, n_row, channels, block), shape(BF16, channels, block),
                   shape(BF16, n_row, 2 * STATE + heads + -heads % 32, block)],
        scratch_shapes=[pltpu.SemaphoreType.DMA((2, 5 + 2 * parts + 2 * (n_col - 1)))],
        compiler_params=pltpu.CompilerParams(vmem_limit_bytes=VMEM_LIMIT, collective_id=2, has_side_effects=True),
        cost_estimate=pl.CostEstimate(flops=0, bytes_accessed=10**8, transcendentals=0),
        name="open",
    )(hidden, inner, state_w, step_w)


def joined(w4_ref):
    return jnp.concatenate([w4_ref[j] for j in range(w4_ref.shape[0])], 1)


def by_distance(n_row, n_dp):
    row, dp = lax.axis_index("row"), lax.axis_index("dp")
    return [lax.rem(dp + k, n_dp) * n_row + (row ^ place) for place in sum_stages(n_row)[0] for k in range(n_dp)]


def put_by_distance(n_row, n_dp, source, target, skip):
    each = target.shape[0] // (n_row * n_dp)
    for k, place in enumerate(by_distance(n_row, n_dp)):
        target[k * each : (k + 1) * each, :] = source[pl.ds(pl.multiple_of(place * each, 32), each), skip:]


def project_kernel(n_row, n_dp, hb, lengths_ref, hx_ref, gain8_ref, x4_ref, bd4_ref, normed_ref, by_ref, rstd_ref, live_ref, xin_ref, bd_ref, dt_ref, gain_ref):
    @pl.when(pl.program_id(0) == 0)
    def _():
        spread(gain8_ref, gain_ref)
        width, count = hx_ref.shape

        def square(i, total):
            v = hx_ref[pl.ds(i * 16, 16), :].astype(F32)
            v = v * v
            return total + v[:8] + v[8:]

        total = lax.fori_loop(0, width // 16, square, jnp.zeros((8, count), F32), unroll=4)
        rstd = lax.rsqrt(jnp.sum(total, 0, keepdims=True) / width + EPS)
        rstd_ref[...] = jnp.broadcast_to(rstd[:, Q:], rstd_ref.shape)
        base, ends = scalars(lengths_ref, count - Q)
        live_ref[...] = (base + iota(live_ref.shape, 1) < ends[-1]).astype(F32)

        def norm(i, _):
            at = pl.ds(i * 16, 16)
            normed_ref[at, :] = (hx_ref[at, :].astype(F32) * rstd * gain_ref[0, at, 0:1]).astype(BF16)
            return 0

        lax.fori_loop(0, width // 16, norm, 0, unroll=4)
        put_by_distance(n_row, n_dp, normed_ref, by_ref, Q)
        bd = nn(joined(bd4_ref), normed_ref[...])
        bd_ref[...] = bd[: 2 * STATE]
        dt_ref[...] = jnp.zeros_like(dt_ref)
        for n in range(dt_ref.shape[0]):
            dt_ref[n, :hb, :] = bd[2 * STATE + n * hb : 2 * STATE + (n + 1) * hb, Q:]

    xin_ref[...] = nn(joined(x4_ref), normed_ref[...])


def second_kernel(n_row, n_dp, steps, hb, given, *refs):
    refs = list(refs)
    take = lambda count: [refs.pop(0) for _ in range(count)]
    far_refs = [take(2), take(2)]
    near_refs = [take(2), take(2)]
    normed, = take(1)
    grads = take(2 if given else 1)
    live, final, keep = take(3)
    z4, z, out4, gg, state_in, grad_by = take(6)
    whole_grad, come, came, kept, sems, sems_state = take(6)
    row, col = lax.axis_index("row"), lax.axis_index("col")
    n = pl.program_id(0)
    each = z4.shape[1]

    def piece(side, which, s):
        rows = pl.ds(s * each, each)
        return far(far_refs[side][which].at[rows], come.at[side, which, rows], sems, (side * 2 + which) * steps + s, "row", row ^ 1)

    def pieces(at):
        return [piece(at // steps, which, at % steps) for which in range(2)]

    def states():
        copies = []
        for k in range(1, n_row):
            there = lax.rem(row + k, n_row)
            copies.append(far(final, came.at[k - 1], sems_state, 2 * k - 2, "row", there))
            copies.append(far(keep, kept.at[k - 1], sems_state, 2 * k - 1, "row", there))
        return copies

    @pl.when(n == 0)
    def _():
        meet([("row", lax.rem(row + k, n_row)) for k in range(1, n_row)])
        for copy in states() + pieces(0) + pieces(1):
            copy.start()

    @pl.when(n == 0)
    def _():
        width = grads[0].shape[0]
        for place, source in zip((col, 1 - col) if given else (0,), grads):
            def body(i, _):
                at = pl.ds(pl.multiple_of(place * width + i * 16, 16), 16)
                whole_grad[at, :] = (source[pl.ds(i * 16, 16), :].astype(F32) * live[0:1, :]).astype(BF16)
                return 0

            lax.fori_loop(0, width // 16, body, 0, unroll=4)
        put_by_distance(n_row, n_dp, whole_grad, grad_by, 0)

    for at in range(2 * steps):
        @pl.when(n == at)
        def _():
            side = at // steps
            if at + 2 < 2 * steps:
                for copy in pieces(at + 2):
                    copy.start()
            for copy in pieces(at):
                copy.wait_recv()
            rows = slice(at % steps * each, (at % steps + 1) * each)
            w4, out = ((z4, z), (out4, gg))[side]
            w4[row] = near_refs[side][0][...]
            w4[row ^ 2] = near_refs[side][1][...]
            w4[row ^ 1] = come[side, 0, rows, :]
            w4[row ^ 3] = come[side, 1, rows, :]
            value = normed[:, Q:] if side == 0 else whole_grad[...]
            out[...] = nn(joined(w4), value)

    @pl.when(n == 2 * steps - 1)
    def _():
        for copy in states():
            copy.wait_recv()
        for head in range(final.shape[0] // HEADDIM):
            at = slice(head * HEADDIM, (head + 1) * HEADDIM)
            total, decay = None, None
            for k in range(1, n_row):
                part = jnp.where(row >= k, came[k - 1, at, :].astype(F32), 0.0)
                total = part if total is None else total + decay * part
                passing = kept[k - 1, head // hb, head % hb : head % hb + 1, :]
                decay = passing if decay is None else decay * passing
            state_in[at, :] = total
        for copy in states():
            copy.wait_send()
        for at in range(2 * steps):
            for copy in pieces(at):
                copy.wait_send()


def placed(value, index, count):
    out = jnp.zeros((count,) + value.shape, F32)
    return lax.dynamic_update_slice(out, value[None], (index,) + (0,) * value.ndim)


def turned(value, axis):
    return lax.all_gather(value, axis, axis=0, tiled=True)


def per_device(hidden_in, grad_out, lengths, norm_gain, inner_proj, state_proj, step_proj, conv_inner, conv_inner_bias,
               conv_state, conv_state_bias, step_bias, decay_log, skip_gain, gate_gain, out_proj):
    cols_here, rows = hidden_in.shape
    ncols = lax.axis_size("col")
    nrow = lax.axis_size("row")
    width = cols_here * ncols
    inner = inner_proj.shape[0]
    heads = step_proj.shape[0]
    col_index = lax.axis_index("col")
    nc = rows // Q
    hb = max(k for k in (1, 2, 3, 4) if heads % k == 0)
    nb = heads // hb
    bh = hb * HEADDIM


    gain_full = norm_gain.astype(F32)
    gain8 = jnp.broadcast_to(gain_full[None], (8, width))
    hx, x4, z_w, bd4 = open_up(hidden_in, inner_proj, state_proj, step_proj)
    out_w, grad_now, hx = lax.optimization_barrier((out_proj, grad_out, hx))
    z_far = swapped(z_w, "row", 2)
    z_far, out_w = lax.optimization_barrier((z_far, out_w))
    out_far = swapped(out_w, "row", 2)
    if ncols == 2:
        grads = [grad_now, swapped(grad_now, "col", 1)]
    else:
        grads = [lax.all_gather(grad_now, "col", axis=0, tiled=True)]

    bm = 2 * bh if nb % 2 == 0 else bh
    part4 = pl.BlockSpec((nrow, bm, width // nrow), lambda n: (0, n, 0))
    ext = rows + Q
    normed_ext, normed_by, rstd8, live8, xin, bdin, dt = pl.pallas_call(
        functools.partial(project_kernel, nrow, lax.axis_size("dp"), hb),
        grid=(inner // bm,),
        in_specs=[SMEM, whole(width, ext), whole(8, width), part4, whole(*bd4.shape)],
        out_specs=[whole(width, ext), whole(width, rows), whole(8, rows), whole(8, rows), pl.BlockSpec((bm, ext), lambda n: (n, 0)), whole(2 * STATE, ext), whole(nb, 8, rows)],
        out_shape=[shape(BF16, width, ext), shape(BF16, width, rows), shape(F32, 8, rows), shape(F32, 8, rows), shape(F32, inner, ext), shape(F32, 2 * STATE, ext), shape(F32, nb, 8, rows)],
        compiler_params=params(),
        scratch_shapes=[pltpu.VMEM((1, width, Q), F32)],
        cost_estimate=pl.CostEstimate(flops=8 * 10**9, bytes_accessed=20 * 10**6, transcendentals=0),
        name="project",
    )(lengths, hx, gain8, x4, bd4)
    rstd_in = rstd8[:1]
    by_head = jnp.pad(jnp.stack([step_bias, decay_log, skip_gain]), ((0, 5), (0, 128 - heads)))

    def taps_of(taps, bias):
        return jnp.pad(jnp.concatenate([taps, bias[None]], axis=0).astype(F32), ((0, 7 - CONV), (0, 0)))

    taps = taps_of(conv_inner, conv_inner_bias)
    bctaps = taps_of(conv_state, conv_state_bias)
    gate = jnp.broadcast_to(gate_gain.astype(F32)[None], (8, inner))

    tok = pl.BlockSpec((bh, rows), lambda n: (n, 0))
    tok_ext = pl.BlockSpec((bh, rows + Q), lambda n: (n, 0))
    eight = pl.BlockSpec((8, bh), lambda n: (0, n))
    bc_ext = pl.BlockSpec((2 * STATE, rows + Q), lambda n: (0, 0))
    state_spec = pl.BlockSpec((bh, STATE), lambda n: (n, 0))
    chunks = pl.BlockSpec((nc, bh, STATE), lambda n: (0, n, 0))
    rows_spec = pl.BlockSpec((1, 6, 8, rows), lambda n: (n, 0, 0, 0))
    head_tok = pl.BlockSpec((1, 8, rows), lambda n: (n, 0, 0))
    head_q = pl.BlockSpec((1, 8, Q), lambda n: (n, 0, 0))
    head8 = pl.BlockSpec((1, 8, 8), lambda n: (n, 0, 0))

    u, ubc, bc, rowpack, scores, y_in, fresh, final, keep, hpar = pl.pallas_call(
        functools.partial(enter_kernel, nc, hb),
        grid=(nb,),
        in_specs=[SMEM, tok_ext, bc_ext, whole(nb, 8, rows), whole(8, 128), eight, whole(8, 2 * STATE),
                  pl.BlockSpec(memory_space=pl.ANY)],
        out_specs=[tok, whole(2 * STATE, rows), whole(2 * STATE, rows), whole(nb, 6, 8, rows), whole(nc, Q, Q), tok, chunks,
                   state_spec, whole(nb, 8, Q), whole(nb, 8, 8)],
        out_shape=[shape(F32, inner, rows), shape(F32, 2 * STATE, rows), shape(F32, 2 * STATE, rows),
                   shape(F32, nb, 6, 8, rows), shape(F32, nc, Q, Q), shape(F32, inner, rows), shape(F32, nc, inner, STATE),
                   shape(BF16, inner, STATE), shape(F32, nb, 8, Q), shape(F32, nb, 8, 8)],
        scratch_shapes=[pltpu.VMEM((bh, STATE), F32), pltpu.VMEM((CONV + 1, bh, Q), F32), pltpu.VMEM((CONV + 1, 2 * STATE, Q), F32)],
        compiler_params=params(),
        cost_estimate=pl.CostEstimate(flops=3 * 10**10, bytes_accessed=40 * 10**6, transcendentals=0),
        name="enter",
    )(lengths, xin, bdin, dt, by_head, taps, bctaps, z_far)

    steps = inner // bm
    block = pl.BlockSpec((bm, width // nrow), lambda n: (jnp.minimum(n, steps - 1), 0))
    block_after = pl.BlockSpec((bm, width // nrow), lambda n: (jnp.maximum(n - steps, 0), 0))
    anywhere = pl.BlockSpec(memory_space=pl.ANY)
    second = pl.pallas_call(
        functools.partial(second_kernel, nrow, lax.axis_size("dp"), steps, hb, ncols == 2),
        grid=(2 * steps,),
        in_specs=[anywhere] * 4 + [block] * 2 + [block_after] * 2 + [whole(width, ext)] + [whole(*value.shape) for value in grads]
        + [whole(8, rows), whole(inner, STATE), whole(nb, 8, Q)],
        out_specs=[pl.BlockSpec((nrow, bm, width // nrow), lambda n: (0, jnp.minimum(n, steps - 1), 0)),
                   pl.BlockSpec((bm, rows), lambda n: (jnp.minimum(n, steps - 1), 0)),
                   pl.BlockSpec((nrow, bm, width // nrow), lambda n: (0, jnp.maximum(n - steps, 0), 0)),
                   pl.BlockSpec((bm, rows), lambda n: (jnp.maximum(n - steps, 0), 0)),
                   whole(inner, STATE), whole(width, rows)],
        out_shape=[shape(BF16, nrow, inner, width // nrow), shape(F32, inner, rows)] * 2 + [shape(F32, inner, STATE), shape(BF16, width, rows)],
        scratch_shapes=[pltpu.VMEM((width, rows), BF16), pltpu.VMEM((2, 2, inner, width // nrow), BF16), pltpu.VMEM((nrow - 1, inner, STATE), BF16),
                        pltpu.VMEM((nrow - 1, nb, 8, Q), F32), pltpu.SemaphoreType.DMA((2, 4 * steps)),
                        pltpu.SemaphoreType.DMA((2, 2 * (nrow - 1)))],
        compiler_params=pltpu.CompilerParams(vmem_limit_bytes=VMEM_LIMIT, collective_id=3, has_side_effects=True),
        cost_estimate=pl.CostEstimate(flops=10**10, bytes_accessed=30 * 10**6, transcendentals=0),
        name="second",
    )(z_w, z_far, out_w, out_far, z_w, z_far, out_w, out_far, normed_ext, *grads, live8, final, keep)
    z4, z, out4, grad_gated, state_in, grad_by = second

    y, states, stats = pl.pallas_call(
        functools.partial(across_kernel, nc, hb),
        grid=(nb,),
        in_specs=[tok, chunks, state_spec, whole(2 * STATE, rows), rows_spec, tok, tok, eight],
        out_specs=[tok, chunks, whole(2, 8, rows)],
        out_shape=[shape(F32, inner, rows), shape(F32, nc, inner, STATE), shape(F32, 2, 8, rows)],
        scratch_shapes=[pltpu.VMEM((bh, STATE), F32), pltpu.VMEM((1, bh, Q), F32)],
        compiler_params=params(),
        cost_estimate=pl.CostEstimate(flops=10**10, bytes_accessed=35 * 10**6, transcendentals=0),
        name="across",
    )(y_in, fresh, state_in, bc, rowpack, z, grad_gated, gate)

    sums = col_sum(jnp.sum(stats, axis=1))
    inner_width = inner * ncols
    rstd_gate = lax.rsqrt(sums[0] / inner_width + EPS)
    pull = rstd_gate * rstd_gate * rstd_gate * (sums[1] / inner_width)
    token_rows = jnp.concatenate([rstd_gate[None], pull[None], jnp.zeros((6, rows), F32)], axis=0)

    gated, grad_z, grad_y, adj, adj_first, ggate = pl.pallas_call(
        functools.partial(gate_kernel, nc, hb),
        grid=(nb,),
        in_specs=[tok, tok, tok, whole(8, rows), eight, whole(2 * STATE, rows), rows_spec],
        out_specs=[tok, tok, tok, chunks, state_spec, eight],
        out_shape=[shape(BF16, inner, rows), shape(BF16, inner, rows), shape(F32, inner, rows),
                   shape(F32, nc, inner, STATE), shape(BF16, inner, STATE), shape(F32, 8, inner)],
        scratch_shapes=[pltpu.VMEM((bh, STATE), F32), pltpu.VMEM((bh, Q), F32), pltpu.VMEM((1, bh, Q), F32)],
        compiler_params=params(),
        cost_estimate=pl.CostEstimate(flops=10**10, bytes_accessed=40 * 10**6, transcendentals=0),
        name="gate",
    )(y, z, grad_gated, token_rows, gate, bc, rowpack)

    adj_in = chained(adj_first, keep, hb, -1)
    def turned_product(w4, value):
        return lax.dot_general(w4, value, (((1,), (0,)), ((), ())), preferred_element_type=F32).reshape(-1, rows)

    def halves_of_features(products):
        return [sum(turned_product(lax.dynamic_slice_in_dim(w4, at * (nrow // 2), nrow // 2, 0), value) for w4, value in products)
                for at in (1 - col_index, col_index)]

    if ncols == 2:
        mixed_other, mixed = halves_of_features([(out4, gated)])
        mixed_come = swapped(mixed_other.astype(BF16), "col", 1)

    n_dp = lax.axis_size("dp")
    early, grads_early, first_z = {}, [], 0
    if nb >= 5 and inner % 768 == 0:
        first_z = inner // 3
        grads_early = [nt(grad_by, gated).astype(BF16), nt(normed_by, grad_z[:first_z]).astype(BF16)]
        each = inner // 6
        places = [(0, k * each, each) for k in range(6)] + [(1, k * each, each) for k in range(2)]
        early = {"pieces": places, "groups": [(2 * k, 2 * k + 1) for k in range(4)], "steps": nb}
    quarter = width // 4
    once = pl.Buffered(1)
    held = pl.BlockSpec(memory_space=pltpu.VMEM)
    back_out = pl.pallas_call(
        functools.partial(back_kernel, nc, hb, heads, early, n_dp),
        grid=(nb,),
        in_specs=[SMEM, tok, tok_ext, tok, tok, chunks, chunks, state_spec, whole(2 * STATE, rows), whole(nc, Q, Q), rows_spec, head8, eight]
        + [pl.BlockSpec(value.shape, lambda n: (0, 0), pipeline_mode=once) for value in grads_early],
        out_specs=[tok, pl.BlockSpec((bh, Q), lambda n: (n, 0)), pl.BlockSpec((bh, Q), lambda n: (n, 0)), eight, head_tok,
                   whole(nc, Q, Q), whole(2 * STATE, rows), whole(8, Q)] + [whole(quarter // n_dp, value.shape[1]) for value in grads_early],
        out_shape=[shape(BF16, inner, rows), shape(F32, inner, Q), shape(BF16, inner, Q), shape(F32, 8, inner), shape(F32, nb, 8, rows),
                   shape(F32, nc, Q, Q), shape(F32, 2 * STATE, rows), shape(F32, 8, Q)]
        + [shape(F32, quarter // n_dp, value.shape[1]) for value in grads_early],
        scratch_shapes=[pltpu.VMEM((bh, STATE), F32), pltpu.VMEM((bh, Q), F32), pltpu.VMEM((CONV + 1, bh, Q), F32),
                        pltpu.VMEM((5, nb, 8, rows), F32), pltpu.VMEM((CONV + 1, bh, Q), F32), pltpu.VMEM((2, bh, Q), F32)]
        + ([pltpu.VMEM((8, 2 * quarter, each), BF16), pltpu.VMEM((8, quarter, each), BF16),
            pltpu.VMEM((8, quarter // n_dp * (n_dp - 1), each), BF16), pltpu.SemaphoreType.DMA((2, 8 * (n_dp + 1)))] if early else []),
        compiler_params=pltpu.CompilerParams(vmem_limit_bytes=VMEM_LIMIT, collective_id=4, has_side_effects=True) if early else params(),
        cost_estimate=pl.CostEstimate(flops=6 * 10**10, bytes_accessed=50 * 10**6, transcendentals=0),
        name="back",
    )(lengths, u, xin, grad_y, y, states, adj, adj_in, bc, scores, rowpack, hpar, taps, *grads_early)
    gx, gx_last, rim_x, gtaps, gdt, gscores, gbct, hsum = back_out[:8]
    if ncols == 2:
        mixed_come, gx = lax.optimization_barrier((mixed_come, gx))

    if ncols == 2:
        mixed = mixed + mixed_come.astype(F32)
    else:
        mixed = lax.psum_scatter(turned_product(out4, gated).astype(BF16), "col", scatter_dimension=0, tiled=True).astype(F32)
    hidden_f = hidden_in.astype(F32)
    block_out = (hidden_f + live8[:1] * mixed).astype(BF16)

    small_width = -(-(2 * STATE + heads) // 128) * 128
    fused = ncols == 2 and bool(early)
    each = inner // 6 if inner % 768 == 0 else inner + -inner % 128
    sources = [(0, 0, None), (0, 0, 0), (0, first_z, 1)]
    pieces = [(0, 0, 2 * STATE), (0, 2 * STATE, small_width - 2 * STATE)]
    z_pieces = [(2, at, each) for at in range(0, inner - first_z, each)]
    x_pieces = [(1, at, each) for at in range(0, inner, each)]
    pieces = z_pieces + pieces + x_pieces if fused else pieces + z_pieces + x_pieces
    gbd = None
    if not fused:
        vmem = pl.BlockSpec(memory_space=pltpu.VMEM)
        gbc, gbc_last, rim_bc, gbctaps = pl.pallas_call(
            functools.partial(state_kernel, nc),
            grid=(1,),
            out_shape=[shape(BF16, 2 * STATE, rows), shape(F32, 2 * STATE, Q), shape(BF16, 2 * STATE, Q),
                       shape(F32, 8, (CONV + 1) * 2 * STATE)],
            in_specs=[SMEM, vmem, vmem, bc_ext, vmem, vmem, vmem],
            out_specs=[vmem] * 4,
            scratch_shapes=[pltpu.VMEM((2 * STATE, Q), F32), pltpu.VMEM((CONV + 1, 2 * STATE, Q), F32),
                            pltpu.VMEM((CONV + 1, 2 * STATE, Q), F32), pltpu.VMEM((2, 2 * STATE, Q), F32)],
            compiler_params=params(),
            cost_estimate=pl.CostEstimate(flops=10**9, bytes_accessed=6 * 10**6, transcendentals=0),
            name="state",
        )(lengths, bc, ubc, bdin, bctaps, gscores, gbct)

        def last_tokens(value, last, rim):
            return lax.dynamic_update_slice(value, (last + rim.astype(F32)).astype(BF16), (0, rows - Q))

        back_x, back_bc = from_before(rim_x, -1), from_before(rim_bc, -1)
        gx = last_tokens(gx, gx_last, back_x)
        gbd = jnp.concatenate([last_tokens(gbc, gbc_last, back_bc), gdt[:, :hb].reshape(heads, rows).astype(BF16),
                               jnp.zeros((bd4.shape[1] - 2 * STATE - heads, rows), BF16)], axis=0)

        gbd_padded = jnp.pad(gbd, ((0, small_width - gbd.shape[0]), (0, 0)))
    lefts, later = [normed_by], [gx, grad_z]
    if ncols == 2:
        later += [x4, z4, bd4, hx, grad_out]
        gn_given, plain = (gain8, rstd8), None
        if fused:
            later += [rim_x, gx_last, bc, ubc, bdin, bctaps, gscores, gbct, gdt]
    else:
        grad_normed = turned_product(z4, grad_z) + turned_product(x4, gx) + turned_product(bd4, gbd)
        whole_rows = hx[:, Q:].astype(F32) * rstd_in
        gain_here = lax.dynamic_slice_in_dim(gain_full, col_index * cols_here, cols_here)[:, None]
        gn_given, plain = None, (jnp.sum(whole_rows * gain_full[:, None] * grad_normed, axis=0)[None], jnp.sum(whole_rows * grad_normed, axis=1)[None])
        gn_here = lax.psum_scatter(grad_normed.astype(BF16), "col", scatter_dimension=0, tiled=True).astype(F32)
    if not early:
        sources.append((1, 0, len(later)))
        lefts.append(grad_by)
        later.append(gated)
        pieces += [(3, at, each) for at in range(0, inner, each)]
    sums, state_out, small_out, stat_out, grad_in = close(
        sources, pieces, lefts, None if fused else gbd_padded, (lengths, gtaps, ggate, hsum) if fused else (gtaps, ggate, gbctaps, hsum),
        gn_given, plain, later, (nc, hb, len(later)) if fused else ())
    if ncols != 2:
        stat_total = jnp.sum(stat_out, axis=0)
        grad_in = (grad_out.astype(F32) + rstd_in * gain_here * gn_here - hidden_f * (rstd_in * rstd_in) * (stat_total / width)).astype(BF16)
    g_out = back_out[8] if early else sums[3][:, :inner]
    (g_norm_gain, g_inner, g_state, g_step, g_taps, g_bias, g_bc_taps, g_bc_bias, g_step_bias, g_decay, g_skip, g_gate) = last(
        sums[0], sums[1], state_out, small_out, [back_out[9], sums[2]] if early else [sums[2]], heads, inner)
    return (
        block_out,
        grad_in,
        g_norm_gain[0],
        jnp.transpose(g_inner, (2, 0, 1)),
        g_state,
        g_step,
        g_taps,
        g_bias[0],
        g_bc_taps,
        g_bc_bias[0],
        g_step_bias[0],
        g_decay[0],
        g_skip[0],
        g_gate[0],
        g_out.T,
    )


def solution(mesh):
    col, tokens, sums = P("col"), P("col", ("dp", "row")), P("col", ("dp", "row"))
    return jax.shard_map(
        per_device,
        mesh=mesh,
        in_specs=(tokens, tokens, P("dp", None), P(), P("col", None, "row"), P("row", None), P("col", "row"),
                  P(None, "col"), col, P(), P(), col, col, col, col, P("col", "row")),
        out_specs=(tokens, tokens, P(), P("col", None, ("dp", "row")), P(), sums, P(), P(), P(), P(), P(), P(), P(), P(), sums),
        check_vma=False,
    )
```

time: 2030 us -> 403 us (0.20); the launches traced: 2000 us -> 398 us
  waiting for transfers between devices: 762 us -> 8.46 us
  local copies, waits for them, and re-layouts: 582 us -> 6.53 us
  Pallas kernels: 0 us -> 343 us
  matrix products: 330 us -> 20.8 us
  other arithmetic: 255 us -> 10.9 us
  blocking collectives: 35.5 us -> 0 us
    pallas_call x0 -> x9, Pallas kernels: none -> 343 us  [the longest x1 114 us: close(): pl.pallas_call(functools.partial(close_kernel, n_row, n_dp, n_col, source...]
    reduce_scatter x4 -> x0, waiting for transfers between devices: 338 us -> none  [the longest x1 201 us: per_device(): lax.psum_scatter(grad_inner_w, ('dp', 'row'), scatter_dimension=2, tiled=...]
    dynamic_update_slice x37 -> x0, local copies, waits for them, and re-layouts: 314 us -> none  [the longest x32 312 us: scan_spans(): final, outputs = lax.scan(jax.checkpoint(step), state, pieces)]
    dot_general x69 -> x4, matrix products: 330 us -> 20.8 us  [the longest x2 11.6 us: nt(): lax.dot_general(a, b, (((1,), (1,)), ((), ())), precision=precision, pref...]
    psum x2 -> x0, waiting for transfers between devices: 268 us -> none  [per_device(): lax.psum((grad_state_w, place_block(grad_gain_here, ncols, col_index, 0),...]
    all_gather x6 -> x0, waiting for transfers between devices: 133 us -> none  [the longest x1 62.5 us: per_device(): lax.all_gather(inner_proj, 'row', axis=2, tiled=True)]
    another operation x51 -> x1, other arithmetic: 68.4 us -> 0.6 us  [per_device(): jnp.stack([step_bias, decay_log, skip_gain])]
    unnamed x247 -> x44, local copies, waits for them, and re-layouts: 58.2 us -> 3.84 us
  transfers between devices with their start and end apart: 17 -> 8, of which waited for: 10 -> 2; matrix products, arithmetic and copies ran while one was open for 40% -> 6% of each run, Pallas kernels for 0% -> 28%
where the time goes in v1:
time: 403 us; the launch traced here: 398 us
  Pallas kernels  343 us (85%)
  matrix products  20.8 us (5%)
  other arithmetic  10.9 us (3%)
  waiting for transfers between devices  8.46 us (2%)
  starting transfers between devices  6.96 us (2%)
  local copies, waits for them, and re-layouts  6.53 us (2%)
    pallas_call x1, Pallas kernels, close(): pl.pallas_call(functools.partial(close_kernel, n_row, n_dp, n_col, source...  114 us
    pallas_call x1, Pallas kernels, per_device(): pl.pallas_call(functools.partial(back_kernel, nc, hb, heads, early, n_dp)...  65.9 us
    pallas_call x1, Pallas kernels, open_up(): pl.pallas_call(functools.partial(open_kernel, n_row, n_col, parts), in_sp...  49.8 us
    pallas_call x1, Pallas kernels, per_device(): pl.pallas_call(functools.partial(second_kernel, nrow, lax.axis_size('dp')...  28.4 us
    pallas_call x1, Pallas kernels, per_device(): pl.pallas_call(functools.partial(enter_kernel, nc, hb), grid=(nb,), in_sp...  27.8 us
    pallas_call x1, Pallas kernels, per_device(): pl.pallas_call(functools.partial(gate_kernel, nc, hb), grid=(nb,), in_spe...  18.9 us
    pallas_call x1, Pallas kernels, per_device(): pl.pallas_call(functools.partial(across_kernel, nc, hb), grid=(nb,), in_s...  17.4 us
    pallas_call x1, Pallas kernels, per_device(): pl.pallas_call(functools.partial(project_kernel, nrow, lax.axis_size('dp'...  17.1 us
  transfers between devices with their start and end apart: 8, of which 2 were waited for; matrix products, arithmetic and copies ran while one was open for 6% of the time, Pallas kernels for 28%

profile of v1, /device:TPU:0, one launch (start us, length us, event | category | flops | bytes accessed | tf_op | source)
XLA Modules:
  0.0 397.8 jit_solution(11087469430699767787)
XLA Ops:
  0.6 0.0 copy-start.2
  0.7 0.0 copy-start.17
  0.7 0.0 copy-start.8
  0.7 0.0 copy-start.9
  0.7 49.8 %open.1 = (bf16[1536,1152]{1,0:T(8,128)(2,1)}, bf16[4,1536,384]{2,1,0:T(8,128)(2,1)}, bf16[1536,384]{1,0:T(8,128)(2,1)}, bf16[4,288,384]{2,1,0:T(8,128)(2,1)}) custom-call(bf16[768,1024]{1,0:T(8,128)(2,1)} %hidden.1, bf16[1536,2,384]{2,1,0:T(2,128)(2,1)} %inner.1, bf16[384,256]{1,0:T(8,128)(2,1)} %state_w.1, bf16[24,384]{1,0:T(8,128)(2,1)} %step_w.1), custom_call_target="tpu_custom_call" | custom-call | bytes 100000000 | tf_op jit(solution)/shard_map/open/pallas_call | solution.py:1129
  50.5 0.6 collective-permute-start
  51.1 0.0 copy-done.2
  51.1 0.9 collective-permute-start.2
  52.0 0.0 copy-done.17
  52.0 0.0 copy-done.8
  52.0 0.0 copy-done.9
  52.0 0.6 broadcast_in_dim.14.gain8_ref.refs_5_
  52.7 0.0 copy-start.7
  52.7 17.1 %project.1 = (bf16[1536,1152]{1,0:T(8,128)(2,1)}, bf16[1536,1024]{1,0:T(8,128)(2,1)}, f32[8,1024]{1,0:T(8,128)}, f32[8,1024]{1,0:T(8,128)}, f32[1536,1152]{1,0:T...) custom-call(s32[1,3]{1,0:T(1,128)} %refs_1_.1, bf16[1536,1152]{1,0:T(8,128)(2,1)} %get-tuple-element.87.hx_ref.refs_12_, ...), custom_call_target="tpu_custom_call" | custom-call | flops 8000000000 | bytes 20000000 | tf_op jit(solution)/shard_map/project/pallas_call | solution.py:1314
  69.8 1.3 slice.39
  71.1 0.1 pad.26.clone
  71.2 0.6 select_maximum_fusion.heads_ref
  71.8 0.6 fusion.27.bctaps8_ref.refs_19_
  72.4 0.6 fusion.21.taps8_ref
  73.1 5.3 %collective-permute-done.wait_ref.refs_1_.refs_5_ = bf16[1536,384]{1,0:T(8,128)(2,1)} collective-permute-done((bf16[1536,384]{1,0:T(8,128)(2,1)}, bf16[1536,384]{1,0:T(8,128)(2,1)}, u32[]{:S(2)}, u32[]{:S(2)}) %collective-permute-start) | collective-permute-done | bytes 1179680 | tf_op jit(solution)/shard_map/ppermute | solution.py:550
  78.4 0.5 collective-permute-start.1
  78.8 27.8 %enter.1 = (f32[1536,1024]{1,0:T(8,128)}, f32[256,1024]{1,0:T(8,128)}, f32[256,1024]{1,0:T(8,128)}, f32[6,6,8,1024]{3,2,1,0:T(8,128)}, f32[8,128,128]{2,1,0:T(8,...) custom-call(s32[1,3]{1,0:T(1,128)} %refs_1_.1, ...), custom_call_target="tpu_custom_call" | custom-call | flops 30000001024 | bytes 40000000 | tf_op jit(solution)/shard_map/enter/pallas_call | solution.py:1346
  106.7 0.0 collective-permute-done.2.refs_10_
  106.7 0.0 copy-start.15
  106.7 0.0 collective-permute-done.1.refs_3_.refs_7_
  106.7 0.0 copy-start.16
  106.7 1.1 copy-done.15
  107.8 0.4 copy-done.16
  108.2 28.4 %second.1 = (bf16[4,1536,384]{2,1,0:T(8,128)(2,1)}, f32[1536,1024]{1,0:T(8,128)}, bf16[4,1536,384]{2,1,0:T(8,128)(2,1)}, f32[1536,1024]{1,0:T(8,128)}, f32[1536,128]{1,0:T(8,128)}, /*index=5*/bf16[1536,1024]{1,0:T(8,128)(2,1)}) custom-call(bf16[1536,384]{1,0:T(8,128)(2,1)} %get-tuple-element.91.refs_0_.refs_4_, ...), custom_call_target="tpu_custom_call" | custom-call | flops 10000000000 | bytes 30000000 | tf_op jit(solution)/shard_map/second/pallas_call | solution.py:1366
  136.6 0.6 broadcast_in_dim.32.gate8_ref
  137.2 17.4 %across.1 = (f32[1536,1024]{1,0:T(8,128)}, f32[8,1536,128]{2,1,0:T(8,128)}, f32[2,8,1024]{2,1,0:T(8,128)}) custom-call(f32[1536,1024]{1,0:T(8,128)} %get-tuple-element.103.y_ref, f32[8,1536,128]{2,1,0:T(8,128)} %get-tuple-element.104.fresh_ref, f32[1536,128]{1,0:T(8,128)} %get-tuple-element.105.start_ref, f32[256,1024]{1,0:T(8,128)} %get-tuple-element.106.bc_ref.refs_16_, ...), custom_call_target="tpu_custom_call" | custom-call | flops 10000000000 | bytes 35000000 | tf_op jit(solution)/shard_map/across/pallas_call | solution.py:1386
  154.6 0.9 reduce_sum.9
  155.5 0.6 collective-permute-start.3
  156.1 3.1 collective-permute-done.3
  159.3 0.7 maximum_maximum_fusion.tok_ref
  160.0 18.9 %gate.1 = (bf16[1536,1024]{1,0:T(8,128)(2,1)}, bf16[1536,1024]{1,0:T(8,128)(2,1)}, f32[1536,1024]{1,0:T(8,128)}, f32[8,1536,128]{2,1,0:T(8,128)}, bf16[1536,128]{1,0:T(8,128)(2,1)}, /*index=5*/f32[8,1536]{1,0:T(8,128)}) custom-call(f32[1536,1024]{1,0:T(8,128)} %get-tuple-element.110.y_ref, f32[1536,1024]{1,0:T(8,128)} %get-tuple-element.108.z_ref, ...), custom_call_target="tpu_custom_call" | custom-call | flops 10000000000 | bytes 40000000 | tf_op jit(solution)/shard_map/gate/pallas_call | solution.py:1404
  178.9 1.0 pad_maximum_fusion
  179.9 1.3 collective-permute-start.7
  181.2 1.3 collective-permute-start.6
  182.5 1.3 collective-permute-start.5
  183.8 0.0 copy-done.18
  183.8 0.0 copy-start.19
  183.8 4.7 %fusion.9 = bf16[2,384,1024]{2,1,0:T(8,128)(2,1)S(1)} fusion(bf16[1536,1024]{1,0:T(8,128)(2,1)} %get-tuple-element.112, bf16[4,1536,384]{2,1,0:T(8,128)(2,1)S(1)} %copy-done.18, s32[]{:T(128)S(6)} %select_n.7), kind=kOutput, calls=%fused_computation.12 | convolution fusion | flops 2416705536 | bytes 7077892 | tf_op jit(solution)/shard_map/dot_general | solution.py:1419
  188.5 4.5 %fusion.5 = f32[2,384,1024]{2,1,0:T(8,128)} fusion(bf16[1536,1024]{1,0:T(8,128)(2,1)S(1)} %copy-done.19, bf16[4,1536,384]{2,1,0:T(8,128)(2,1)S(1)} %copy-done.18, s32[]{:T(128)S(6)} %select_n.6), kind=kOutput, calls=%fused_computation.7 | convolution fusion | flops 2415919104 | bytes 8650756 | tf_op jit(solution)/shard_map/dot_general | solution.py:1419
  193.0 7.3 %convolution_convert_fusion.refs_0_ = bf16[1536,1536]{1,0:T(8,128)(2,1)} fusion(bf16[1536,1024]{1,0:T(8,128)(2,1)S(1)} %copy-done.20, bf16[1536,1024]{1,0:T(8,128)(2,1)S(1)} %copy-done.19), kind=kOutput, calls=%fused_computation | convolution fusion | flops 4834197504 | bytes 11010048 | tf_op jit(solution)/shard_map/dot_general | solution.py:29
  200.4 0.5 collective-permute-start.4
  200.9 0.0 copy-done.1
  200.9 4.2 %convolution_convert_fusion.1.refs_1_ = bf16[1536,512]{1,0:T(8,128)(2,1)} fusion(bf16[1536,1024]{1,0:T(8,128)(2,1)S(1)} %copy-done.1, bf16[1536,1024]{1,0:T(8,128)(2,1)} %get-tuple-element.122.refs_8_), kind=kOutput, calls=%fused_computation.9 | convolution fusion | flops 1611399168 | bytes 5767168 | tf_op jit(solution)/shard_map/dot_general | solution.py:29
  205.1 0.0 collective-permute-done.6
  205.2 0.0 collective-permute-done.5
  205.2 0.0 collective-permute-done.7
  205.2 1.1 fusion.16.start_ref
  206.3 65.9 %back.1 = (bf16[1536,1024]{1,0:T(8,128)(2,1)}, f32[1536,128]{1,0:T(8,128)}, bf16[1536,128]{1,0:T(8,128)(2,1)}, f32[8,1536]{1,0:T(8,128)}, f32[6,8,1024]{2,1,0:T(...) custom-call(s32[1,3]{1,0:T(1,128)} %refs_1_.1, ...), custom_call_target="tpu_custom_call" | custom-call | flops 60000002048 | bytes 50000000 | tf_op jit(solution)/shard_map/back/pallas_call | solution.py:1440
  272.2 0.0 collective-permute-done.4
  272.2 0.0 copy-start.6
  272.2 114.4 %close.1 = (f32[96,384]{1,0:T(8,128)}, f32[96,1536]{1,0:T(8,128)}, f32[96,1024]{1,0:T(8,128)}, bf16[1536,256]{1,0:T(8,128)(2,1)}, f32[2,16,1536]{2,1,0:T(8,128)}...) custom-call(bf16[1536,1024]{1,0:T(8,128)(2,1)} %get-tuple-element.121.refs_0_, s32[1,3]{1,0:T(1,128)} %refs_1_.1, ...), custom_call_target="tpu_custom_call" | custom-call | flops 1000000 | bytes 100000000 | tf_op jit(solution)/shard_map/close/pallas_call | solution.py:975
  386.6 0.0 copy-start
  386.6 3.4 last.1
  389.9 1.3 reduce
  391.3 4.1 %fusion.2 = bf16[768,1024]{1,0:T(8,128)(2,1)} fusion(f32[2,384,1024]{2,1,0:T(8,128)} %fusion.5, bf16[768,1024]{1,0:T(8,128)(2,1)S(1)} %collective-permute-done.4, bf16[768,1024]{1,0:T(8,128)(2,1)S(1)} %copy-done, f32[1024]{0:T(1024)S(1)} %bitcast.59), kind=kLoop, calls=%fused_computation.4 | loop fusion | flops 4718592 | bytes 7868416 | tf_op jit(solution)/shard_map/convert_element_type | solution.py:1467
  395.3 0.0 copy-done.3
  395.3 1.1 copy.37
  396.5 0.3 copy-done.4
  396.8 0.8 copy.38
  (32 shorter events, 0.1 us)
Async XLA Ops:
  0.6 50.4 %copy-start.2 = (bf16[768,1024]{1,0:T(8,128)(2,1)S(1)}, bf16[768,1024]{1,0:T(8,128)(2,1)}, u32[]{:S(2)}) copy-start(bf16[768,1024]{1,0:T(8,128)(2,1)} %refs_13_.1) | copy-start | bytes 4718596
  0.7 51.3 %copy-start.17 = (bf16[256]{0:T(256)(128)(2,1)S(1)}, bf16[256]{0:T(256)(128)(2,1)}, u32[]{:S(2)}) copy-start(bf16[256]{0:T(256)(128)(2,1)} %param.26) | copy-start | bytes 1540
  0.7 51.3 %copy-start.8 = (bf16[1536]{0:T(1024)(128)(2,1)S(1)}, bf16[1536]{0:T(1024)(128)(2,1)}, u32[]{:S(2)}) copy-start(bf16[1536]{0:T(1024)(128)(2,1)} %param.24) | copy-start | bytes 9220
  0.7 51.3 %copy-start.9 = (bf16[1536]{0:T(1024)(128)(2,1)S(1)}, bf16[1536]{0:T(1024)(128)(2,1)}, u32[]{:S(2)}) copy-start(bf16[1536]{0:T(1024)(128)(2,1)} %param.19) | copy-start | bytes 9220
  50.5 27.9 %collective-permute-start = (bf16[1536,384]{1,0:T(8,128)(2,1)}, bf16[1536,384]{1,0:T(8,128)(2,1)}, u32[]{:S(2)}, u32[]{:S(2)}) collective-permute-start(bf16[1536,384]{1,0:T(8,128)(2,1)} %get-tuple-element.91.refs_0_.refs_4_), channel_id=1, source_target_pairs={{0,4},{2,6},{4,0},{6,2},{1,5},{3,7},{5,1},{7,3},{8,12},{10,14},{12... | collective-permute-start | bytes 3538952 | tf_op jit(solution)/shard_map/ppermute | solution.py:550
  51.1 55.6 %collective-permute-start.2 = (bf16[768,1024]{1,0:T(8,128)(2,1)S(1)}, bf16[768,1024]{1,0:T(8,128)(2,1)S(1)}, u32[]{:S(2)}, u32[]{:S(2)}) collective-permute-start(bf16[768,1024]{1,0:T(8,128)(2,1)S(1)} %copy-done.2), channel_id=1, source_target_pairs={{0,1},{1,0},{2,3},{3,2},{4,5},{5,4},{6,7},{7,6},{8,9},{9,8},{10,11... | collective-permute-start | bytes 4718600 | tf_op jit(solution)/shard_map/ppermute | solution.py:550
  52.6 18.6 %copy-start.12 = (f32[24]{0:T(128)S(1)}, f32[24]{0:T(128)}, u32[]{:S(2)}) copy-start(f32[24]{0:T(128)} %param.29) | copy-start | bytes 292
  52.7 18.6 %copy-start.13 = (f32[24]{0:T(128)S(1)}, f32[24]{0:T(128)}, u32[]{:S(2)}) copy-start(f32[24]{0:T(128)} %param.28) | copy-start | bytes 292
  52.7 18.6 %copy-start.14 = (f32[24]{0:T(128)S(1)}, f32[24]{0:T(128)}, u32[]{:S(2)}) copy-start(f32[24]{0:T(128)} %param.27) | copy-start | bytes 292
  52.7 19.2 %copy-start.11 = (bf16[4,256]{1,0:T(4,128)(2,1)S(1)}, bf16[4,256]{1,0:T(4,128)(2,1)}, u32[]{:S(2)}) copy-start(bf16[4,256]{1,0:T(4,128)(2,1)} %param.25) | copy-start | bytes 6148
  52.7 19.8 %copy-start.7 = (bf16[4,1536]{1,0:T(4,128)(2,1)S(1)}, bf16[4,1536]{1,0:T(4,128)(2,1)}, u32[]{:S(2)}) copy-start(bf16[4,1536]{1,0:T(4,128)(2,1)} %param.23) | copy-start | bytes 36868
  78.4 28.3 %collective-permute-start.1 = (bf16[1536,384]{1,0:T(8,128)(2,1)}, bf16[1536,384]{1,0:T(8,128)(2,1)S(1)}, u32[]{:S(2)}, u32[]{:S(2)}) collective-permute-start(bf16[1536,384]{1,0:T(8,128)(2,1)} %refs_6_), channel_id=1, source_target_pairs={{0,4},{2,6},{4,0},{6,2},{1,5},{3,7},{5,1},{7,3},{8,12},{10,14},{12... | collective-permute-start | bytes 3538952 | tf_op jit(solution)/shard_map/ppermute | solution.py:550
  106.7 1.1 copy-start.15
  106.7 1.5 copy-start.16
  108.2 28.4 %copy-start.10 = (bf16[1536]{0:T(1024)(128)(2,1)S(1)}, bf16[1536]{0:T(1024)(128)(2,1)}, u32[]{:S(2)}) copy-start(bf16[1536]{0:T(1024)(128)(2,1)} %param.30) | copy-start | bytes 9220
  137.2 18.9 %copy-start.5 = (f32[6,8,128]{2,1,0:T(8,128)S(1)}, f32[6,8,128]{2,1,0:T(8,128)}, u32[]{:S(2)}) copy-start(f32[6,8,128]{2,1,0:T(8,128)} %get-tuple-element.101.refs_13_) | copy-start | bytes 73732
  155.5 3.8 collective-permute-start.3
  160.0 23.8 %copy-start.18 = (bf16[4,1536,384]{2,1,0:T(8,128)(2,1)S(1)}, bf16[4,1536,384]{2,1,0:T(8,128)(2,1)}, u32[]{:S(2)}) copy-start(bf16[4,1536,384]{2,1,0:T(8,128)(2,1)} %get-tuple-element.102) | copy-start | bytes 14155780
  179.9 25.3 %collective-permute-start.7 = (bf16[1632,128]{1,0:T(8,128)(2,1)S(1)}, bf16[1632,128]{1,0:T(8,128)(2,1)S(1)}, u32[]{:S(2)}, u32[]{:S(2)}) collective-permute-start(bf16[1632,128]{1,0:T(8,128)(2,1)S(1)} %pad_maximum_fusion), channel_id=1, source_target_pairs={{6,0},{7,1},{14,8},{15,9},{22,16},{23,17},{30,24},{31,25}} | collective-permute-start | bytes 1253384 | tf_op jit(solution)/shard_map/ppermute | solution.py:562
  181.2 23.9 %collective-permute-start.6 = (bf16[1632,128]{1,0:T(8,128)(2,1)S(1)}, bf16[1632,128]{1,0:T(8,128)(2,1)S(1)}, u32[]{:S(2)}, u32[]{:S(2)}) collective-permute-start(bf16[1632,128]{1,0:T(8,128)(2,1)S(1)} %pad_maximum_fusion), channel_id=1, source_target_pairs={{4,0},{6,2},{5,1},{7,3},{12,8},{14,10},{13,9},{15,11},{20,16},{22,... | collective-permute-start | bytes 1253384 | tf_op jit(solution)/shard_map/ppermute | solution.py:562
  182.5 22.7 %collective-permute-start.5 = (bf16[1632,128]{1,0:T(8,128)(2,1)S(1)}, bf16[1632,128]{1,0:T(8,128)(2,1)S(1)}, u32[]{:S(2)}, u32[]{:S(2)}) collective-permute-start(bf16[1632,128]{1,0:T(8,128)(2,1)S(1)} %pad_maximum_fusion), channel_id=1, source_target_pairs={{2,0},{4,2},{6,4},{3,1},{5,3},{7,5},{10,8},{12,10},{14,12},{11,9},... | collective-permute-start | bytes 1253384 | tf_op jit(solution)/shard_map/ppermute | solution.py:562
  183.8 4.7 %copy-start.19 = (bf16[1536,1024]{1,0:T(8,128)(2,1)S(1)}, bf16[1536,1024]{1,0:T(8,128)(2,1)}, u32[]{:S(2)}) copy-start(bf16[1536,1024]{1,0:T(8,128)(2,1)} %get-tuple-element.112) | copy-start | bytes 9437188
  188.5 4.5 %copy-start.20 = (bf16[1536,1024]{1,0:T(8,128)(2,1)S(1)}, bf16[1536,1024]{1,0:T(8,128)(2,1)}, u32[]{:S(2)}) copy-start(bf16[1536,1024]{1,0:T(8,128)(2,1)} %get-tuple-element.120) | copy-start | bytes 9437188
  193.0 7.9 %copy-start.1 = (bf16[1536,1024]{1,0:T(8,128)(2,1)S(1)}, bf16[1536,1024]{1,0:T(8,128)(2,1)}, u32[]{:S(2)}) copy-start(bf16[1536,1024]{1,0:T(8,128)(2,1)} %get-tuple-element.121.refs_0_) | copy-start | bytes 9437188
  200.4 71.8 %collective-permute-start.4 = (bf16[768,1024]{1,0:T(8,128)(2,1)S(1)}, bf16[768,1024]{1,0:T(8,128)(2,1)S(1)}, u32[]{:S(2)}, u32[]{:S(2)}) collective-permute-start(bf16[768,1024]{1,0:T(8,128)(2,1)S(1)} %bitcast.63), channel_id=1, source_target_pairs={{0,1},{1,0},{2,3},{3,2},{4,5},{5,4},{6,7},{7,6},{8,9},{9,8},{10,11... | collective-permute-start | bytes 4718600 | tf_op jit(solution)/shard_map/ppermute | solution.py:550
  272.2 119.1 %copy-start.6 = (f32[1,1024]{1,0:T(1,128)S(1)}, f32[1,1024]{1,0:T(1,128)}, u32[]{:S(2)}) copy-start(f32[1,1024]{1,0:T(1,128)} %slice.39) | copy-start | bytes 12292
  386.6 4.7 %copy-start = (bf16[768,1024]{1,0:T(8,128)(2,1)S(1)}, bf16[768,1024]{1,0:T(8,128)(2,1)}, u32[]{:S(2)}) copy-start(bf16[768,1024]{1,0:T(8,128)(2,1)} %hidden.1) | copy-start | bytes 4718596
  391.3 4.1 %copy-start.3 = (bf16[768,1024]{1,0:T(8,128)(2,1)S(1)}, bf16[768,1024]{1,0:T(8,128)(2,1)}, u32[]{:S(2)}) copy-start(bf16[768,1024]{1,0:T(8,128)(2,1)} %get-tuple-element.177) | copy-start | bytes 4718596
  395.3 1.4 copy-start.4

commit v2 on v1

--- a/solution.py
+++ b/solution.py
@@ -668,8 +668,7 @@
 def add_rows(out, out_at, other, other_at, count):
     def body(i, _):
         at = i * 32
-        out[pl.ds(out_at + at, 32), :] = (
-            out[pl.ds(out_at + at, 32), :].astype(F32) + other[pl.ds(other_at + at, 32), :].astype(F32)).astype(out.dtype)
+        out[pl.ds(out_at + at, 32), :] = out[pl.ds(out_at + at, 32), :] + other[pl.ds(other_at + at, 32), :]
         return 0
 
     lax.fori_loop(0, count // 32, body, 0, unroll=4)
@@ -786,11 +785,15 @@
         later["rim_bc"].wait_recv()
         add_rim(gbd, gbclast, held(8).shape[0], 2 * STATE)
 
-    def product(place, unit):
-        gx, gz, x4, z4, bd4 = (held(k) for k in range(5))
-        each = x4.shape[2]
-        index = place * (n_row // 2) + unit
-        gn_sum[unit * each : (unit + 1) * each, :] = tn(x4[index], gx[...]) + tn(z4[index], gz[...]) + tn(bd4[index], gbd[: bd4.shape[1], :])
+    def product(place, which):
+        value, w4 = held(which), held(2 + which)
+        weights = lambda w4: jnp.concatenate([w4[place * (n_row // 2) + k] for k in range(n_row // 2)], 1)
+        part = tn(weights(w4), value[...])
+        if which:
+            gn_sum[...] = part
+        else:
+            bd4 = held(4)
+            gn_sum[...] += part + tn(weights(bd4), gbd[: bd4.shape[1], :])
 
     def prepare(k, place):
         hx = held(5)
@@ -919,12 +922,12 @@
     ahead_of = {}
     if fused:
         ahead_of = {4: [take_rim_bc], 6: [take_rim]}
-        extra = {0: [send_rim], 1: [state_back], 7: [lambda: product(1 - col, 0)], 8: [lambda: product(1 - col, 1), send_norm],
-                 9: [lambda: product(col, 0), state_col], 10: [lambda: product(col, 1), send_small], 11: [state_dp, small_pair],
+        extra = {0: [send_rim], 1: [state_back], 3: [lambda: product(1 - col, 1)], 7: [lambda: product(1 - col, 0), send_norm],
+                 8: [lambda: product(col, 1)], 9: [state_col], 10: [lambda: product(col, 0), send_small], 11: [state_dp, small_pair],
                  12: [state_row, small_dp], 13: [state_pair, small_col], 15: [norm_back]}
     elif has_gn:
-        extra = {1: [lambda: product(1 - col, 0)], 2: [lambda: product(1 - col, 1), send_norm], 4: [lambda: product(col, 0)],
-                 6: [lambda: product(col, 1), send_small], 7: [state_col], 8: [small_pair], 9: [state_dp], 10: [small_dp], 11: [state_row],
+        extra = {1: [lambda: product(1 - col, 1)], 2: [lambda: product(1 - col, 0), send_norm], 4: [lambda: product(col, 1)],
+                 6: [lambda: product(col, 0), send_small], 7: [state_col], 8: [small_pair], 9: [state_dp], 10: [small_dp], 11: [state_row],
                  12: [small_col], 13: [state_pair, norm_back]}
     else:
         extra = {1: [send_small], 3: [small_pair], 4: [small_dp], 5: [small_col], 7: [state_col], 8: [state_dp], 9: [state_row],
@@ -980,7 +983,7 @@
         + [shape(BF16, rows, 2 * STATE), shape(F32, n_col, *small), shape(F32, n_col, 1, tokens)] + [shape(BF16, here, tokens)] * has_gn,
         scratch_shapes=[pltpu.VMEM((half, width), BF16) for width in widths] + [pltpu.VMEM((quarter, width), BF16) for width in widths]
         + [pltpu.VMEM(((n_dp - 1) * block, width), BF16) for width in widths]
-        + [pltpu.VMEM((min(3 if fused else 4, len(pieces)), rows, max(width for _, _, width in pieces)), BF16)]
+        + [pltpu.VMEM((min(2 if fused else 4, len(pieces)), rows, max(width for _, _, width in pieces)), BF16)]
         + [pltpu.VMEM(value.shape, value.dtype) for value in later]
         + [pltpu.VMEM((2,) + small, F32), pltpu.VMEM((2,) + small, F32), pltpu.VMEM((n_dp,) + small, F32),
            pltpu.VMEM((n_col, block, 2 * STATE), F32), pltpu.VMEM((block, 2 * STATE), BF16),
@@ -1473,6 +1476,8 @@
     pieces = [(0, 0, 2 * STATE), (0, 2 * STATE, small_width - 2 * STATE)]
     z_pieces = [(2, at, each) for at in range(0, inner - first_z, each)]
     x_pieces = [(1, at, each) for at in range(0, inner, each)]
+    if inner % 768 == 0:
+        x_pieces[-1:] = [(1, inner - each, each // 2), (1, inner - each // 2, each // 2)]
     pieces = z_pieces + pieces + x_pieces if fused else pieces + z_pieces + x_pieces
     gbd = None
     if not fused:

time: 403 us -> 399 us (0.990)
    pallas_call x1, Pallas kernels: 114 us -> 110 us  [close(): pl.pallas_call(functools.partial(close_kernel, n_row, n_dp, n_col, source...]
where the time goes in v2:
time: 399 us; the launch traced here: 394 us
  Pallas kernels  339 us (85%)
  matrix products  20.5 us (5%)
  other arithmetic  10.9 us (3%)
  waiting for transfers between devices  8.47 us (2%)
  starting transfers between devices  6.95 us (2%)
  local copies, waits for them, and re-layouts  6.53 us (2%)
    pallas_call x1, Pallas kernels, close(): pl.pallas_call(functools.partial(close_kernel, n_row, n_dp, n_col, source...  110 us
    pallas_call x1, Pallas kernels, per_device(): pl.pallas_call(functools.partial(back_kernel, nc, hb, heads, early, n_dp)...  65.8 us
    pallas_call x1, Pallas kernels, open_up(): pl.pallas_call(functools.partial(open_kernel, n_row, n_col, parts), in_sp...  49.8 us
    pallas_call x1, Pallas kernels, per_device(): pl.pallas_call(functools.partial(second_kernel, nrow, lax.axis_size('dp')...  28.8 us
    pallas_call x1, Pallas kernels, per_device(): pl.pallas_call(functools.partial(enter_kernel, nc, hb), grid=(nb,), in_sp...  27.8 us
    pallas_call x1, Pallas kernels, per_device(): pl.pallas_call(functools.partial(gate_kernel, nc, hb), grid=(nb,), in_spe...  18.9 us
    pallas_call x1, Pallas kernels, per_device(): pl.pallas_call(functools.partial(across_kernel, nc, hb), grid=(nb,), in_s...  17.4 us
    pallas_call x1, Pallas kernels, per_device(): pl.pallas_call(functools.partial(project_kernel, nrow, lax.axis_size('dp'...  17.1 us
  transfers between devices with their start and end apart: 8, of which 2 were waited for; matrix products, arithmetic and copies ran while one was open for 6% of the time, Pallas kernels for 28%

profile of v2, /device:TPU:0, one launch (start us, length us, event | category | flops | bytes accessed | tf_op | source)
XLA Modules:
  0.0 393.9 jit_solution(4785491733373066195)
XLA Ops:
  0.6 0.0 copy-start.2
  0.7 0.0 copy-start.17
  0.7 0.0 copy-start.8
  0.7 0.0 copy-start.9
  0.7 49.8 %open.1 = (bf16[1536,1152]{1,0:T(8,128)(2,1)}, bf16[4,1536,384]{2,1,0:T(8,128)(2,1)}, bf16[1536,384]{1,0:T(8,128)(2,1)}, bf16[4,288,384]{2,1,0:T(8,128)(2,1)}) custom-call(bf16[768,1024]{1,0:T(8,128)(2,1)} %hidden.1, bf16[1536,2,384]{2,1,0:T(2,128)(2,1)} %inner.1, bf16[384,256]{1,0:T(8,128)(2,1)} %state_w.1, bf16[24,384]{1,0:T(8,128)(2,1)} %step_w.1), custom_call_target="tpu_custom_call" | custom-call | bytes 100000000 | tf_op jit(solution)/shard_map/open/pallas_call | solution.py:1132
  50.5 0.6 collective-permute-start
  51.1 0.9 collective-permute-start.2
  52.0 0.0 copy-done.8
  52.0 0.0 copy-done.9
  52.0 0.6 broadcast_in_dim.14.gain8_ref.refs_5_
  52.7 0.0 copy-start.7
  52.7 17.1 %project.1 = (bf16[1536,1152]{1,0:T(8,128)(2,1)}, bf16[1536,1024]{1,0:T(8,128)(2,1)}, f32[8,1024]{1,0:T(8,128)}, f32[8,1024]{1,0:T(8,128)}, f32[1536,1152]{1,0:T...) custom-call(s32[1,3]{1,0:T(1,128)} %refs_1_.1, bf16[1536,1152]{1,0:T(8,128)(2,1)} %get-tuple-element.87.hx_ref.refs_12_, ...), custom_call_target="tpu_custom_call" | custom-call | flops 8000000000 | bytes 20000000 | tf_op jit(solution)/shard_map/project/pallas_call | solution.py:1317
  69.8 1.3 slice.39
  71.1 0.1 pad.26.clone
  71.2 0.0 copy-done.14
  71.2 0.6 select_maximum_fusion.heads_ref
  71.8 0.6 fusion.27.bctaps8_ref.refs_19_
  72.4 0.0 copy-done.7
  72.4 0.6 fusion.21.taps8_ref
  73.1 5.3 %collective-permute-done.wait_ref.refs_1_.refs_5_ = bf16[1536,384]{1,0:T(8,128)(2,1)} collective-permute-done((bf16[1536,384]{1,0:T(8,128)(2,1)}, bf16[1536,384]{1,0:T(8,128)(2,1)}, u32[]{:S(2)}, u32[]{:S(2)}) %collective-permute-start) | collective-permute-done | bytes 1179680 | tf_op jit(solution)/shard_map/ppermute | solution.py:550
  78.4 0.5 collective-permute-start.1
  78.8 27.8 %enter.1 = (f32[1536,1024]{1,0:T(8,128)}, f32[256,1024]{1,0:T(8,128)}, f32[256,1024]{1,0:T(8,128)}, f32[6,6,8,1024]{3,2,1,0:T(8,128)}, f32[8,128,128]{2,1,0:T(8,...) custom-call(s32[1,3]{1,0:T(1,128)} %refs_1_.1, ...), custom_call_target="tpu_custom_call" | custom-call | flops 30000001024 | bytes 40000000 | tf_op jit(solution)/shard_map/enter/pallas_call | solution.py:1349
  106.7 0.0 collective-permute-done.2.refs_10_
  106.7 0.0 copy-start.15
  106.7 0.0 collective-permute-done.1.refs_3_.refs_7_
  106.7 0.0 copy-start.16
  106.7 1.1 copy-done.15
  107.8 0.4 copy-done.16
  108.2 28.8 %second.1 = (bf16[4,1536,384]{2,1,0:T(8,128)(2,1)}, f32[1536,1024]{1,0:T(8,128)}, bf16[4,1536,384]{2,1,0:T(8,128)(2,1)}, f32[1536,1024]{1,0:T(8,128)}, f32[1536,128]{1,0:T(8,128)}, /*index=5*/bf16[1536,1024]{1,0:T(8,128)(2,1)}) custom-call(bf16[1536,384]{1,0:T(8,128)(2,1)} %get-tuple-element.91.refs_0_.refs_4_, ...), custom_call_target="tpu_custom_call" | custom-call | flops 10000000000 | bytes 30000000 | tf_op jit(solution)/shard_map/second/pallas_call | solution.py:1369
  137.0 0.0 copy-done.10
  137.0 0.6 broadcast_in_dim.32.gate8_ref
  137.6 17.4 %across.1 = (f32[1536,1024]{1,0:T(8,128)}, f32[8,1536,128]{2,1,0:T(8,128)}, f32[2,8,1024]{2,1,0:T(8,128)}) custom-call(f32[1536,1024]{1,0:T(8,128)} %get-tuple-element.103.y_ref, f32[8,1536,128]{2,1,0:T(8,128)} %get-tuple-element.104.fresh_ref, f32[1536,128]{1,0:T(8,128)} %get-tuple-element.105.start_ref, f32[256,1024]{1,0:T(8,128)} %get-tuple-element.106.bc_ref.refs_16_, ...), custom_call_target="tpu_custom_call" | custom-call | flops 10000000000 | bytes 35000000 | tf_op jit(solution)/shard_map/across/pallas_call | solution.py:1389
  155.1 0.9 reduce_sum.9
  155.9 0.6 collective-permute-start.3
  156.6 3.2 collective-permute-done.3
  159.7 0.7 maximum_maximum_fusion.tok_ref
  160.4 18.9 %gate.1 = (bf16[1536,1024]{1,0:T(8,128)(2,1)}, bf16[1536,1024]{1,0:T(8,128)(2,1)}, f32[1536,1024]{1,0:T(8,128)}, f32[8,1536,128]{2,1,0:T(8,128)}, bf16[1536,128]{1,0:T(8,128)(2,1)}, /*index=5*/f32[8,1536]{1,0:T(8,128)}) custom-call(f32[1536,1024]{1,0:T(8,128)} %get-tuple-element.110.y_ref, f32[1536,1024]{1,0:T(8,128)} %get-tuple-element.108.z_ref, ...), custom_call_target="tpu_custom_call" | custom-call | flops 10000000000 | bytes 40000000 | tf_op jit(solution)/shard_map/gate/pallas_call | solution.py:1407
  179.3 1.0 pad_maximum_fusion
  180.3 1.3 collective-permute-start.7
  181.6 1.3 collective-permute-start.6
  182.9 1.3 collective-permute-start.5
  184.2 0.0 copy-done.18
  184.3 0.0 copy-start.19
  184.3 4.7 %fusion.9 = bf16[2,384,1024]{2,1,0:T(8,128)(2,1)S(1)} fusion(bf16[1536,1024]{1,0:T(8,128)(2,1)} %get-tuple-element.112, bf16[4,1536,384]{2,1,0:T(8,128)(2,1)S(1)} %copy-done.18, s32[]{:T(128)S(6)} %select_n.7), kind=kOutput, calls=%fused_computation.12 | convolution fusion | flops 2416705536 | bytes 7077892 | tf_op jit(solution)/shard_map/dot_general | solution.py:1422
  189.0 0.0 copy-done.19
  189.0 0.0 copy-start.20
  189.0 4.5 %fusion.5 = f32[2,384,1024]{2,1,0:T(8,128)} fusion(bf16[1536,1024]{1,0:T(8,128)(2,1)S(1)} %copy-done.19, bf16[4,1536,384]{2,1,0:T(8,128)(2,1)S(1)} %copy-done.18, s32[]{:T(128)S(6)} %select_n.6), kind=kOutput, calls=%fused_computation.7 | convolution fusion | flops 2415919104 | bytes 8650756 | tf_op jit(solution)/shard_map/dot_general | solution.py:1422
  193.5 7.1 %convolution_convert_fusion.refs_0_ = bf16[1536,1536]{1,0:T(8,128)(2,1)} fusion(bf16[1536,1024]{1,0:T(8,128)(2,1)S(1)} %copy-done.20, bf16[1536,1024]{1,0:T(8,128)(2,1)S(1)} %copy-done.19), kind=kOutput, calls=%fused_computation | convolution fusion | flops 4834197504 | bytes 11010048 | tf_op jit(solution)/shard_map/dot_general | solution.py:29
  200.6 0.5 collective-permute-start.4
  201.1 4.2 %convolution_convert_fusion.1.refs_1_ = bf16[1536,512]{1,0:T(8,128)(2,1)} fusion(bf16[1536,1024]{1,0:T(8,128)(2,1)S(1)} %copy-done.1, bf16[1536,1024]{1,0:T(8,128)(2,1)} %get-tuple-element.122.refs_8_), kind=kOutput, calls=%fused_computation.9 | convolution fusion | flops 1611399168 | bytes 5767168 | tf_op jit(solution)/shard_map/dot_general | solution.py:29
  205.3 0.0 collective-permute-done.6
  205.4 0.0 collective-permute-done.5
  205.4 0.0 collective-permute-done.7
  205.4 1.1 fusion.16.start_ref
  206.5 65.8 %back.1 = (bf16[1536,1024]{1,0:T(8,128)(2,1)}, f32[1536,128]{1,0:T(8,128)}, bf16[1536,128]{1,0:T(8,128)(2,1)}, f32[8,1536]{1,0:T(8,128)}, f32[6,8,1024]{2,1,0:T(...) custom-call(s32[1,3]{1,0:T(1,128)} %refs_1_.1, ...), custom_call_target="tpu_custom_call" | custom-call | flops 60000002048 | bytes 50000000 | tf_op jit(solution)/shard_map/back/pallas_call | solution.py:1443
  272.2 0.0 collective-permute-done.4
  272.3 110.1 %close.1 = (f32[96,384]{1,0:T(8,128)}, f32[96,1536]{1,0:T(8,128)}, f32[96,1024]{1,0:T(8,128)}, bf16[1536,256]{1,0:T(8,128)(2,1)}, f32[2,16,1536]{2,1,0:T(8,128)}...) custom-call(bf16[1536,1024]{1,0:T(8,128)(2,1)} %get-tuple-element.121.refs_0_, s32[1,3]{1,0:T(1,128)} %refs_1_.1, ...), custom_call_target="tpu_custom_call" | custom-call | flops 1000000 | bytes 100000000 | tf_op jit(solution)/shard_map/close/pallas_call | solution.py:978
  382.4 0.0 copy-start
  382.4 3.4 last.1
  385.8 1.3 reduce
  387.1 4.1 %fusion.2 = bf16[768,1024]{1,0:T(8,128)(2,1)} fusion(f32[2,384,1024]{2,1,0:T(8,128)} %fusion.5, bf16[768,1024]{1,0:T(8,128)(2,1)S(1)} %collective-permute-done.4, bf16[768,1024]{1,0:T(8,128)(2,1)S(1)} %copy-done, f32[1024]{0:T(1024)S(1)} %bitcast.59), kind=kLoop, calls=%fused_computation.4 | loop fusion | flops 4718592 | bytes 7868416 | tf_op jit(solution)/shard_map/convert_element_type | solution.py:1470
  391.2 1.1 copy.37
  392.3 0.3 copy-done.4
  392.6 0.8 copy.38
  (32 shorter events, 0.1 us)
Async XLA Ops:
  0.6 50.4 %copy-start.2 = (bf16[768,1024]{1,0:T(8,128)(2,1)S(1)}, bf16[768,1024]{1,0:T(8,128)(2,1)}, u32[]{:S(2)}) copy-start(bf16[768,1024]{1,0:T(8,128)(2,1)} %refs_13_.1) | copy-start | bytes 4718596
  0.7 51.3 %copy-start.17 = (bf16[256]{0:T(256)(128)(2,1)S(1)}, bf16[256]{0:T(256)(128)(2,1)}, u32[]{:S(2)}) copy-start(bf16[256]{0:T(256)(128)(2,1)} %param.26) | copy-start | bytes 1540
  0.7 51.3 %copy-start.8 = (bf16[1536]{0:T(1024)(128)(2,1)S(1)}, bf16[1536]{0:T(1024)(128)(2,1)}, u32[]{:S(2)}) copy-start(bf16[1536]{0:T(1024)(128)(2,1)} %param.24) | copy-start | bytes 9220
  0.7 51.3 %copy-start.9 = (bf16[1536]{0:T(1024)(128)(2,1)S(1)}, bf16[1536]{0:T(1024)(128)(2,1)}, u32[]{:S(2)}) copy-start(bf16[1536]{0:T(1024)(128)(2,1)} %param.19) | copy-start | bytes 9220
  50.5 27.9 %collective-permute-start = (bf16[1536,384]{1,0:T(8,128)(2,1)}, bf16[1536,384]{1,0:T(8,128)(2,1)}, u32[]{:S(2)}, u32[]{:S(2)}) collective-permute-start(bf16[1536,384]{1,0:T(8,128)(2,1)} %get-tuple-element.91.refs_0_.refs_4_), channel_id=1, source_target_pairs={{0,4},{2,6},{4,0},{6,2},{1,5},{3,7},{5,1},{7,3},{8,12},{10,14},{12... | collective-permute-start | bytes 3538952 | tf_op jit(solution)/shard_map/ppermute | solution.py:550
  51.1 55.6 %collective-permute-start.2 = (bf16[768,1024]{1,0:T(8,128)(2,1)S(1)}, bf16[768,1024]{1,0:T(8,128)(2,1)S(1)}, u32[]{:S(2)}, u32[]{:S(2)}) collective-permute-start(bf16[768,1024]{1,0:T(8,128)(2,1)S(1)} %copy-done.2), channel_id=1, source_target_pairs={{0,1},{1,0},{2,3},{3,2},{4,5},{5,4},{6,7},{7,6},{8,9},{9,8},{10,11... | collective-permute-start | bytes 4718600 | tf_op jit(solution)/shard_map/ppermute | solution.py:550
  52.6 18.6 %copy-start.12 = (f32[24]{0:T(128)S(1)}, f32[24]{0:T(128)}, u32[]{:S(2)}) copy-start(f32[24]{0:T(128)} %param.29) | copy-start | bytes 292
  52.7 18.6 %copy-start.13 = (f32[24]{0:T(128)S(1)}, f32[24]{0:T(128)}, u32[]{:S(2)}) copy-start(f32[24]{0:T(128)} %param.28) | copy-start | bytes 292
  52.7 18.6 %copy-start.14 = (f32[24]{0:T(128)S(1)}, f32[24]{0:T(128)}, u32[]{:S(2)}) copy-start(f32[24]{0:T(128)} %param.27) | copy-start | bytes 292
  52.7 19.2 %copy-start.11 = (bf16[4,256]{1,0:T(4,128)(2,1)S(1)}, bf16[4,256]{1,0:T(4,128)(2,1)}, u32[]{:S(2)}) copy-start(bf16[4,256]{1,0:T(4,128)(2,1)} %param.25) | copy-start | bytes 6148
  52.7 19.8 %copy-start.7 = (bf16[4,1536]{1,0:T(4,128)(2,1)S(1)}, bf16[4,1536]{1,0:T(4,128)(2,1)}, u32[]{:S(2)}) copy-start(bf16[4,1536]{1,0:T(4,128)(2,1)} %param.23) | copy-start | bytes 36868
  78.4 28.3 %collective-permute-start.1 = (bf16[1536,384]{1,0:T(8,128)(2,1)}, bf16[1536,384]{1,0:T(8,128)(2,1)S(1)}, u32[]{:S(2)}, u32[]{:S(2)}) collective-permute-start(bf16[1536,384]{1,0:T(8,128)(2,1)} %refs_6_), channel_id=1, source_target_pairs={{0,4},{2,6},{4,0},{6,2},{1,5},{3,7},{5,1},{7,3},{8,12},{10,14},{12... | collective-permute-start | bytes 3538952 | tf_op jit(solution)/shard_map/ppermute | solution.py:550
  106.7 1.1 copy-start.15
  106.7 1.5 copy-start.16
  108.2 28.8 %copy-start.10 = (bf16[1536]{0:T(1024)(128)(2,1)S(1)}, bf16[1536]{0:T(1024)(128)(2,1)}, u32[]{:S(2)}) copy-start(bf16[1536]{0:T(1024)(128)(2,1)} %param.30) | copy-start | bytes 9220
  137.6 18.9 %copy-start.5 = (f32[6,8,128]{2,1,0:T(8,128)S(1)}, f32[6,8,128]{2,1,0:T(8,128)}, u32[]{:S(2)}) copy-start(f32[6,8,128]{2,1,0:T(8,128)} %get-tuple-element.101.refs_13_) | copy-start | bytes 73732
  155.9 3.8 collective-permute-start.3
  160.4 23.8 %copy-start.18 = (bf16[4,1536,384]{2,1,0:T(8,128)(2,1)S(1)}, bf16[4,1536,384]{2,1,0:T(8,128)(2,1)}, u32[]{:S(2)}) copy-start(bf16[4,1536,384]{2,1,0:T(8,128)(2,1)} %get-tuple-element.102) | copy-start | bytes 14155780
  180.3 25.0 %collective-permute-start.7 = (bf16[1632,128]{1,0:T(8,128)(2,1)S(1)}, bf16[1632,128]{1,0:T(8,128)(2,1)S(1)}, u32[]{:S(2)}, u32[]{:S(2)}) collective-permute-start(bf16[1632,128]{1,0:T(8,128)(2,1)S(1)} %pad_maximum_fusion), channel_id=1, source_target_pairs={{6,0},{7,1},{14,8},{15,9},{22,16},{23,17},{30,24},{31,25}} | collective-permute-start | bytes 1253384 | tf_op jit(solution)/shard_map/ppermute | solution.py:562
  181.6 23.7 %collective-permute-start.6 = (bf16[1632,128]{1,0:T(8,128)(2,1)S(1)}, bf16[1632,128]{1,0:T(8,128)(2,1)S(1)}, u32[]{:S(2)}, u32[]{:S(2)}) collective-permute-start(bf16[1632,128]{1,0:T(8,128)(2,1)S(1)} %pad_maximum_fusion), channel_id=1, source_target_pairs={{4,0},{6,2},{5,1},{7,3},{12,8},{14,10},{13,9},{15,11},{20,16},{22,... | collective-permute-start | bytes 1253384 | tf_op jit(solution)/shard_map/ppermute | solution.py:562
  182.9 22.4 %collective-permute-start.5 = (bf16[1632,128]{1,0:T(8,128)(2,1)S(1)}, bf16[1632,128]{1,0:T(8,128)(2,1)S(1)}, u32[]{:S(2)}, u32[]{:S(2)}) collective-permute-start(bf16[1632,128]{1,0:T(8,128)(2,1)S(1)} %pad_maximum_fusion), channel_id=1, source_target_pairs={{2,0},{4,2},{6,4},{3,1},{5,3},{7,5},{10,8},{12,10},{14,12},{11,9},... | collective-permute-start | bytes 1253384 | tf_op jit(solution)/shard_map/ppermute | solution.py:562
  184.3 4.7 %copy-start.19 = (bf16[1536,1024]{1,0:T(8,128)(2,1)S(1)}, bf16[1536,1024]{1,0:T(8,128)(2,1)}, u32[]{:S(2)}) copy-start(bf16[1536,1024]{1,0:T(8,128)(2,1)} %get-tuple-element.112) | copy-start | bytes 9437188
  189.0 4.5 %copy-start.20 = (bf16[1536,1024]{1,0:T(8,128)(2,1)S(1)}, bf16[1536,1024]{1,0:T(8,128)(2,1)}, u32[]{:S(2)}) copy-start(bf16[1536,1024]{1,0:T(8,128)(2,1)} %get-tuple-element.120) | copy-start | bytes 9437188
  193.5 7.6 %copy-start.1 = (bf16[1536,1024]{1,0:T(8,128)(2,1)S(1)}, bf16[1536,1024]{1,0:T(8,128)(2,1)}, u32[]{:S(2)}) copy-start(bf16[1536,1024]{1,0:T(8,128)(2,1)} %get-tuple-element.121.refs_0_) | copy-start | bytes 9437188
  200.6 71.7 %collective-permute-start.4 = (bf16[768,1024]{1,0:T(8,128)(2,1)S(1)}, bf16[768,1024]{1,0:T(8,128)(2,1)S(1)}, u32[]{:S(2)}, u32[]{:S(2)}) collective-permute-start(bf16[768,1024]{1,0:T(8,128)(2,1)S(1)} %bitcast.63), channel_id=1, source_target_pairs={{0,1},{1,0},{2,3},{3,2},{4,5},{5,4},{6,7},{7,6},{8,9},{9,8},{10,11... | collective-permute-start | bytes 4718600 | tf_op jit(solution)/shard_map/ppermute | solution.py:550
  272.2 114.9 %copy-start.6 = (f32[1,1024]{1,0:T(1,128)S(1)}, f32[1,1024]{1,0:T(1,128)}, u32[]{:S(2)}) copy-start(f32[1,1024]{1,0:T(1,128)} %slice.39) | copy-start | bytes 12292
  382.4 4.7 %copy-start = (bf16[768,1024]{1,0:T(8,128)(2,1)S(1)}, bf16[768,1024]{1,0:T(8,128)(2,1)}, u32[]{:S(2)}) copy-start(bf16[768,1024]{1,0:T(8,128)(2,1)} %hidden.1) | copy-start | bytes 4718596
  387.1 4.1 %copy-start.3 = (bf16[768,1024]{1,0:T(8,128)(2,1)S(1)}, bf16[768,1024]{1,0:T(8,128)(2,1)}, u32[]{:S(2)}) copy-start(bf16[768,1024]{1,0:T(8,128)(2,1)} %get-tuple-element.177) | copy-start | bytes 4718596
  391.2 1.4 copy-start.4

commit v3 on v2

--- a/solution.py
+++ b/solution.py
@@ -243,7 +243,7 @@
         stat_ref[1, :, chunk_of(c)] += cross
         return 0
 
-    lax.fori_loop(0, nc, chunk, 0, unroll=2)
+    lax.fori_loop(0, nc, chunk, 0, unroll=4)
 
 
 def lane_sums(v):
@@ -283,7 +283,7 @@
             adjoint[at, :] = adjoint[at, :] * rows_ref[0, DEC, h : h + 1, chunk_of(c)] + adj[at, :]
         return 0
 
-    lax.fori_loop(0, nc, chunk, 0, unroll=2)
+    lax.fori_loop(0, nc, chunk, 0, unroll=4)
     first_ref[...] = adjoint[...].astype(BF16)
     ggate_ref[...] = lane_sums(gsum[...])
 
@@ -706,15 +706,22 @@
         rows_given = rows_given[:2] + [gbctaps] + rows_given[2:]
 
     loads = [pltpu.make_async_copy(source, held, sems_local.at[k]) for k, (source, held) in enumerate(zip(later_given, later_held))]
-    for load in loads:
-        load.start()
-    loaded = set()
+    loading, loaded = set(), set()
+
+    def fetch(*keys):
+        for k in keys:
+            if k not in loading:
+                loads[k].start()
+                loading.add(k)
 
     def held(k):
+        fetch(k)
         if k not in loaded:
             loads[k].wait()
             loaded.add(k)
         return later_held[k]
+
+    fetch(*((1, 7) if fused else range(len(loads))))
 
     row, dp, col = lax.axis_index("row"), lax.axis_index("dp"), lax.axis_index("col")
     dps = [lax.rem(dp + k, n_dp) for k in range(n_dp)]
@@ -922,7 +929,7 @@
     ahead_of = {}
     if fused:
         ahead_of = {4: [take_rim_bc], 6: [take_rim]}
-        extra = {0: [send_rim], 1: [state_back], 3: [lambda: product(1 - col, 1)], 7: [lambda: product(1 - col, 0), send_norm],
+        extra = {0: [send_rim], 2: [state_back], 4: [lambda: product(1 - col, 1)], 7: [lambda: product(1 - col, 0), send_norm],
                  8: [lambda: product(col, 1)], 9: [state_col], 10: [lambda: product(col, 0), send_small], 11: [state_dp, small_pair],
                  12: [state_row, small_dp], 13: [state_pair, small_col], 15: [norm_back]}
     elif has_gn:
@@ -935,15 +942,17 @@
     for step in extra.get(0, ()):
         step()
     make(0)
-    if not fused:
+    if fused:
+        fetch(*range(9, 16), 3, 0, 8, 2, 4, 5, 6)
+    else:
         begin()
     for t in range(1, max(count + 6, 16)):
-        if 0 <= t - 1 < count:
-            sums.across(t - 1)
         for step in ahead_of.get(t, ()):
             step()
         if t < count:
             make(t)
+        if 0 <= t - 1 < count:
+            sums.across(t - 1)
         if 0 <= t - 3 < count:
             sums.along(t - 3)
         if 0 <= t - 5 < count:

time: 399 us -> 394 us (0.987)
  Pallas kernels: 339 us -> 332 us
    pallas_call x1, Pallas kernels: 110 us -> 103 us  [close(): pl.pallas_call(functools.partial(close_kernel, n_row, n_dp, n_col, source...]
  transfers between devices with their start and end apart: 8 -> 8, of which waited for: 2 -> 2; matrix products, arithmetic and copies ran while one was open for 6% -> 7% of each run, Pallas kernels for 28% -> 29%
where the time goes in v3:
time: 394 us; the launch traced here: 387 us
  Pallas kernels  332 us (84%)
  matrix products  20.5 us (5%)
  other arithmetic  10.9 us (3%)
  waiting for transfers between devices  8.45 us (2%)
  starting transfers between devices  6.96 us (2%)
  local copies, waits for them, and re-layouts  6.53 us (2%)
    pallas_call x1, Pallas kernels, close(): pl.pallas_call(functools.partial(close_kernel, n_row, n_dp, n_col, source...  103 us
    pallas_call x1, Pallas kernels, per_device(): pl.pallas_call(functools.partial(back_kernel, nc, hb, heads, early, n_dp)...  65.8 us
    pallas_call x1, Pallas kernels, open_up(): pl.pallas_call(functools.partial(open_kernel, n_row, n_col, parts), in_sp...  49.8 us
    pallas_call x1, Pallas kernels, per_device(): pl.pallas_call(functools.partial(second_kernel, nrow, lax.axis_size('dp')...  28.8 us
    pallas_call x1, Pallas kernels, per_device(): pl.pallas_call(functools.partial(enter_kernel, nc, hb), grid=(nb,), in_sp...  27.8 us
    pallas_call x1, Pallas kernels, per_device(): pl.pallas_call(functools.partial(gate_kernel, nc, hb), grid=(nb,), in_spe...  19.3 us
    pallas_call x1, Pallas kernels, per_device(): pl.pallas_call(functools.partial(project_kernel, nrow, lax.axis_size('dp'...  17.1 us
    pallas_call x1, Pallas kernels, per_device(): pl.pallas_call(functools.partial(across_kernel, nc, hb), grid=(nb,), in_s...  16.6 us
  transfers between devices with their start and end apart: 8, of which 2 were waited for; matrix products, arithmetic and copies ran while one was open for 7% of the time, Pallas kernels for 29%

profile of v3, /device:TPU:0, one launch (start us, length us, event | category | flops | bytes accessed | tf_op | source)
XLA Modules:
  0.0 386.7 jit_solution(16860017816658342869)
XLA Ops:
  0.6 0.0 copy-start.2
  0.7 0.0 copy-start.17
  0.7 0.0 copy-start.8
  0.7 0.0 copy-start.9
  0.7 49.8 %open.1 = (bf16[1536,1152]{1,0:T(8,128)(2,1)}, bf16[4,1536,384]{2,1,0:T(8,128)(2,1)}, bf16[1536,384]{1,0:T(8,128)(2,1)}, bf16[4,288,384]{2,1,0:T(8,128)(2,1)}) custom-call(bf16[768,1024]{1,0:T(8,128)(2,1)} %hidden.1, bf16[1536,2,384]{2,1,0:T(2,128)(2,1)} %inner.1, bf16[384,256]{1,0:T(8,128)(2,1)} %state_w.1, bf16[24,384]{1,0:T(8,128)(2,1)} %step_w.1), custom_call_target="tpu_custom_call" | custom-call | bytes 100000000 | tf_op jit(solution)/shard_map/open/pallas_call | solution.py:1141
  50.5 0.6 collective-permute-start
  51.1 0.0 copy-done.2
  51.1 0.9 collective-permute-start.2
  52.0 0.0 copy-done.17
  52.0 0.6 broadcast_in_dim.14.gain8_ref.refs_5_
  52.7 0.0 copy-start.7
  52.7 17.1 %project.1 = (bf16[1536,1152]{1,0:T(8,128)(2,1)}, bf16[1536,1024]{1,0:T(8,128)(2,1)}, f32[8,1024]{1,0:T(8,128)}, f32[8,1024]{1,0:T(8,128)}, f32[1536,1152]{1,0:T...) custom-call(s32[1,3]{1,0:T(1,128)} %refs_1_.1, bf16[1536,1152]{1,0:T(8,128)(2,1)} %get-tuple-element.87.hx_ref.refs_12_, ...), custom_call_target="tpu_custom_call" | custom-call | flops 8000000000 | bytes 20000000 | tf_op jit(solution)/shard_map/project/pallas_call | solution.py:1326
  69.8 1.3 slice.39
  71.1 0.1 pad.26.clone
  71.2 0.0 copy-done.12
  71.2 0.0 copy-done.14
  71.2 0.6 select_maximum_fusion.heads_ref
  71.8 0.6 fusion.27.bctaps8_ref.refs_19_
  72.4 0.6 fusion.21.taps8_ref
  73.1 5.3 %collective-permute-done.wait_ref.refs_1_.refs_5_ = bf16[1536,384]{1,0:T(8,128)(2,1)} collective-permute-done((bf16[1536,384]{1,0:T(8,128)(2,1)}, bf16[1536,384]{1,0:T(8,128)(2,1)}, u32[]{:S(2)}, u32[]{:S(2)}) %collective-permute-start) | collective-permute-done | bytes 1179680 | tf_op jit(solution)/shard_map/ppermute | solution.py:550
  78.4 0.5 collective-permute-start.1
  78.8 27.8 %enter.1 = (f32[1536,1024]{1,0:T(8,128)}, f32[256,1024]{1,0:T(8,128)}, f32[256,1024]{1,0:T(8,128)}, f32[6,6,8,1024]{3,2,1,0:T(8,128)}, f32[8,128,128]{2,1,0:T(8,...) custom-call(s32[1,3]{1,0:T(1,128)} %refs_1_.1, ...), custom_call_target="tpu_custom_call" | custom-call | flops 30000001024 | bytes 40000000 | tf_op jit(solution)/shard_map/enter/pallas_call | solution.py:1358
  106.7 0.0 collective-permute-done.2.refs_10_
  106.7 0.0 copy-start.15
  106.7 0.0 collective-permute-done.1.refs_3_.refs_7_
  106.7 0.0 copy-start.16
  106.7 1.1 copy-done.15
  107.8 0.4 copy-done.16
  108.2 28.8 %second.1 = (bf16[4,1536,384]{2,1,0:T(8,128)(2,1)}, f32[1536,1024]{1,0:T(8,128)}, bf16[4,1536,384]{2,1,0:T(8,128)(2,1)}, f32[1536,1024]{1,0:T(8,128)}, f32[1536,128]{1,0:T(8,128)}, /*index=5*/bf16[1536,1024]{1,0:T(8,128)(2,1)}) custom-call(bf16[1536,384]{1,0:T(8,128)(2,1)} %get-tuple-element.91.refs_0_.refs_4_, ...), custom_call_target="tpu_custom_call" | custom-call | flops 10000000000 | bytes 30000000 | tf_op jit(solution)/shard_map/second/pallas_call | solution.py:1378
  137.0 0.0 copy-done.10
  137.0 0.6 broadcast_in_dim.32.gate8_ref
  137.6 16.6 %across.1 = (f32[1536,1024]{1,0:T(8,128)}, f32[8,1536,128]{2,1,0:T(8,128)}, f32[2,8,1024]{2,1,0:T(8,128)}) custom-call(f32[1536,1024]{1,0:T(8,128)} %get-tuple-element.103.y_ref, f32[8,1536,128]{2,1,0:T(8,128)} %get-tuple-element.104.fresh_ref, f32[1536,128]{1,0:T(8,128)} %get-tuple-element.105.start_ref, f32[256,1024]{1,0:T(8,128)} %get-tuple-element.106.bc_ref.refs_16_, ...), custom_call_target="tpu_custom_call" | custom-call | flops 10000000000 | bytes 35000000 | tf_op jit(solution)/shard_map/across/pallas_call | solution.py:1398
  154.3 0.9 reduce_sum.9
  155.1 0.6 collective-permute-start.3
  155.7 3.1 collective-permute-done.3
  158.9 0.7 maximum_maximum_fusion.tok_ref
  159.6 19.3 %gate.1 = (bf16[1536,1024]{1,0:T(8,128)(2,1)}, bf16[1536,1024]{1,0:T(8,128)(2,1)}, f32[1536,1024]{1,0:T(8,128)}, f32[8,1536,128]{2,1,0:T(8,128)}, bf16[1536,128]{1,0:T(8,128)(2,1)}, /*index=5*/f32[8,1536]{1,0:T(8,128)}) custom-call(f32[1536,1024]{1,0:T(8,128)} %get-tuple-element.110.y_ref, f32[1536,1024]{1,0:T(8,128)} %get-tuple-element.108.z_ref, ...), custom_call_target="tpu_custom_call" | custom-call | flops 10000000000 | bytes 40000000 | tf_op jit(solution)/shard_map/gate/pallas_call | solution.py:1416
  178.9 1.0 pad_maximum_fusion
  179.9 1.3 collective-permute-start.7
  181.2 1.3 collective-permute-start.6
  182.5 1.3 collective-permute-start.5
  183.8 4.7 %fusion.9 = bf16[2,384,1024]{2,1,0:T(8,128)(2,1)S(1)} fusion(bf16[1536,1024]{1,0:T(8,128)(2,1)} %get-tuple-element.112, bf16[4,1536,384]{2,1,0:T(8,128)(2,1)S(1)} %copy-done.18, s32[]{:T(128)S(6)} %select_n.7), kind=kOutput, calls=%fused_computation.12 | convolution fusion | flops 2416705536 | bytes 7077892 | tf_op jit(solution)/shard_map/dot_general | solution.py:1431
  188.5 0.0 copy-done.19
  188.5 0.0 copy-start.20
  188.5 4.5 %fusion.5 = f32[2,384,1024]{2,1,0:T(8,128)} fusion(bf16[1536,1024]{1,0:T(8,128)(2,1)S(1)} %copy-done.19, bf16[4,1536,384]{2,1,0:T(8,128)(2,1)S(1)} %copy-done.18, s32[]{:T(128)S(6)} %select_n.6), kind=kOutput, calls=%fused_computation.7 | convolution fusion | flops 2415919104 | bytes 8650756 | tf_op jit(solution)/shard_map/dot_general | solution.py:1431
  193.0 7.1 %convolution_convert_fusion.refs_0_ = bf16[1536,1536]{1,0:T(8,128)(2,1)} fusion(bf16[1536,1024]{1,0:T(8,128)(2,1)S(1)} %copy-done.20, bf16[1536,1024]{1,0:T(8,128)(2,1)S(1)} %copy-done.19), kind=kOutput, calls=%fused_computation | convolution fusion | flops 4834197504 | bytes 11010048 | tf_op jit(solution)/shard_map/dot_general | solution.py:29
  200.1 0.5 collective-permute-start.4
  200.6 0.0 copy-done.1
  200.6 4.2 %convolution_convert_fusion.1.refs_1_ = bf16[1536,512]{1,0:T(8,128)(2,1)} fusion(bf16[1536,1024]{1,0:T(8,128)(2,1)S(1)} %copy-done.1, bf16[1536,1024]{1,0:T(8,128)(2,1)} %get-tuple-element.122.refs_8_), kind=kOutput, calls=%fused_computation.9 | convolution fusion | flops 1611399168 | bytes 5767168 | tf_op jit(solution)/shard_map/dot_general | solution.py:29
  204.9 0.0 collective-permute-done.6
  204.9 0.0 collective-permute-done.5
  204.9 0.0 collective-permute-done.7
  205.0 1.1 fusion.16.start_ref
  206.0 65.8 %back.1 = (bf16[1536,1024]{1,0:T(8,128)(2,1)}, f32[1536,128]{1,0:T(8,128)}, bf16[1536,128]{1,0:T(8,128)(2,1)}, f32[8,1536]{1,0:T(8,128)}, f32[6,8,1024]{2,1,0:T(...) custom-call(s32[1,3]{1,0:T(1,128)} %refs_1_.1, ...), custom_call_target="tpu_custom_call" | custom-call | flops 60000002048 | bytes 50000000 | tf_op jit(solution)/shard_map/back/pallas_call | solution.py:1452
  271.8 0.0 collective-permute-done.4
  271.8 103.4 %close.1 = (f32[96,384]{1,0:T(8,128)}, f32[96,1536]{1,0:T(8,128)}, f32[96,1024]{1,0:T(8,128)}, bf16[1536,256]{1,0:T(8,128)(2,1)}, f32[2,16,1536]{2,1,0:T(8,128)}...) custom-call(bf16[1536,1024]{1,0:T(8,128)(2,1)} %get-tuple-element.121.refs_0_, s32[1,3]{1,0:T(1,128)} %refs_1_.1, ...), custom_call_target="tpu_custom_call" | custom-call | flops 1000000 | bytes 100000000 | tf_op jit(solution)/shard_map/close/pallas_call | solution.py:987
  375.2 0.0 copy-start
  375.2 3.4 last.1
  378.6 1.3 reduce
  379.9 0.0 copy-done
  379.9 4.1 %fusion.2 = bf16[768,1024]{1,0:T(8,128)(2,1)} fusion(f32[2,384,1024]{2,1,0:T(8,128)} %fusion.5, bf16[768,1024]{1,0:T(8,128)(2,1)S(1)} %collective-permute-done.4, bf16[768,1024]{1,0:T(8,128)(2,1)S(1)} %copy-done, f32[1024]{0:T(1024)S(1)} %bitcast.59), kind=kLoop, calls=%fused_computation.4 | loop fusion | flops 4718592 | bytes 7868416 | tf_op jit(solution)/shard_map/convert_element_type | solution.py:1479
  384.0 1.1 copy.37
  385.1 0.3 copy-done.4
  385.4 0.8 copy.38
  (32 shorter events, 0.1 us)
Async XLA Ops:
  0.6 50.4 %copy-start.2 = (bf16[768,1024]{1,0:T(8,128)(2,1)S(1)}, bf16[768,1024]{1,0:T(8,128)(2,1)}, u32[]{:S(2)}) copy-start(bf16[768,1024]{1,0:T(8,128)(2,1)} %refs_13_.1) | copy-start | bytes 4718596
  0.7 51.3 %copy-start.17 = (bf16[256]{0:T(256)(128)(2,1)S(1)}, bf16[256]{0:T(256)(128)(2,1)}, u32[]{:S(2)}) copy-start(bf16[256]{0:T(256)(128)(2,1)} %param.26) | copy-start | bytes 1540
  0.7 51.3 %copy-start.8 = (bf16[1536]{0:T(1024)(128)(2,1)S(1)}, bf16[1536]{0:T(1024)(128)(2,1)}, u32[]{:S(2)}) copy-start(bf16[1536]{0:T(1024)(128)(2,1)} %param.24) | copy-start | bytes 9220
  0.7 51.3 %copy-start.9 = (bf16[1536]{0:T(1024)(128)(2,1)S(1)}, bf16[1536]{0:T(1024)(128)(2,1)}, u32[]{:S(2)}) copy-start(bf16[1536]{0:T(1024)(128)(2,1)} %param.19) | copy-start | bytes 9220
  50.5 27.9 %collective-permute-start = (bf16[1536,384]{1,0:T(8,128)(2,1)}, bf16[1536,384]{1,0:T(8,128)(2,1)}, u32[]{:S(2)}, u32[]{:S(2)}) collective-permute-start(bf16[1536,384]{1,0:T(8,128)(2,1)} %get-tuple-element.91.refs_0_.refs_4_), channel_id=1, source_target_pairs={{0,4},{2,6},{4,0},{6,2},{1,5},{3,7},{5,1},{7,3},{8,12},{10,14},{12... | collective-permute-start | bytes 3538952 | tf_op jit(solution)/shard_map/ppermute | solution.py:550
  51.1 55.6 %collective-permute-start.2 = (bf16[768,1024]{1,0:T(8,128)(2,1)S(1)}, bf16[768,1024]{1,0:T(8,128)(2,1)S(1)}, u32[]{:S(2)}, u32[]{:S(2)}) collective-permute-start(bf16[768,1024]{1,0:T(8,128)(2,1)S(1)} %copy-done.2), channel_id=1, source_target_pairs={{0,1},{1,0},{2,3},{3,2},{4,5},{5,4},{6,7},{7,6},{8,9},{9,8},{10,11... | collective-permute-start | bytes 4718600 | tf_op jit(solution)/shard_map/ppermute | solution.py:550
  52.6 18.6 %copy-start.12 = (f32[24]{0:T(128)S(1)}, f32[24]{0:T(128)}, u32[]{:S(2)}) copy-start(f32[24]{0:T(128)} %param.29) | copy-start | bytes 292
  52.7 18.6 %copy-start.13 = (f32[24]{0:T(128)S(1)}, f32[24]{0:T(128)}, u32[]{:S(2)}) copy-start(f32[24]{0:T(128)} %param.28) | copy-start | bytes 292
  52.7 18.6 %copy-start.14 = (f32[24]{0:T(128)S(1)}, f32[24]{0:T(128)}, u32[]{:S(2)}) copy-start(f32[24]{0:T(128)} %param.27) | copy-start | bytes 292
  52.7 19.2 %copy-start.11 = (bf16[4,256]{1,0:T(4,128)(2,1)S(1)}, bf16[4,256]{1,0:T(4,128)(2,1)}, u32[]{:S(2)}) copy-start(bf16[4,256]{1,0:T(4,128)(2,1)} %param.25) | copy-start | bytes 6148
  52.7 19.8 %copy-start.7 = (bf16[4,1536]{1,0:T(4,128)(2,1)S(1)}, bf16[4,1536]{1,0:T(4,128)(2,1)}, u32[]{:S(2)}) copy-start(bf16[4,1536]{1,0:T(4,128)(2,1)} %param.23) | copy-start | bytes 36868
  78.4 28.3 %collective-permute-start.1 = (bf16[1536,384]{1,0:T(8,128)(2,1)}, bf16[1536,384]{1,0:T(8,128)(2,1)S(1)}, u32[]{:S(2)}, u32[]{:S(2)}) collective-permute-start(bf16[1536,384]{1,0:T(8,128)(2,1)} %refs_6_), channel_id=1, source_target_pairs={{0,4},{2,6},{4,0},{6,2},{1,5},{3,7},{5,1},{7,3},{8,12},{10,14},{12... | collective-permute-start | bytes 3538952 | tf_op jit(solution)/shard_map/ppermute | solution.py:550
  106.7 1.1 copy-start.15
  106.7 1.5 copy-start.16
  108.2 28.8 %copy-start.10 = (bf16[1536]{0:T(1024)(128)(2,1)S(1)}, bf16[1536]{0:T(1024)(128)(2,1)}, u32[]{:S(2)}) copy-start(bf16[1536]{0:T(1024)(128)(2,1)} %param.30) | copy-start | bytes 9220
  137.6 18.1 %copy-start.5 = (f32[6,8,128]{2,1,0:T(8,128)S(1)}, f32[6,8,128]{2,1,0:T(8,128)}, u32[]{:S(2)}) copy-start(f32[6,8,128]{2,1,0:T(8,128)} %get-tuple-element.101.refs_13_) | copy-start | bytes 73732
  155.1 3.7 collective-permute-start.3
  159.6 24.2 %copy-start.18 = (bf16[4,1536,384]{2,1,0:T(8,128)(2,1)S(1)}, bf16[4,1536,384]{2,1,0:T(8,128)(2,1)}, u32[]{:S(2)}) copy-start(bf16[4,1536,384]{2,1,0:T(8,128)(2,1)} %get-tuple-element.102) | copy-start | bytes 14155780
  179.9 25.1 %collective-permute-start.7 = (bf16[1632,128]{1,0:T(8,128)(2,1)S(1)}, bf16[1632,128]{1,0:T(8,128)(2,1)S(1)}, u32[]{:S(2)}, u32[]{:S(2)}) collective-permute-start(bf16[1632,128]{1,0:T(8,128)(2,1)S(1)} %pad_maximum_fusion), channel_id=1, source_target_pairs={{6,0},{7,1},{14,8},{15,9},{22,16},{23,17},{30,24},{31,25}} | collective-permute-start | bytes 1253384 | tf_op jit(solution)/shard_map/ppermute | solution.py:562
  181.2 23.7 %collective-permute-start.6 = (bf16[1632,128]{1,0:T(8,128)(2,1)S(1)}, bf16[1632,128]{1,0:T(8,128)(2,1)S(1)}, u32[]{:S(2)}, u32[]{:S(2)}) collective-permute-start(bf16[1632,128]{1,0:T(8,128)(2,1)S(1)} %pad_maximum_fusion), channel_id=1, source_target_pairs={{4,0},{6,2},{5,1},{7,3},{12,8},{14,10},{13,9},{15,11},{20,16},{22,... | collective-permute-start | bytes 1253384 | tf_op jit(solution)/shard_map/ppermute | solution.py:562
  182.5 22.4 %collective-permute-start.5 = (bf16[1632,128]{1,0:T(8,128)(2,1)S(1)}, bf16[1632,128]{1,0:T(8,128)(2,1)S(1)}, u32[]{:S(2)}, u32[]{:S(2)}) collective-permute-start(bf16[1632,128]{1,0:T(8,128)(2,1)S(1)} %pad_maximum_fusion), channel_id=1, source_target_pairs={{2,0},{4,2},{6,4},{3,1},{5,3},{7,5},{10,8},{12,10},{14,12},{11,9},... | collective-permute-start | bytes 1253384 | tf_op jit(solution)/shard_map/ppermute | solution.py:562
  183.8 4.7 %copy-start.19 = (bf16[1536,1024]{1,0:T(8,128)(2,1)S(1)}, bf16[1536,1024]{1,0:T(8,128)(2,1)}, u32[]{:S(2)}) copy-start(bf16[1536,1024]{1,0:T(8,128)(2,1)} %get-tuple-element.112) | copy-start | bytes 9437188
  188.5 4.5 %copy-start.20 = (bf16[1536,1024]{1,0:T(8,128)(2,1)S(1)}, bf16[1536,1024]{1,0:T(8,128)(2,1)}, u32[]{:S(2)}) copy-start(bf16[1536,1024]{1,0:T(8,128)(2,1)} %get-tuple-element.120) | copy-start | bytes 9437188
  193.0 7.6 %copy-start.1 = (bf16[1536,1024]{1,0:T(8,128)(2,1)S(1)}, bf16[1536,1024]{1,0:T(8,128)(2,1)}, u32[]{:S(2)}) copy-start(bf16[1536,1024]{1,0:T(8,128)(2,1)} %get-tuple-element.121.refs_0_) | copy-start | bytes 9437188
  200.1 71.7 %collective-permute-start.4 = (bf16[768,1024]{1,0:T(8,128)(2,1)S(1)}, bf16[768,1024]{1,0:T(8,128)(2,1)S(1)}, u32[]{:S(2)}, u32[]{:S(2)}) collective-permute-start(bf16[768,1024]{1,0:T(8,128)(2,1)S(1)} %bitcast.63), channel_id=1, source_target_pairs={{0,1},{1,0},{2,3},{3,2},{4,5},{5,4},{6,7},{7,6},{8,9},{9,8},{10,11... | collective-permute-start | bytes 4718600 | tf_op jit(solution)/shard_map/ppermute | solution.py:550
  271.8 108.1 %copy-start.6 = (f32[1,1024]{1,0:T(1,128)S(1)}, f32[1,1024]{1,0:T(1,128)}, u32[]{:S(2)}) copy-start(f32[1,1024]{1,0:T(1,128)} %slice.39) | copy-start | bytes 12292
  375.2 4.7 %copy-start = (bf16[768,1024]{1,0:T(8,128)(2,1)S(1)}, bf16[768,1024]{1,0:T(8,128)(2,1)}, u32[]{:S(2)}) copy-start(bf16[768,1024]{1,0:T(8,128)(2,1)} %hidden.1) | copy-start | bytes 4718596
  379.9 4.1 %copy-start.3 = (bf16[768,1024]{1,0:T(8,128)(2,1)S(1)}, bf16[768,1024]{1,0:T(8,128)(2,1)}, u32[]{:S(2)}) copy-start(bf16[768,1024]{1,0:T(8,128)(2,1)} %get-tuple-element.177) | copy-start | bytes 4718596
  384.0 1.4 copy-start.4

commit v4 on v3

--- a/solution.py
+++ b/solution.py
@@ -930,14 +930,14 @@
     if fused:
         ahead_of = {4: [take_rim_bc], 6: [take_rim]}
         extra = {0: [send_rim], 2: [state_back], 4: [lambda: product(1 - col, 1)], 7: [lambda: product(1 - col, 0), send_norm],
-                 8: [lambda: product(col, 1)], 9: [state_col], 10: [lambda: product(col, 0), send_small], 11: [state_dp, small_pair],
-                 12: [state_row, small_dp], 13: [state_pair, small_col], 15: [norm_back]}
+                 8: [lambda: product(col, 1)], 10: [lambda: product(col, 0), send_small, state_col], 12: [state_dp, small_pair],
+                 13: [state_row, small_dp], 14: [state_pair, small_col], 15: [norm_back]}
     elif has_gn:
         extra = {1: [lambda: product(1 - col, 1)], 2: [lambda: product(1 - col, 0), send_norm], 4: [lambda: product(col, 1)],
-                 6: [lambda: product(col, 0), send_small], 7: [state_col], 8: [small_pair], 9: [state_dp], 10: [small_dp], 11: [state_row],
+                 6: [lambda: product(col, 0), send_small], 8: [state_col, small_pair], 10: [state_dp, small_dp], 11: [state_row],
                  12: [small_col], 13: [state_pair, norm_back]}
     else:
-        extra = {1: [send_small], 3: [small_pair], 4: [small_dp], 5: [small_col], 7: [state_col], 8: [state_dp], 9: [state_row],
+        extra = {1: [send_small], 3: [small_pair], 4: [small_dp], 5: [small_col], 8: [state_col], 9: [state_dp, state_row],
                  10: [state_pair], 11: [norm_back]}
     for step in extra.get(0, ()):
         step()
@@ -946,17 +946,17 @@
         fetch(*range(9, 16), 3, 0, 8, 2, 4, 5, 6)
     else:
         begin()
-    for t in range(1, max(count + 6, 16)):
+    for t in range(1, max(count + 7, 17)):
         for step in ahead_of.get(t, ()):
             step()
         if t < count:
             make(t)
-        if 0 <= t - 1 < count:
-            sums.across(t - 1)
-        if 0 <= t - 3 < count:
-            sums.along(t - 3)
-        if 0 <= t - 5 < count:
-            sums.finish(t - 5)
+        if 0 <= t - 2 < count:
+            sums.across(t - 2)
+        if 0 <= t - 4 < count:
+            sums.along(t - 4)
+        if 0 <= t - 6 < count:
+            sums.finish(t - 6)
         for step in extra.get(t, ()):
             step()
     for copy in later["small4"] + later["state4"]:
@@ -992,7 +992,7 @@
         + [shape(BF16, rows, 2 * STATE), shape(F32, n_col, *small), shape(F32, n_col, 1, tokens)] + [shape(BF16, here, tokens)] * has_gn,
         scratch_shapes=[pltpu.VMEM((half, width), BF16) for width in widths] + [pltpu.VMEM((quarter, width), BF16) for width in widths]
         + [pltpu.VMEM(((n_dp - 1) * block, width), BF16) for width in widths]
-        + [pltpu.VMEM((min(2 if fused else 4, len(pieces)), rows, max(width for _, _, width in pieces)), BF16)]
+        + [pltpu.VMEM((min(3 if fused else 4, len(pieces)), rows, max(width for _, _, width in pieces)), BF16)]
         + [pltpu.VMEM(value.shape, value.dtype) for value in later]
         + [pltpu.VMEM((2,) + small, F32), pltpu.VMEM((2,) + small, F32), pltpu.VMEM((n_dp,) + small, F32),
            pltpu.VMEM((n_col, block, 2 * STATE), F32), pltpu.VMEM((block, 2 * STATE), BF16),
@@ -1005,7 +1005,7 @@
             pltpu.VMEM((2 * STATE, Q), BF16), pltpu.VMEM((channels + 2 * STATE, Q), BF16), pltpu.VMEM((2 * STATE, Q), F32),
             pltpu.VMEM((CONV + 1, 2 * STATE, Q), F32), pltpu.VMEM((CONV + 1, 2 * STATE, Q), F32), pltpu.VMEM((2, 2 * STATE, Q), F32),
             pltpu.SemaphoreType.DMA((2, 2))] if fused else []),
-        compiler_params=pltpu.CompilerParams(vmem_limit_bytes=60 * 1024 * 1024, collective_id=1, has_side_effects=True),
+        compiler_params=pltpu.CompilerParams(vmem_limit_bytes=61 * 1024 * 1024, collective_id=1, has_side_effects=True),
         cost_estimate=pl.CostEstimate(flops=10**6, bytes_accessed=10**8, transcendentals=0),
         name="close",
     )(*lefts, *([] if fused else [gbd]), *given, *extra, *later)

time: 394 us -> 391 us (level)
  no operation moved by 1% of the time
where the time goes in v4:
time: 391 us; the launch traced here: 384 us
  Pallas kernels  329 us (84%)
  matrix products  20.5 us (5%)
  other arithmetic  10.9 us (3%)
  waiting for transfers between devices  8.37 us (2%)
  starting transfers between devices  6.97 us (2%)
  local copies, waits for them, and re-layouts  6.03 us (2%)
    pallas_call x1, Pallas kernels, close(): pl.pallas_call(functools.partial(close_kernel, n_row, n_dp, n_col, source...  101 us
    pallas_call x1, Pallas kernels, per_device(): pl.pallas_call(functools.partial(back_kernel, nc, hb, heads, early, n_dp)...  65.8 us
    pallas_call x1, Pallas kernels, open_up(): pl.pallas_call(functools.partial(open_kernel, n_row, n_col, parts), in_sp...  49.8 us
    pallas_call x1, Pallas kernels, per_device(): pl.pallas_call(functools.partial(second_kernel, nrow, lax.axis_size('dp')...  28.6 us
    pallas_call x1, Pallas kernels, per_device(): pl.pallas_call(functools.partial(enter_kernel, nc, hb), grid=(nb,), in_sp...  27.8 us
    pallas_call x1, Pallas kernels, per_device(): pl.pallas_call(functools.partial(gate_kernel, nc, hb), grid=(nb,), in_spe...  19.3 us
    pallas_call x1, Pallas kernels, per_device(): pl.pallas_call(functools.partial(project_kernel, nrow, lax.axis_size('dp'...  17.2 us
    pallas_call x1, Pallas kernels, per_device(): pl.pallas_call(functools.partial(across_kernel, nc, hb), grid=(nb,), in_s...  16.7 us
  transfers between devices with their start and end apart: 8, of which 2 were waited for; matrix products, arithmetic and copies ran while one was open for 7% of the time, Pallas kernels for 29%

profile of v4, /device:TPU:0, one launch (start us, length us, event | category | flops | bytes accessed | tf_op | source)
XLA Modules:
  0.0 383.6 jit_solution(15924660050626290728)
XLA Ops:
  0.6 0.0 copy-start.2
  0.7 0.0 copy-start.17
  0.7 0.0 copy-start.8
  0.7 0.0 copy-start.9
  0.7 49.8 %open.1 = (bf16[1536,1152]{1,0:T(8,128)(2,1)}, bf16[4,1536,384]{2,1,0:T(8,128)(2,1)}, bf16[1536,384]{1,0:T(8,128)(2,1)}, bf16[4,288,384]{2,1,0:T(8,128)(2,1)}) custom-call(bf16[768,1024]{1,0:T(8,128)(2,1)} %hidden.1, bf16[1536,2,384]{2,1,0:T(2,128)(2,1)} %inner.1, bf16[384,256]{1,0:T(8,128)(2,1)} %state_w.1, bf16[24,384]{1,0:T(8,128)(2,1)} %step_w.1), custom_call_target="tpu_custom_call" | custom-call | bytes 100000000 | tf_op jit(solution)/shard_map/open/pallas_call | solution.py:1141
  50.5 0.6 collective-permute-start
  51.1 0.0 copy-done.2
  51.1 0.9 collective-permute-start.2
  52.0 0.0 copy-done.17
  52.0 0.0 copy-done.8
  52.1 0.0 copy-done.9
  52.1 0.6 broadcast_in_dim.14.gain8_ref.refs_5_
  52.7 0.0 copy-start.7
  52.7 0.0 copy-start.15
  52.7 17.2 %project.1 = (bf16[1536,1152]{1,0:T(8,128)(2,1)}, bf16[1536,1024]{1,0:T(8,128)(2,1)}, f32[8,1024]{1,0:T(8,128)}, f32[8,1024]{1,0:T(8,128)}, f32[1536,1152]{1,0:T...) custom-call(s32[1,3]{1,0:T(1,128)} %refs_1_.1, bf16[1536,1152]{1,0:T(8,128)(2,1)} %get-tuple-element.87.hx_ref.refs_12_, ...), custom_call_target="tpu_custom_call" | custom-call | flops 8000000000 | bytes 20000000 | tf_op jit(solution)/shard_map/project/pallas_call | solution.py:1326
  69.9 1.4 slice.39
  71.3 0.1 pad.26.clone
  71.4 0.0 copy-done.14
  71.4 0.6 select_maximum_fusion.heads_ref
  72.0 0.6 fusion.27.bctaps8_ref.refs_19_
  72.6 0.6 fusion.21.taps8_ref
  73.2 5.2 %collective-permute-done.wait_ref.refs_1_.refs_5_ = bf16[1536,384]{1,0:T(8,128)(2,1)} collective-permute-done((bf16[1536,384]{1,0:T(8,128)(2,1)}, bf16[1536,384]{1,0:T(8,128)(2,1)}, u32[]{:S(2)}, u32[]{:S(2)}) %collective-permute-start) | collective-permute-done | bytes 1179680 | tf_op jit(solution)/shard_map/ppermute | solution.py:550
  78.4 0.5 collective-permute-start.1
  78.9 27.8 %enter.1 = (f32[1536,1024]{1,0:T(8,128)}, f32[256,1024]{1,0:T(8,128)}, f32[256,1024]{1,0:T(8,128)}, f32[6,6,8,1024]{3,2,1,0:T(8,128)}, f32[8,128,128]{2,1,0:T(8,...) custom-call(s32[1,3]{1,0:T(1,128)} %refs_1_.1, ...), custom_call_target="tpu_custom_call" | custom-call | flops 30000001024 | bytes 40000000 | tf_op jit(solution)/shard_map/enter/pallas_call | solution.py:1358
  106.7 0.0 collective-permute-done.2.refs_10_
  106.7 0.0 collective-permute-done.1.refs_3_.refs_7_
  106.7 0.0 copy-start.16
  106.7 1.0 copy-done.16
  107.7 28.6 %second.1 = (bf16[4,1536,384]{2,1,0:T(8,128)(2,1)}, f32[1536,1024]{1,0:T(8,128)}, bf16[4,1536,384]{2,1,0:T(8,128)(2,1)}, f32[1536,1024]{1,0:T(8,128)}, f32[1536,128]{1,0:T(8,128)}, /*index=5*/bf16[1536,1024]{1,0:T(8,128)(2,1)}) custom-call(bf16[1536,384]{1,0:T(8,128)(2,1)} %get-tuple-element.91.refs_0_.refs_4_, ...), custom_call_target="tpu_custom_call" | custom-call | flops 10000000000 | bytes 30000000 | tf_op jit(solution)/shard_map/second/pallas_call | solution.py:1378
  136.4 0.6 broadcast_in_dim.32.gate8_ref
  137.0 16.7 %across.1 = (f32[1536,1024]{1,0:T(8,128)}, f32[8,1536,128]{2,1,0:T(8,128)}, f32[2,8,1024]{2,1,0:T(8,128)}) custom-call(f32[1536,1024]{1,0:T(8,128)} %get-tuple-element.103.y_ref, f32[8,1536,128]{2,1,0:T(8,128)} %get-tuple-element.104.fresh_ref, f32[1536,128]{1,0:T(8,128)} %get-tuple-element.105.start_ref, f32[256,1024]{1,0:T(8,128)} %get-tuple-element.106.bc_ref.refs_16_, ...), custom_call_target="tpu_custom_call" | custom-call | flops 10000000000 | bytes 35000000 | tf_op jit(solution)/shard_map/across/pallas_call | solution.py:1398
  153.7 0.9 reduce_sum.9
  154.6 0.6 collective-permute-start.3
  155.2 3.1 collective-permute-done.3
  158.3 0.7 maximum_maximum_fusion.tok_ref
  159.0 19.3 %gate.1 = (bf16[1536,1024]{1,0:T(8,128)(2,1)}, bf16[1536,1024]{1,0:T(8,128)(2,1)}, f32[1536,1024]{1,0:T(8,128)}, f32[8,1536,128]{2,1,0:T(8,128)}, bf16[1536,128]{1,0:T(8,128)(2,1)}, /*index=5*/f32[8,1536]{1,0:T(8,128)}) custom-call(f32[1536,1024]{1,0:T(8,128)} %get-tuple-element.110.y_ref, f32[1536,1024]{1,0:T(8,128)} %get-tuple-element.108.z_ref, ...), custom_call_target="tpu_custom_call" | custom-call | flops 10000000000 | bytes 40000000 | tf_op jit(solution)/shard_map/gate/pallas_call | solution.py:1416
  178.3 1.0 pad_maximum_fusion
  179.3 1.3 collective-permute-start.7
  180.6 1.3 collective-permute-start.6
  181.9 1.3 collective-permute-start.5
  183.2 0.0 slice-done
  183.2 0.0 slice-done.1
  183.2 0.0 copy-start.18
  183.3 4.7 %fusion.9 = bf16[2,384,1024]{2,1,0:T(8,128)(2,1)S(1)} fusion(bf16[1536,1024]{1,0:T(8,128)(2,1)} %get-tuple-element.112, bf16[4,1536,384]{2,1,0:T(8,128)(2,1)S(1)} %bitcast.72, s32[]{:T(128)S(6)} %select_n.7), kind=kOutput, calls=%fused_computation.12 | convolution fusion | flops 2416705536 | bytes 7077892 | tf_op jit(solution)/shard_map/dot_general | solution.py:1431
  188.0 4.5 %fusion.5 = f32[2,384,1024]{2,1,0:T(8,128)} fusion(bf16[1536,1024]{1,0:T(8,128)(2,1)S(1)} %copy-done.18, bf16[4,1536,384]{2,1,0:T(8,128)(2,1)S(1)} %bitcast.72, s32[]{:T(128)S(6)} %select_n.6), kind=kOutput, calls=%fused_computation.7 | convolution fusion | flops 2415919104 | bytes 8650756 | tf_op jit(solution)/shard_map/dot_general | solution.py:1431
  192.5 0.0 copy-done.19
  192.5 7.1 %convolution_convert_fusion.refs_0_ = bf16[1536,1536]{1,0:T(8,128)(2,1)} fusion(bf16[1536,1024]{1,0:T(8,128)(2,1)S(1)} %copy-done.19, bf16[1536,1024]{1,0:T(8,128)(2,1)S(1)} %copy-done.18), kind=kOutput, calls=%fused_computation | convolution fusion | flops 4834197504 | bytes 11010048 | tf_op jit(solution)/shard_map/dot_general | solution.py:29
  199.6 0.5 collective-permute-start.4
  200.1 0.0 copy-done.1
  200.1 4.2 %convolution_convert_fusion.1.refs_1_ = bf16[1536,512]{1,0:T(8,128)(2,1)} fusion(bf16[1536,1024]{1,0:T(8,128)(2,1)S(1)} %copy-done.1, bf16[1536,1024]{1,0:T(8,128)(2,1)} %get-tuple-element.122.refs_8_), kind=kOutput, calls=%fused_computation.9 | convolution fusion | flops 1611399168 | bytes 5767168 | tf_op jit(solution)/shard_map/dot_general | solution.py:29
  204.3 0.0 collective-permute-done.6
  204.4 0.0 collective-permute-done.5
  204.4 0.0 collective-permute-done.7
  204.4 1.1 fusion.16.start_ref
  205.5 65.8 %back.1 = (bf16[1536,1024]{1,0:T(8,128)(2,1)}, f32[1536,128]{1,0:T(8,128)}, bf16[1536,128]{1,0:T(8,128)(2,1)}, f32[8,1536]{1,0:T(8,128)}, f32[6,8,1024]{2,1,0:T(...) custom-call(s32[1,3]{1,0:T(1,128)} %refs_1_.1, ...), custom_call_target="tpu_custom_call" | custom-call | flops 60000002048 | bytes 50000000 | tf_op jit(solution)/shard_map/back/pallas_call | solution.py:1452
  271.3 0.0 collective-permute-done.4
  271.3 100.9 %close.1 = (f32[96,384]{1,0:T(8,128)}, f32[96,1536]{1,0:T(8,128)}, f32[96,1024]{1,0:T(8,128)}, bf16[1536,256]{1,0:T(8,128)(2,1)}, f32[2,16,1536]{2,1,0:T(8,128)}...) custom-call(bf16[1536,1024]{1,0:T(8,128)(2,1)} %get-tuple-element.121.refs_0_, s32[1,3]{1,0:T(1,128)} %refs_1_.1, ...), custom_call_target="tpu_custom_call" | custom-call | flops 1000000 | bytes 100000000 | tf_op jit(solution)/shard_map/close/pallas_call | solution.py:987
  372.2 0.0 copy-start
  372.2 3.4 last.1
  375.6 1.3 reduce
  376.9 4.0 %fusion.2 = bf16[768,1024]{1,0:T(8,128)(2,1)} fusion(f32[2,384,1024]{2,1,0:T(8,128)} %fusion.5, bf16[768,1024]{1,0:T(8,128)(2,1)S(1)} %collective-permute-done.4, bf16[768,1024]{1,0:T(8,128)(2,1)S(1)} %copy-done, f32[1024]{0:T(1024)S(1)} %bitcast.59), kind=kLoop, calls=%fused_computation.4 | loop fusion | flops 4718592 | bytes 7868416 | tf_op jit(solution)/shard_map/convert_element_type | solution.py:1479
  380.9 1.1 copy.37
  382.0 0.3 copy-done.4
  382.3 0.8 copy.38
  (35 shorter events, 0.1 us)
Async XLA Ops:
  0.6 50.5 %copy-start.2 = (bf16[768,1024]{1,0:T(8,128)(2,1)S(1)}, bf16[768,1024]{1,0:T(8,128)(2,1)}, u32[]{:S(2)}) copy-start(bf16[768,1024]{1,0:T(8,128)(2,1)} %refs_13_.1) | copy-start | bytes 4718596
  0.7 51.4 %copy-start.17 = (bf16[256]{0:T(256)(128)(2,1)S(1)}, bf16[256]{0:T(256)(128)(2,1)}, u32[]{:S(2)}) copy-start(bf16[256]{0:T(256)(128)(2,1)} %param.26) | copy-start | bytes 1540
  0.7 51.4 %copy-start.8 = (bf16[1536]{0:T(1024)(128)(2,1)S(1)}, bf16[1536]{0:T(1024)(128)(2,1)}, u32[]{:S(2)}) copy-start(bf16[1536]{0:T(1024)(128)(2,1)} %param.24) | copy-start | bytes 9220
  0.7 51.4 %copy-start.9 = (bf16[1536]{0:T(1024)(128)(2,1)S(1)}, bf16[1536]{0:T(1024)(128)(2,1)}, u32[]{:S(2)}) copy-start(bf16[1536]{0:T(1024)(128)(2,1)} %param.19) | copy-start | bytes 9220
  50.5 27.9 %collective-permute-start = (bf16[1536,384]{1,0:T(8,128)(2,1)}, bf16[1536,384]{1,0:T(8,128)(2,1)}, u32[]{:S(2)}, u32[]{:S(2)}) collective-permute-start(bf16[1536,384]{1,0:T(8,128)(2,1)} %get-tuple-element.91.refs_0_.refs_4_), channel_id=1, source_target_pairs={{0,4},{2,6},{4,0},{6,2},{1,5},{3,7},{5,1},{7,3},{8,12},{10,14},{12... | collective-permute-start | bytes 3538952 | tf_op jit(solution)/shard_map/ppermute | solution.py:550
  51.1 55.6 %collective-permute-start.2 = (bf16[768,1024]{1,0:T(8,128)(2,1)S(1)}, bf16[768,1024]{1,0:T(8,128)(2,1)}, u32[]{:S(2)}, u32[]{:S(2)}) collective-permute-start(bf16[768,1024]{1,0:T(8,128)(2,1)S(1)} %copy-done.2), channel_id=1, source_target_pairs={{0,1},{1,0},{2,3},{3,2},{4,5},{5,4},{6,7},{7,6},{8,9},{9,8},{10,11... | collective-permute-start | bytes 4718600 | tf_op jit(solution)/shard_map/ppermute | solution.py:550
  52.7 18.7 %copy-start.12 = (f32[24]{0:T(128)S(1)}, f32[24]{0:T(128)}, u32[]{:S(2)}) copy-start(f32[24]{0:T(128)} %param.29) | copy-start | bytes 292
  52.7 18.7 %copy-start.13 = (f32[24]{0:T(128)S(1)}, f32[24]{0:T(128)}, u32[]{:S(2)}) copy-start(f32[24]{0:T(128)} %param.28) | copy-start | bytes 292
  52.7 18.7 %copy-start.14 = (f32[24]{0:T(128)S(1)}, f32[24]{0:T(128)}, u32[]{:S(2)}) copy-start(f32[24]{0:T(128)} %param.27) | copy-start | bytes 292
  52.7 19.3 %copy-start.11 = (bf16[4,256]{1,0:T(4,128)(2,1)S(1)}, bf16[4,256]{1,0:T(4,128)(2,1)}, u32[]{:S(2)}) copy-start(bf16[4,256]{1,0:T(4,128)(2,1)} %param.25) | copy-start | bytes 6148
  52.7 19.9 %copy-start.7 = (bf16[4,1536]{1,0:T(4,128)(2,1)S(1)}, bf16[4,1536]{1,0:T(4,128)(2,1)}, u32[]{:S(2)}) copy-start(bf16[4,1536]{1,0:T(4,128)(2,1)} %param.23) | copy-start | bytes 36868
  52.7 25.7 %copy-start.15 = (bf16[1536,384]{1,0:T(8,128)(2,1)S(1)}, bf16[1536,384]{1,0:T(8,128)(2,1)}, u32[]{:S(2)}) copy-start(bf16[1536,384]{1,0:T(8,128)(2,1)} %refs_6_) | copy-start | bytes 3538948
  78.4 28.3 %collective-permute-start.1 = (bf16[1536,384]{1,0:T(8,128)(2,1)S(1)}, bf16[1536,384]{1,0:T(8,128)(2,1)S(1)}, u32[]{:S(2)}, u32[]{:S(2)}) collective-permute-start(bf16[1536,384]{1,0:T(8,128)(2,1)S(1)} %copy-done.15), channel_id=1, source_target_pairs={{0,4},{2,6},{4,0},{6,2},{1,5},{3,7},{5,1},{7,3},{8,12},{10,14},{12... | collective-permute-start | bytes 3538952 | tf_op jit(solution)/shard_map/ppermute | solution.py:550
  106.7 1.0 copy-start.16
  107.7 28.7 %copy-start.10 = (bf16[1536]{0:T(1024)(128)(2,1)S(1)}, bf16[1536]{0:T(1024)(128)(2,1)}, u32[]{:S(2)}) copy-start(bf16[1536]{0:T(1024)(128)(2,1)} %param.30) | copy-start | bytes 9220
  137.0 18.1 %copy-start.5 = (f32[6,8,128]{2,1,0:T(8,128)S(1)}, f32[6,8,128]{2,1,0:T(8,128)}, u32[]{:S(2)}) copy-start(f32[6,8,128]{2,1,0:T(8,128)} %get-tuple-element.101.refs_13_) | copy-start | bytes 73732
  137.0 46.2 %slice-start = ((s8[4718592]{0:T(1024)(128)(4,1)}), s8[524288]{0:T(1024)(128)(4,1)S(1)}, s32[]{:S(2)}) async-start(s8[4718592]{0:T(1024)(128)(4,1)} %bitcast.71), calls=%async_computation | async-start | bytes 1048576
  154.6 3.8 collective-permute-start.3
  159.0 24.2 %slice-start.1 = ((s8[4718592]{0:T(1024)(128)(4,1)}), s8[4194304]{0:T(1024)(128)(4,1)S(1)}, s32[]{:S(2)}) async-start(s8[4718592]{0:T(1024)(128)(4,1)} %bitcast.71), calls=%async_computation.1 | async-start | bytes 8388608
  179.3 25.1 %collective-permute-start.7 = (bf16[1632,128]{1,0:T(8,128)(2,1)S(1)}, bf16[1632,128]{1,0:T(8,128)(2,1)S(1)}, u32[]{:S(2)}, u32[]{:S(2)}) collective-permute-start(bf16[1632,128]{1,0:T(8,128)(2,1)S(1)} %pad_maximum_fusion), channel_id=1, source_target_pairs={{6,0},{7,1},{14,8},{15,9},{22,16},{23,17},{30,24},{31,25}} | collective-permute-start | bytes 1253384 | tf_op jit(solution)/shard_map/ppermute | solution.py:562
  180.6 23.7 %collective-permute-start.6 = (bf16[1632,128]{1,0:T(8,128)(2,1)S(1)}, bf16[1632,128]{1,0:T(8,128)(2,1)S(1)}, u32[]{:S(2)}, u32[]{:S(2)}) collective-permute-start(bf16[1632,128]{1,0:T(8,128)(2,1)S(1)} %pad_maximum_fusion), channel_id=1, source_target_pairs={{4,0},{6,2},{5,1},{7,3},{12,8},{14,10},{13,9},{15,11},{20,16},{22,... | collective-permute-start | bytes 1253384 | tf_op jit(solution)/shard_map/ppermute | solution.py:562
  181.9 22.5 %collective-permute-start.5 = (bf16[1632,128]{1,0:T(8,128)(2,1)S(1)}, bf16[1632,128]{1,0:T(8,128)(2,1)S(1)}, u32[]{:S(2)}, u32[]{:S(2)}) collective-permute-start(bf16[1632,128]{1,0:T(8,128)(2,1)S(1)} %pad_maximum_fusion), channel_id=1, source_target_pairs={{2,0},{4,2},{6,4},{3,1},{5,3},{7,5},{10,8},{12,10},{14,12},{11,9},... | collective-permute-start | bytes 1253384 | tf_op jit(solution)/shard_map/ppermute | solution.py:562
  183.2 4.7 %copy-start.18 = (bf16[1536,1024]{1,0:T(8,128)(2,1)S(1)}, bf16[1536,1024]{1,0:T(8,128)(2,1)}, u32[]{:S(2)}) copy-start(bf16[1536,1024]{1,0:T(8,128)(2,1)} %get-tuple-element.112) | copy-start | bytes 9437188
  188.0 4.5 %copy-start.19 = (bf16[1536,1024]{1,0:T(8,128)(2,1)S(1)}, bf16[1536,1024]{1,0:T(8,128)(2,1)}, u32[]{:S(2)}) copy-start(bf16[1536,1024]{1,0:T(8,128)(2,1)} %get-tuple-element.120) | copy-start | bytes 9437188
  192.5 7.6 %copy-start.1 = (bf16[1536,1024]{1,0:T(8,128)(2,1)S(1)}, bf16[1536,1024]{1,0:T(8,128)(2,1)}, u32[]{:S(2)}) copy-start(bf16[1536,1024]{1,0:T(8,128)(2,1)} %get-tuple-element.121.refs_0_) | copy-start | bytes 9437188
  199.6 71.7 %collective-permute-start.4 = (bf16[768,1024]{1,0:T(8,128)(2,1)S(1)}, bf16[768,1024]{1,0:T(8,128)(2,1)S(1)}, u32[]{:S(2)}, u32[]{:S(2)}) collective-permute-start(bf16[768,1024]{1,0:T(8,128)(2,1)S(1)} %bitcast.63), channel_id=1, source_target_pairs={{0,1},{1,0},{2,3},{3,2},{4,5},{5,4},{6,7},{7,6},{8,9},{9,8},{10,11... | collective-permute-start | bytes 4718600 | tf_op jit(solution)/shard_map/ppermute | solution.py:550
  271.3 105.6 %copy-start.6 = (f32[1,1024]{1,0:T(1,128)S(1)}, f32[1,1024]{1,0:T(1,128)}, u32[]{:S(2)}) copy-start(f32[1,1024]{1,0:T(1,128)} %slice.39) | copy-start | bytes 12292
  372.2 4.7 %copy-start = (bf16[768,1024]{1,0:T(8,128)(2,1)S(1)}, bf16[768,1024]{1,0:T(8,128)(2,1)}, u32[]{:S(2)}) copy-start(bf16[768,1024]{1,0:T(8,128)(2,1)} %hidden.1) | copy-start | bytes 4718596
  376.9 4.0 %copy-start.3 = (bf16[768,1024]{1,0:T(8,128)(2,1)S(1)}, bf16[768,1024]{1,0:T(8,128)(2,1)}, u32[]{:S(2)}) copy-start(bf16[768,1024]{1,0:T(8,128)(2,1)} %get-tuple-element.177) | copy-start | bytes 4718596
  380.9 1.4 copy-start.4
